TPU v7x, 256 devices: a whole 4x4x8 slice. The times are simulated.
256 devices in a mesh: space: 64 (over z, y, core), cfg: 4 (over x).
Axes of the slice: x: 4, y: 4, z: 8, core: 2. Of those that a mesh axis runs over, the one named last changes fastest.
Arguments:
- snapshots: bfloat16 [393216, 2048], P('space', 'cfg'), may hold values from -6 to 6
- sketch_input: bfloat16 [2048, 256], P('cfg'), may hold values from -0.125 to 0.125
Outputs:
- basis: float32 [393216, 256], P(('space', 'cfg'))
- coefficients: float32 [256, 2048], P('space', 'cfg')
All inputs are finite; a program needn't handle non-finite values.
Results may differ from a plain program's by a relative error of at most 0.0055.
Values may be sent and summed in bfloat16 or wider, within the bound.
No kernel may reach another device: no remote copies, remote signals or barrier semaphores. Data moves between devices by JAX's collectives and lax.ppermute only.
A program may use at most 64 MiB of HBM per device.

v0:
```python
import jax
import jax.numpy as jnp
from jax import lax
from jax.sharding import PartitionSpec as P

CHOL_BLOCK = 64


def blocked_cholesky(gram):
    order = gram.shape[0]
    lower = jnp.zeros_like(gram)
    rest = gram
    for first in range(0, order, CHOL_BLOCK):
        last = first + CHOL_BLOCK
        diag = jnp.linalg.cholesky(rest[first:last, first:last])
        lower = lower.at[first:last, first:last].set(diag)
        if last < order:
            below = rest[last:, first:last]
            solved = lax.linalg.triangular_solve(
                diag, below, left_side=False, lower=True, transpose_a=True
            )
            lower = lower.at[last:, first:last].set(solved)
            update = jnp.dot(solved, solved.T, precision=lax.Precision.HIGHEST)
            rest = rest.at[last:, last:].add(-update)
    return lower


def lower_inverse(gram):
    lower = blocked_cholesky(gram)
    ident = jnp.eye(gram.shape[0], dtype=jnp.float32)
    return lax.linalg.triangular_solve(lower, ident, left_side=True, lower=True)


def self_gram(block):
    return jnp.dot(block.T, block, precision=lax.Precision.HIGHEST)


def per_device(snapshots, sketch_input):
    n_cfg = lax.axis_size("cfg")
    n_space = lax.axis_size("space")
    slab_rows = snapshots.shape[0]
    share = slab_rows // n_cfg
    total_rows = slab_rows * n_space
    total_cols = snapshots.shape[1] * n_cfg
    partial_value = jnp.dot(snapshots, sketch_input, preferred_element_type=jnp.float32)
    sketch = lax.psum(partial_value, "cfg")
    mine = lax.dynamic_slice_in_dim(sketch, lax.axis_index("cfg") * share, share, 0)
    gram_part = self_gram(sketch)
    slab_low = sketch.astype(jnp.bfloat16)
    rank = slab_low.shape[1]
    mine_count = rank // n_space
    gram = lax.psum(gram_part, "space")
    cross_mine = lax.psum_scatter(
        lax.dot_general(
            slab_low, snapshots, (((0,), (0,)), ((), ())), preferred_element_type=jnp.float32
        ),
        "space",
        scatter_dimension=0,
        tiled=True,
    )
    cross = lax.all_gather(cross_mine, "space", axis=0, tiled=True)
    inverse = lower_inverse(gram)
    own = jnp.dot(mine, inverse.T, precision=lax.Precision.HIGHEST)
    basis = own * jnp.sqrt(jnp.float32(total_rows))
    factor = jnp.sqrt(jnp.float32(total_cols) / jnp.float32(total_rows))
    inverse_rows = lax.dynamic_slice_in_dim(
        inverse, lax.axis_index("space") * mine_count, mine_count, 0
    )
    coeff = jnp.dot(inverse_rows, cross, precision=lax.Precision.HIGHEST)
    return (basis, coeff * factor)


def solution(mesh):
    in_specs = (P("space", "cfg"), P("cfg", None))
    out_specs = (P(("space", "cfg"), None), P("space", "cfg"))
    return jax.shard_map(
        per_device, mesh=mesh, in_specs=in_specs, out_specs=out_specs, check_vma=False
    )
```

profile of v0, /device:TPU:1, one launch (start us, length us, event | category | flops | bytes accessed | tf_op | source)
XLA Modules:
  0.0 496.5 jit_solution(17638215272333172609)
XLA Ops:
  7.2 0.9 copy-done
  8.1 7.2 %fusion.37 = f32[6144,256]{1,0:T(8,128)} fusion(bf16[6144,512]{1,0:T(8,128)(2,1)} %param.23, bf16[512,256]{1,0:T(8,128)(2,1)S(1)} %copy-done), kind=kOutput, calls=%fused_computation.71 | convolution fusion | flops 1610612736 | bytes 12845056 | tf_op jit(solution)/shard_map/dot_general | solution.py:45
  15.4 135.9 %all-reduce.6.cloned.1.call-done = f32[6144,256]{1,0:T(8,128)} async-done(((f32[6144,256]{1,0:T(8,128)}), f32[6144,256]{1,0:T(8,128)}) %all-reduce.6.cloned.1.call-update) | async-done | bytes 6291472 | tf_op jit(solution)/shard_map/psum | solution.py:46
  151.3 7.4 %fusion = f32[256,512]{1,0:T(8,128)} fusion(bf16[6144,512]{1,0:T(8,128)(2,1)} %param.23, f32[6144,256]{1,0:T(8,128)} %all-reduce.6.cloned.1.call-done), kind=kOutput, calls=%fused_computation.2 | convolution fusion | flops 1612185600 | bytes 13107200 | tf_op jit(solution)/shard_map/dot_general | solution.py:54
  158.7 11.0 %fusion.38 = f32[256,256]{0,1:T(8,128)} fusion(f32[6144,256]{1,0:T(8,128)S(1)} %copy-done.1), kind=kOutput, calls=%fused_computation.72 | convolution fusion | flops 4831838208 | bytes 6553600 | tf_op jit(solution)/shard_map/dot_general | solution.py:35
  169.7 0.7 dynamic-slice.76
  171.1 181.1 %all-reduce.8.cloned.1.call-done = (f32[256,256]{0,1:T(8,128)}, f32[256,512]{1,0:T(8,128)}) async-done(((f32[256,256]{0,1:T(8,128)}, f32[256,512]{1,0:T(8,128)}), (f32[256,256]{0,1:T(8,128)}, f32[256,512]{1,0:T(8,128)})) %all-reduce.8.cloned.1.call-update) | async-done | bytes 786448 | tf_op jit(solution)/shard_map/psum | solution.py:52
  352.2 0.8 slice.287
  353.0 0.8 fusion.23
  353.8 6.0 %cholesky.74 = f32[64,64]{1,0:T(8,128)S(1)} custom-call(f32[64,64]{1,0:T(8,128)S(1)} %fusion.23), custom_call_target="Cholesky" | custom-call | tf_op jit(solution)/shard_map/jit(cholesky)/cholesky | solution.py:15
  360.5 0.7 fusion.27
  361.1 4.9 custom-call.14
  366.0 1.1 fusion.11
  367.2 1.3 fusion.3
  368.6 5.8 %cholesky.85 = f32[64,64]{1,0:T(8,128)S(1)} custom-call(f32[64,64]{1,0:T(8,128)S(1)} %fusion.21), custom_call_target="Cholesky" | custom-call | tf_op jit(solution)/shard_map/jit(cholesky)/cholesky | solution.py:15
  375.8 4.9 custom-call.15
  381.6 5.8 %cholesky.96 = f32[64,64]{1,0:T(8,128)S(1)} custom-call(f32[64,64]{1,0:T(8,128)S(1)} %fusion.19), custom_call_target="Cholesky" | custom-call | tf_op jit(solution)/shard_map/jit(cholesky)/cholesky | solution.py:15
  388.7 4.9 custom-call.16
  394.3 5.8 %cholesky.107 = f32[64,64]{1,0:T(8,128)S(1)} custom-call(f32[64,64]{1,0:T(8,128)S(1)} %fusion.17), custom_call_target="Cholesky" | custom-call | tf_op jit(solution)/shard_map/jit(cholesky)/cholesky | solution.py:15
  401.5 1.7 scatter.25
  403.2 1.4 scatter.26
  404.6 1.5 scatter.29
  406.1 0.8 scatter.30
  407.6 1.0 scatter.34
  408.7 4.1 while.11
  409.3 1.4 bitcast_dynamic-update-slice_fusion.2
  411.3 1.4 bitcast_dynamic-update-slice_fusion.2
  412.8 19.7 %custom-call.17 = f32[2,128,128]{1,2,0:T(8,128)S(1)} custom-call(f32[2,128,128]{2,1,0:T(8,128)S(1)} %get-tuple-element.130), custom_call_target="InvertDiagBlocksLowerTriangular" | custom-call | tf_op jit(solution)/shard_map/triangular_solve | solution.py:31
  433.3 0.7 dynamic-slice_bitcast_fusion
  434.1 50.4 %all-gather = f32[64,4,512]{2,1,0:T(4,128)S(1)} all-gather(f32[1,4,512]{2,1,0:T(4,128)S(1)} %dynamic-slice_bitcast_fusion), channel_id=1, replica_groups=mesh['space'=64,'cfg'=4] {'space'}, dimensions={0}, use_global_device_ids=true | all-gather | bytes 532480 | tf_op jit(solution)/shard_map/all_gather | solution.py:61
  484.7 1.0 convolution_multiply_fusion.1
  485.6 4.0 convolution_multiply_fusion
  (50 shorter events, 9.4 us)
Async XLA Ops:
  7.2 1.0 copy-start
  7.2 144.1 %all-reduce.6.cloned.1.call-start = ((), (), s32[]{:S(2)}) async-start(), calls=%async_computation | async-start | bytes 12582912 | tf_op jit(solution)/shard_map/psum | solution.py:46
  15.4 336.8 %all-reduce.8.cloned.1.call-start = ((), (), s32[]{:S(2)}) async-start(), calls=%async_computation.1 | async-start | bytes 1572864 | tf_op jit(solution)/shard_map/psum | solution.py:52
  151.3 7.4 %copy-start.1 = (f32[6144,256]{1,0:T(8,128)S(1)}, f32[6144,256]{1,0:T(8,128)}, u32[]{:S(2)}) copy-start(f32[6144,256]{1,0:T(8,128)} %all-reduce.6.cloned.1.call-done) | copy-start | bytes 18874372
  158.7 11.1 %copy-start.2 = (u32[256]{0:T(256)S(1)}, u32[256]{0:T(256)}, u32[]{:S(2)}) copy-start(u32[256]{0:T(256)} %constant.334) | copy-start | bytes 3076
Sparse Core Ops, SparseCore 0:
  15.5 135.7 all-reduce.5
  169.8 182.3 all-reduce.7
where the time goes:
time: 497 us; the launch traced here: 496 us
  waiting for transfers between devices  317 us (64%)
  other arithmetic  64 us (13%)
  blocking collectives  50.4 us (10%)
  matrix products  34.9 us (7%)
  between operations  15.1 us (3%)
  local copies, waits for them, and re-layouts  15 us (3%)
    psum x1, waiting for transfers between devices, per_device(): gram = lax.psum(gram_part, 'space')  181 us
    psum x1, waiting for transfers between devices, per_device(): sketch = lax.psum(partial_value, 'cfg')  136 us
    all_gather x1, blocking collectives, per_device(): cross = lax.all_gather(cross_mine, 'space', axis=0, tiled=True)  50.4 us
    another operation x12, other arithmetic, blocked_cholesky(): diag = jnp.linalg.cholesky(rest[first:last, first:last])  26.2 us
    another operation x3, other arithmetic, lower_inverse(): return lax.linalg.triangular_solve(lower, ident, left_side=True, lower=True)  19.7 us
    another operation x6, other arithmetic, blocked_cholesky(): lax.linalg.triangular_solve(diag, below, left_side=False, lower=True, tra...  16.6 us
    dot_general x1, matrix products, self_gram(): return jnp.dot(block.T, block, precision=lax.Precision.HIGHEST)  11 us
  transfers between devices with their start and end apart: 2, of which 2 were waited for; matrix products, arithmetic and copies ran while one was open for 0% of the time, Pallas kernels for 0%

commit v1 on v0

v1 whole, which is shorter than its diff:
```python
import functools

import jax
import jax.numpy as jnp
from jax import lax
from jax.experimental import pallas as pl
from jax.experimental.pallas import tpu as pltpu
from jax.sharding import Mesh, PartitionSpec as P

HIGHEST = lax.Precision.HIGHEST
CHOL_BLOCK = 64
PIVOTS = 8
PAD = 16
VMEM_LIMIT = 48 * 1024 * 1024
FIRST = (((0,), (0,)), ((), ()))


def params():
    return pltpu.CompilerParams(vmem_limit_bytes=VMEM_LIMIT)


def partial_kernel(which, snap, omega, out):
    value = jnp.dot(snap[...], omega[...], preferred_element_type=jnp.float32)
    top = jnp.max(jnp.abs(value), axis=0, keepdims=True)
    power = jnp.ceil(jnp.log2(jnp.maximum(top, 1e-30))) + 1.0
    rows = value.shape[0]
    out[:rows, :] = value * jnp.exp2(14.0 - power)
    out[rows:, :] = jnp.broadcast_to(power, (PAD, power.shape[1]))


def partial_chunk(snapshots, omega, chunk, rows):
    cols, rank = omega.shape
    return pl.pallas_call(
        partial_kernel,
        grid_spec=pltpu.PrefetchScalarGridSpec(
            num_scalar_prefetch=1,
            grid=(1,),
            in_specs=[
                pl.BlockSpec((rows, cols), lambda i, which: (which[0], 0)),
                pl.BlockSpec((cols, rank), lambda i, which: (0, 0)),
            ],
            out_specs=pl.BlockSpec((rows + PAD, rank), lambda i, which: (0, 0)),
        ),
        out_shape=jax.ShapeDtypeStruct((rows + PAD, rank), jnp.float32),
        compiler_params=params(),
        name="partial_chunk",
    )(chunk, snapshots, omega)


def own_kernel(which, snap, omega, out):
    out[...] = jnp.dot(snap[...], omega[...], preferred_element_type=jnp.float32)


def own_chunk(snapshots, omega, chunk, rows):
    cols, rank = omega.shape
    return pl.pallas_call(
        own_kernel,
        grid_spec=pltpu.PrefetchScalarGridSpec(
            num_scalar_prefetch=1,
            grid=(1,),
            in_specs=[
                pl.BlockSpec((rows, cols), lambda i, which: (which[0], 0)),
                pl.BlockSpec((cols, rank), lambda i, which: (0, 0)),
            ],
            out_specs=pl.BlockSpec((rows, rank), lambda i, which: (0, 0)),
        ),
        out_shape=jax.ShapeDtypeStruct((rows, rank), jnp.float32),
        compiler_params=params(),
        name="own_chunk",
    )(chunk, snapshots, omega)


def gram_kernel(mine, out):
    rank = mine.shape[1]
    gram = lax.dot_general(mine[...], mine[...], FIRST, precision=HIGHEST)
    for h in range(rank // 128):
        out[h] = gram[:, 128 * h : 128 * (h + 1)].reshape(rank // 8, 8, 128)


def gram_tiles(mine):
    rank = mine.shape[1]
    tiles = pl.pallas_call(
        gram_kernel,
        out_shape=jax.ShapeDtypeStruct((rank // 128, rank // 8, 8, 128), jnp.float32),
        compiler_params=params(),
        name="gram_tiles",
    )(mine)
    return tiles.reshape(-1, 8, 128)


def cross_kernel(which, snap, *refs):
    lows, out = refs[:-1], refs[-1]
    step = pl.program_id(0)
    for i, low in enumerate(lows):

        @pl.when(step == i)
        def _():
            part = lax.dot_general(low[...], snap[...], FIRST, preferred_element_type=jnp.float32)
            if i == 0:
                out[...] = part
            else:
                out[...] += part


def cross_part(snapshots, order, lows):
    rows, rank = lows[0].shape
    cols = snapshots.shape[1]
    return pl.pallas_call(
        cross_kernel,
        grid_spec=pltpu.PrefetchScalarGridSpec(
            num_scalar_prefetch=1,
            grid=(len(lows),),
            in_specs=[pl.BlockSpec((rows, cols), lambda i, which: (which[i], 0))]
            + [pl.BlockSpec((rows, rank), lambda i, which: (0, 0))] * len(lows),
            out_specs=pl.BlockSpec((rank, cols), lambda i, which: (0, 0)),
        ),
        out_shape=jax.ShapeDtypeStruct((rank, cols), jnp.float32),
        compiler_params=params(),
        name="cross_part",
    )(order, snapshots, *lows)


def eliminate(groups, size, step):
    sub = lax.broadcasted_iota(jnp.int32, (8, 128), 0)
    count = size // 8
    for k in range(0, size, step):
        g, s = divmod(k, 8)
        cols = {
            i: [jnp.broadcast_to(groups[i][:, k + j : k + j + 1], (8, 128)) for j in range(step)]
            for i in range(g, count)
        }
        pivot = [
            [
                jnp.broadcast_to(cols[g][j][s + i : s + i + 1, :], (8, 128)) if j <= i else None
                for j in range(step)
            ]
            for i in range(step)
        ]
        inv, low = [], [[None] * step for _ in range(step)]
        for j in range(step):
            inv.append(1.0 / pivot[j][j])
            for i in range(j + 1, step):
                low[i][j] = pivot[i][j] * inv[j]
            for i in range(j + 1, step):
                for m in range(j + 1, i + 1):
                    pivot[i][m] = pivot[i][m] - low[i][j] * pivot[m][j]
        rows = []
        for i in range(step):
            row = jnp.broadcast_to(groups[g][s + i : s + i + 1, :], (8, 128))
            for j in range(i):
                row = row - low[i][j] * rows[j]
            rows.append(row)
        for i in range(g, count):
            new = groups[i]
            if i > g or s + step < 8:
                mult = []
                for j in range(step):
                    c = cols[i][j]
                    for q in range(j):
                        c = c - mult[q] * pivot[j][q]
                    mult.append(c * inv[j])
                for j in range(step):
                    new = new - mult[j] * rows[j]
            if i == g:
                for j in range(step):
                    new = jnp.where(sub == s + j, rows[j], new)
                if s:
                    new = jnp.where(sub < s, groups[g], new)
            groups[i] = new
    return groups


def block_inverse(block, step):
    size = block.shape[0]
    at = lambda d: lax.broadcasted_iota(jnp.int32, (size, size), d)
    eye = at(0) == at(1)
    both = jnp.concatenate([block, eye.astype(jnp.float32)], axis=1)
    groups = [both[8 * i : 8 * i + 8] for i in range(size // 8)]
    both = jnp.concatenate(eliminate(groups, size, step), axis=0)
    diag = jnp.sum(jnp.where(eye, both[:, :size], 0.0), axis=1, keepdims=True)
    return both[:, size:] * lax.rsqrt(diag)


def inverse_kernel(tiles, inverse, work, rest):
    n = work.shape[0]
    for h in range(n // 128):
        work[:, 128 * h : 128 * (h + 1)] = tiles[h].reshape(n, 128)
    inverse[...] = jnp.zeros_like(inverse)
    rest[...] = jnp.zeros_like(rest)
    for k in range(0, n, CHOL_BLOCK):
        e = k + CHOL_BLOCK
        w = block_inverse(work[k:e, k:e], PIVOTS)
        inverse[k:e, k:e] = w
        if k:
            inverse[k:e, :k] = jnp.dot(w, rest[k:e, :k], precision=HIGHEST)
        if e < n:
            solved = jnp.dot(w, work[k:e, e:], precision=HIGHEST)
            work[e:, e:] -= lax.dot_general(solved, solved, FIRST, precision=HIGHEST)
            rest[e:, :e] -= lax.dot_general(solved, inverse[k:e, :e], FIRST, precision=HIGHEST)


def lower_inverse(tiles, rank):
    return pl.pallas_call(
        inverse_kernel,
        out_shape=jax.ShapeDtypeStruct((rank, rank), jnp.float32),
        scratch_shapes=[pltpu.VMEM((rank, rank), jnp.float32)] * 2,
        compiler_params=params(),
        name="lower_inverse",
    )(tiles.reshape(rank // 128, rank // 8, 8, 128))


def coeff_kernel(inverse, cross, out, *, factor):
    value = jnp.dot(inverse[...], cross[...], precision=HIGHEST) * factor
    rank = value.shape[0]
    cores, chips, sub, _ = out.shape
    blocks = value.shape[1] // 128
    each = sub // blocks
    for q in range(blocks):
        part = value[:, 128 * q : 128 * (q + 1)].reshape(chips, cores * each, 128)
        for c in range(cores):
            out[c, :, each * q : each * (q + 1), :] = part[:, each * c : each * (c + 1), :]


def coeff_parts(inverse, cross, factor, cores, chips):
    rank, cols = cross.shape
    sub = rank // (cores * chips) * (cols // 128)
    return pl.pallas_call(
        functools.partial(coeff_kernel, factor=factor),
        out_shape=jax.ShapeDtypeStruct((cores, chips, sub, 128), jnp.float32),
        compiler_params=params(),
        name="coeff_parts",
    )(inverse, cross)


def basis_kernel(mine, inverse, out, *, factor):
    dims = (((1,), (1,)), ((), ()))
    out[...] = lax.dot_general(mine[...], inverse[...], dims, precision=HIGHEST) * factor


def basis_rows(mine, inverse, factor):
    rows, rank = mine.shape
    tile = rows // 4
    return pl.pallas_call(
        functools.partial(basis_kernel, factor=factor),
        grid=(rows // tile,),
        in_specs=[
            pl.BlockSpec((tile, rank), lambda i: (i, 0)),
            pl.BlockSpec((rank, rank), lambda i: (0, 0)),
        ],
        out_specs=pl.BlockSpec((tile, rank), lambda i: (i, 0)),
        out_shape=jax.ShapeDtypeStruct((rows, rank), jnp.float32),
        compiler_params=params(),
        name="basis_rows",
    )(mine, inverse)


def shift(value, axis, by):
    n = lax.axis_size(axis)
    return lax.ppermute(value, axis, [(i, (i + by) % n) for i in range(n)])


def per_device(snapshots, omega):
    x = lax.axis_index("x")
    nx, chips, cores = 4, lax.axis_size("z") * lax.axis_size("y"), lax.axis_size("c")
    space = ("z", "y", "c")
    rank = omega.shape[1]
    rows = snapshots.shape[0] // nx
    total_rows = snapshots.shape[0] * chips * cores
    total_cols = snapshots.shape[1] * nx
    at = lambda d: lax.rem(x + d, nx).astype(jnp.int32).reshape(1)

    mine = own_chunk(snapshots, omega, at(0), rows)
    for d in (2, 1, 3):
        sent = partial_chunk(snapshots, omega, at(d), rows).astype(jnp.float16)
        got = shift(sent, "x", d).astype(jnp.float32)
        mine = mine + got[:rows] * jnp.exp2(got[rows : rows + 1] - 14.0)
    low = mine.astype(jnp.bfloat16)

    half = rows // 2
    from_left = shift(low, "x", 1)
    from_right = shift(low, "x", -1)
    far = jnp.concatenate([shift(from_left[:half], "x", 1), shift(from_right[half:], "x", -1)], axis=0)
    order = jnp.concatenate([at(0), at(3), at(1), at(2)])
    cross = cross_part(snapshots, order, [low, from_left, from_right, far])

    tiles = gram_tiles(mine)
    tile = jnp.sum(lax.all_to_all(tiles, space, 0, 0, tiled=True), axis=0)
    tile = (tile + shift(tile, "x", 2)) + (shift(tile, "x", 1) + shift(tile, "x", 3))
    tiles = lax.all_to_all(jnp.broadcast_to(tile, tiles.shape), space, 0, 0, tiled=True)
    inverse = lower_inverse(tiles, rank)

    parts = coeff_parts(inverse, cross, (total_cols / total_rows) ** 0.5, cores, chips)
    c = lax.axis_index("c")
    keep = lax.dynamic_index_in_dim(parts, c, 0, keepdims=False)
    send = lax.dynamic_index_in_dim(parts, 1 - c, 0, keepdims=False)
    both = keep + shift(send, "c", 1)
    coeff = jnp.sum(lax.all_to_all(both, ("z", "y"), 0, 0, tiled=True), axis=0)
    blocks = snapshots.shape[1] // 128
    coeff = coeff.reshape(blocks, -1, 128).transpose(1, 0, 2).reshape(-1, snapshots.shape[1])

    basis = basis_rows(mine, inverse, total_rows**0.5)
    return basis, coeff


def solution(mesh):
    fine = Mesh(mesh.devices.reshape(8, 4, 2, 4), ("z", "y", "c", "x"))
    space = ("z", "y", "c")
    return jax.shard_map(
        per_device,
        mesh=fine,
        in_specs=(P(space, "x"), P("x", None)),
        out_specs=(P(space + ("x",), None), P(space, "x")),
        check_vma=False,
    )
```

time: 497 us -> 144 us (0.29)
  waiting for transfers between devices: 317 us -> 52.5 us
  other arithmetic: 64 us -> 7.93 us
  blocking collectives: 50.4 us -> 0 us
  starting transfers between devices: 0.08 us -> 45.3 us
  matrix products: 34.9 us -> 0 us
  Pallas kernels: 0 us -> 30 us
  between operations: 15.1 us -> 0.85 us
  local copies, waits for them, and re-layouts: 15 us -> 5.91 us
    psum x2 -> x0, waiting for transfers between devices: 317 us -> none  [the longest x1 181 us: per_device(): gram = lax.psum(gram_part, 'space')]
    another operation x21 -> x0, other arithmetic: 62.6 us -> none  [the longest x12 26.2 us: blocked_cholesky(): diag = jnp.linalg.cholesky(rest[first:last, first:last])]
    all_gather x1 -> x0, blocking collectives: 50.4 us -> none  [per_device(): cross = lax.all_gather(cross_mine, 'space', axis=0, tiled=True)]
    dot_general x8 -> x0, matrix products: 32.3 us -> none  [the longest x1 11 us: self_gram(): return jnp.dot(block.T, block, precision=lax.Precision.HIGHEST)]
    pallas_call x0 -> x9, Pallas kernels: none -> 30 us  [the longest x1 10.1 us: lower_inverse(): pl.pallas_call(inverse_kernel, out_shape=jax.ShapeDtypeStruct((rank, rank...]
    all_to_all x0 -> x3, starting transfers between devices: none -> 27.7 us  [the longest x1 12.4 us: per_device(): tile = jnp.sum(lax.all_to_all(tiles, space, 0, 0, tiled=True), axis=0)]
    all_to_all x0 -> x3, waiting for transfers between devices: none -> 26.7 us  [the longest x1 10.4 us: per_device(): tile = jnp.sum(lax.all_to_all(tiles, space, 0, 0, tiled=True), axis=0)]
    ppermute x0 -> x11, waiting for transfers between devices: none -> 25.8 us  [shift(): return lax.ppermute(value, axis, [(i, (i + by) % n) for i in range(n)])]
  transfers between devices with their start and end apart: 2 -> 14, of which waited for: 2 -> 7; matrix products, arithmetic and copies ran while one was open for 0% -> 6% of each run, Pallas kernels for 0% -> 14%
where the time goes in v1:
time: 144 us; the launch traced here: 143 us
  waiting for transfers between devices  52.5 us (36%)
  starting transfers between devices  45.3 us (31%)
  Pallas kernels  30 us (21%)
  other arithmetic  7.93 us (6%)
  local copies, waits for them, and re-layouts  5.91 us (4%)
    ppermute x11, waiting for transfers between devices, shift(): return lax.ppermute(value, axis, [(i, (i + by) % n) for i in range(n)])  25.8 us
    ppermute x11, starting transfers between devices, shift(): return lax.ppermute(value, axis, [(i, (i + by) % n) for i in range(n)])  17.6 us
    all_to_all x1, starting transfers between devices, per_device(): tile = jnp.sum(lax.all_to_all(tiles, space, 0, 0, tiled=True), axis=0)  12.4 us
    all_to_all x1, starting transfers between devices, per_device(): lax.all_to_all(jnp.broadcast_to(tile, tiles.shape), space, 0, 0, tiled=True)  11.5 us
    all_to_all x1, waiting for transfers between devices, per_device(): tile = jnp.sum(lax.all_to_all(tiles, space, 0, 0, tiled=True), axis=0)  10.4 us
    pallas_call x1, Pallas kernels, lower_inverse(): pl.pallas_call(inverse_kernel, out_shape=jax.ShapeDtypeStruct((rank, rank...  10.1 us
    all_to_all x1, waiting for transfers between devices, per_device(): coeff = jnp.sum(lax.all_to_all(both, ('z', 'y'), 0, 0, tiled=True), axis=0)  8.48 us
    all_to_all x1, waiting for transfers between devices, per_device(): lax.all_to_all(jnp.broadcast_to(tile, tiles.shape), space, 0, 0, tiled=True)  7.84 us
  transfers between devices with their start and end apart: 14, of which 7 were waited for; matrix products, arithmetic and copies ran while one was open for 6% of the time, Pallas kernels for 14%

profile of v1, /device:TPU:1, one launch (start us, length us, event | category | flops | bytes accessed | tf_op | source)
XLA Modules:
  0.0 142.6 jit_solution(7268090161848303777)
XLA Ops:
  1.6 2.1 %partial_chunk.3 = f32[1552,256]{1,0:T(8,128)S(1)} custom-call(s32[1]{0:T(128)} %bitcast.1.which, bf16[6144,512]{1,0:T(8,128)(2,1)} %snap.9, bf16[512,256]{1,0:T(8,128)(2,1)S(1)} %copy-done), custom_call_target="tpu_custom_call" | custom-call | tf_op jit(solution)/shard_map/partial_chunk/pallas_call | solution.py:33
  3.8 3.7 %collective-permute-start = (f16[1552,256]{1,0:T(8,128)(2,1)S(1)}, f16[1552,256]{1,0:T(8,128)(2,1)}, u32[]{:S(2)}, u32[]{:S(2)}) collective-permute-start(f16[1552,256]{1,0:T(8,128)(2,1)S(1)} %convert_element_type.21), channel_id=1, source_target_pairs={{0,2},{1,3},{2,0},{3,1},{4,6},{5,7},{6,4},{7,5},{8,10},{9,11},{10,... | collective-permute-start | bytes 2383880 | tf_op jit(solution)/shard_map/ppermute | solution.py:259
  7.5 2.1 %partial_chunk.4 = f32[1552,256]{1,0:T(8,128)S(1)} custom-call(s32[1]{0:T(128)} %bitcast.3.which, bf16[6144,512]{1,0:T(8,128)(2,1)} %snap.9, bf16[512,256]{1,0:T(8,128)(2,1)S(1)} %copy-done.1), custom_call_target="tpu_custom_call" | custom-call | tf_op jit(solution)/shard_map/partial_chunk/pallas_call | solution.py:33
  9.6 1.0 convert_element_type.23
  11.0 2.1 %partial_chunk.5 = f32[1552,256]{1,0:T(8,128)S(1)} custom-call(s32[1]{0:T(128)} %bitcast.5.which, bf16[6144,512]{1,0:T(8,128)(2,1)} %snap.9, bf16[512,256]{1,0:T(8,128)(2,1)S(1)} %copy-done.1), custom_call_target="tpu_custom_call" | custom-call | tf_op jit(solution)/shard_map/partial_chunk/pallas_call | solution.py:33
  13.1 1.0 convert_element_type.25
  14.1 2.4 %collective-permute-start.2 = (f16[1552,256]{1,0:T(8,128)(2,1)}, f16[1552,256]{1,0:T(8,128)(2,1)S(1)}, u32[]{:S(2)}, u32[]{:S(2)}) collective-permute-start(f16[1552,256]{1,0:T(8,128)(2,1)} %convert_element_type.25), channel_id=1, source_target_pairs={{0,3},{1,0},{2,1},{3,2},{4,7},{5,4},{6,5},{7,6},{8,11},{9,8},{10,9... | collective-permute-start | bytes 2383880 | tf_op jit(solution)/shard_map/ppermute | solution.py:259
  16.5 2.0 %own_chunk.1 = f32[1536,256]{1,0:T(8,128)S(1)} custom-call(s32[1]{0:T(128)} %bitcast.which, bf16[6144,512]{1,0:T(8,128)(2,1)} %snap.9, bf16[512,256]{1,0:T(8,128)(2,1)S(1)} %copy-done.1), custom_call_target="tpu_custom_call" | custom-call | tf_op jit(solution)/shard_map/own_chunk/pallas_call | solution.py:56
  18.4 5.5 %collective-permute-done = f16[1552,256]{1,0:T(8,128)(2,1)} collective-permute-done((f16[1552,256]{1,0:T(8,128)(2,1)S(1)}, f16[1552,256]{1,0:T(8,128)(2,1)}, u32[]{:S(2)}, u32[]{:S(2)}) %collective-permute-start) | collective-permute-done | bytes 794656 | tf_op jit(solution)/shard_map/ppermute | solution.py:259
  23.9 1.3 convert_element_type.22
  25.2 17.6 %collective-permute-done.1 = f16[1552,256]{1,0:T(8,128)(2,1)} collective-permute-done((f16[1552,256]{1,0:T(8,128)(2,1)}, f16[1552,256]{1,0:T(8,128)(2,1)}, u32[]{:S(2)}, u32[]{:S(2)}) %collective-permute-start.1) | collective-permute-done | bytes 794656 | tf_op jit(solution)/shard_map/ppermute | solution.py:259
  42.8 1.3 convert_element_type.24
  44.7 2.4 %gram_tiles.1 = f32[2,32,8,128]{3,2,1,0:T(8,128)} custom-call(f32[1536,256]{1,0:T(8,128)S(1)} %get-tuple-element.3.mine), custom_call_target="tpu_custom_call" | custom-call | tf_op jit(solution)/shard_map/gram_tiles/pallas_call | solution.py:82
  47.0 12.4 %all-to-all-start = ((f32[64,8,128]{2,1,0:T(8,128)}), f32[64,8,128]{2,1,0:T(8,128)S(1)}, u32[]{:S(2)}, u32[]{:S(2)}) async-start(f32[64,8,128]{2,1,0:T(8,128)} %bitcast.7), calls=%async_computation | async-start | bytes 524288 | tf_op jit(solution)/shard_map/all_to_all | solution.py:287
  59.4 1.4 collective-permute-start.6
  60.8 1.4 collective-permute-start.7
  62.2 10.4 %all-to-all-done = f32[64,8,128]{2,1,0:T(8,128)S(1)} async-done(((f32[64,8,128]{2,1,0:T(8,128)}), f32[64,8,128]{2,1,0:T(8,128)S(1)}, u32[]{:S(2)}, u32[]{:S(2)}) %all-to-all-start) | async-done | bytes 262176 | tf_op jit(solution)/shard_map/all_to_all | solution.py:287
  72.6 2.8 %collective-permute-start.3 = (f32[8,128]{1,0:T(8,128)S(1)}, f32[8,128]{1,0:T(8,128)S(1)}, u32[]{:S(2)}, u32[]{:S(2)}) collective-permute-start(f32[8,128]{1,0:T(8,128)S(1)} %reduce_sum.18), channel_id=1, source_target_pairs={{0,2},{1,3},{2,0},{3,1},{4,6},{5,7},{6,4},{7,5},{8,10},{9,11},{10,... | collective-permute-start | bytes 12296 | tf_op jit(solution)/shard_map/ppermute | solution.py:259
  75.5 2.7 %collective-permute-start.5 = (f32[8,128]{1,0:T(8,128)S(1)}, f32[8,128]{1,0:T(8,128)S(1)}, u32[]{:S(2)}, u32[]{:S(2)}) collective-permute-start(f32[8,128]{1,0:T(8,128)S(1)} %reduce_sum.18), channel_id=1, source_target_pairs={{0,3},{1,0},{2,1},{3,2},{4,7},{5,4},{6,5},{7,6},{8,11},{9,8},{10,9... | collective-permute-start | bytes 12296 | tf_op jit(solution)/shard_map/ppermute | solution.py:259
  78.1 1.4 collective-permute-done.3
  80.3 11.5 %all-to-all-start.1 = ((f32[64,8,128]{2,1,0:T(8,128)}), f32[64,8,128]{2,1,0:T(8,128)S(1)}, u32[]{:S(2)}, u32[]{:S(2)}) async-start(f32[64,8,128]{2,1,0:T(8,128)} %broadcast_in_dim.3), calls=%async_computation.1 | async-start | bytes 524288 | tf_op jit(solution)/shard_map/all_to_all | solution.py:289
  92.6 1.2 collective-permute-start.8
  93.8 1.8 %slice.39 = bf16[768,256]{1,0:T(8,128)(2,1)} slice(bf16[1536,256]{1,0:T(8,128)(2,1)} %collective-permute-done.7.refs_2_), slice={[768:1536], [0:256]} | slice | bytes 786432 | tf_op jit(solution)/shard_map/slice | solution.py:282
  95.5 1.5 %collective-permute-start.9 = (bf16[768,256]{1,0:T(8,128)(2,1)}, bf16[768,256]{1,0:T(8,128)(2,1)}, u32[]{:S(2)}, u32[]{:S(2)}) collective-permute-start(bf16[768,256]{1,0:T(8,128)(2,1)} %slice.39), channel_id=1, source_target_pairs={{0,3},{1,0},{2,1},{3,2},{4,7},{5,4},{6,5},{7,6},{8,11},{9,8},{10,9... | collective-permute-start | bytes 1179656 | tf_op jit(solution)/shard_map/ppermute | solution.py:259
  97.1 7.8 %all-to-all-done.1 = f32[64,8,128]{2,1,0:T(8,128)S(1)} async-done(((f32[64,8,128]{2,1,0:T(8,128)}), f32[64,8,128]{2,1,0:T(8,128)S(1)}, u32[]{:S(2)}, u32[]{:S(2)}) %all-to-all-start.1) | async-done | bytes 262176 | tf_op jit(solution)/shard_map/all_to_all | solution.py:289
  106.6 10.1 %lower_inverse.1.inverse = f32[256,256]{1,0:T(8,128)S(1)} custom-call(f32[2,32,8,128]{3,2,1,0:T(8,128)S(1)} %bitcast.18), custom_call_target="tpu_custom_call" | custom-call | tf_op jit(solution)/shard_map/lower_inverse/pallas_call | solution.py:203
  116.7 1.2 pad_maximum_fusion.refs_3_
  117.9 5.6 %cross_part.1.cross = f32[256,512]{1,0:T(8,128)S(1)} custom-call(s32[4]{0:T(128)S(1)} %pad_add_fusion.which, bf16[6144,512]{1,0:T(8,128)(2,1)} %snap.9, bf16[1536,256]{1,0:T(8,128)(2,1)S(1)} %get-tuple-element.2.refs_0_, bf16[1536,256]{1,0:T(8,128)(2,1)S(1)} %collective-permute-done.6.refs_1_, bf16[1536,256]{1,0:T(8,128)(2,1)} %collective-permute-done.7.refs_2_, ...), custom_call_target="tpu_custom_call" | custom-call | tf_op jit(solution)/shard_map/cross_part/pallas_call | solution.py:108
  124.4 1.3 collective-permute-done.10
  126.5 3.9 %all-to-all-start.2 = ((f32[32,16,128]{2,1,0:T(8,128)}), f32[32,16,128]{2,1,0:T(8,128)S(1)}, u32[]{:S(2)}, u32[]{:S(2)}) async-start(f32[32,16,128]{2,1,0:T(8,128)} %bitcast_add_fusion), calls=%async_computation.2 | async-start | bytes 524288 | tf_op jit(solution)/shard_map/all_to_all | solution.py:297
  130.4 3.1 %basis_rows.1 = f32[1536,256]{1,0:T(8,128)} custom-call(f32[1536,256]{1,0:T(8,128)S(1)} %get-tuple-element.3.mine, f32[256,256]{1,0:T(8,128)S(1)} %lower_inverse.1.inverse), custom_call_target="tpu_custom_call" | custom-call | tf_op jit(solution)/shard_map/basis_rows/pallas_call | solution.py:243
  133.5 8.5 %all-to-all-done.2 = f32[32,16,128]{2,1,0:T(8,128)S(1)} async-done(((f32[32,16,128]{2,1,0:T(8,128)}), f32[32,16,128]{2,1,0:T(8,128)S(1)}, u32[]{:S(2)}, u32[]{:S(2)}) %all-to-all-start.2) | async-done | bytes 262176 | tf_op jit(solution)/shard_map/all_to_all | solution.py:297
  (33 shorter events, 7.6 us)
Async XLA Ops:
  0.6 1.0 copy-start
  3.7 3.8 %copy-start.1 = (bf16[512,256]{1,0:T(8,128)(2,1)S(1)}, bf16[512,256]{1,0:T(8,128)(2,1)}, u32[]{:S(2)}) copy-start(bf16[512,256]{1,0:T(8,128)(2,1)} %omega.7) | copy-start | bytes 786436
  3.8 20.1 %collective-permute-start = (f16[1552,256]{1,0:T(8,128)(2,1)S(1)}, f16[1552,256]{1,0:T(8,128)(2,1)}, u32[]{:S(2)}, u32[]{:S(2)}) collective-permute-start(f16[1552,256]{1,0:T(8,128)(2,1)S(1)} %convert_element_type.21), channel_id=1, source_target_pairs={{0,2},{1,3},{2,0},{3,1},{4,6},{5,7},{6,4},{7,5},{8,10},{9,11},{10,... | collective-permute-start | bytes 2383880 | tf_op jit(solution)/shard_map/ppermute | solution.py:259
  10.7 32.2 %collective-permute-start.1 = (f16[1552,256]{1,0:T(8,128)(2,1)}, f16[1552,256]{1,0:T(8,128)(2,1)}, u32[]{:S(2)}, u32[]{:S(2)}) collective-permute-start(f16[1552,256]{1,0:T(8,128)(2,1)} %convert_element_type.23), channel_id=1, source_target_pairs={{0,1},{1,2},{2,3},{3,0},{4,5},{5,6},{6,7},{7,4},{8,9},{9,10},{10,1... | collective-permute-start | bytes 2383880 | tf_op jit(solution)/shard_map/ppermute | solution.py:259
  14.1 30.0 %collective-permute-start.2 = (f16[1552,256]{1,0:T(8,128)(2,1)}, f16[1552,256]{1,0:T(8,128)(2,1)S(1)}, u32[]{:S(2)}, u32[]{:S(2)}) collective-permute-start(f16[1552,256]{1,0:T(8,128)(2,1)} %convert_element_type.25), channel_id=1, source_target_pairs={{0,3},{1,0},{2,1},{3,2},{4,7},{5,4},{6,5},{7,6},{8,11},{9,8},{10,9... | collective-permute-start | bytes 2383880 | tf_op jit(solution)/shard_map/ppermute | solution.py:259
  47.0 25.5 %all-to-all-start = ((f32[64,8,128]{2,1,0:T(8,128)}), f32[64,8,128]{2,1,0:T(8,128)S(1)}, u32[]{:S(2)}, u32[]{:S(2)}) async-start(f32[64,8,128]{2,1,0:T(8,128)} %bitcast.7), calls=%async_computation | async-start | bytes 524288 | tf_op jit(solution)/shard_map/all_to_all | solution.py:287
  59.4 32.4 %collective-permute-start.6 = (bf16[1536,256]{1,0:T(8,128)(2,1)S(1)}, bf16[1536,256]{1,0:T(8,128)(2,1)S(1)}, u32[]{:S(2)}, u32[]{:S(2)}) collective-permute-start(bf16[1536,256]{1,0:T(8,128)(2,1)S(1)} %get-tuple-element.2.refs_0_), channel_id=1, source_target_pairs={{0,1},{1,2},{2,3},{3,0},{4,5},{5,6},{6,7},{7,4},{8,9},{9,10},{10,1... | collective-permute-start | bytes 2359304 | tf_op jit(solution)/shard_map/ppermute | solution.py:259
  60.8 33.0 %collective-permute-start.7 = (bf16[1536,256]{1,0:T(8,128)(2,1)S(1)}, bf16[1536,256]{1,0:T(8,128)(2,1)}, u32[]{:S(2)}, u32[]{:S(2)}) collective-permute-start(bf16[1536,256]{1,0:T(8,128)(2,1)S(1)} %get-tuple-element.2.refs_0_), channel_id=1, source_target_pairs={{0,3},{1,0},{2,1},{3,2},{4,7},{5,4},{6,5},{7,6},{8,11},{9,8},{10,9... | collective-permute-start | bytes 2359304 | tf_op jit(solution)/shard_map/ppermute | solution.py:259
  72.6 6.9 %collective-permute-start.3 = (f32[8,128]{1,0:T(8,128)S(1)}, f32[8,128]{1,0:T(8,128)S(1)}, u32[]{:S(2)}, u32[]{:S(2)}) collective-permute-start(f32[8,128]{1,0:T(8,128)S(1)} %reduce_sum.18), channel_id=1, source_target_pairs={{0,2},{1,3},{2,0},{3,1},{4,6},{5,7},{6,4},{7,5},{8,10},{9,11},{10,... | collective-permute-start | bytes 12296 | tf_op jit(solution)/shard_map/ppermute | solution.py:259
  75.5 4.1 %collective-permute-start.4 = (f32[8,128]{1,0:T(8,128)S(1)}, f32[8,128]{1,0:T(8,128)S(1)}, u32[]{:S(2)}, u32[]{:S(2)}) collective-permute-start(f32[8,128]{1,0:T(8,128)S(1)} %reduce_sum.18), channel_id=1, source_target_pairs={{0,1},{1,2},{2,3},{3,0},{4,5},{5,6},{6,7},{7,4},{8,9},{9,10},{10,1... | collective-permute-start | bytes 12296 | tf_op jit(solution)/shard_map/ppermute | solution.py:259
  75.5 4.1 %collective-permute-start.5 = (f32[8,128]{1,0:T(8,128)S(1)}, f32[8,128]{1,0:T(8,128)S(1)}, u32[]{:S(2)}, u32[]{:S(2)}) collective-permute-start(f32[8,128]{1,0:T(8,128)S(1)} %reduce_sum.18), channel_id=1, source_target_pairs={{0,3},{1,0},{2,1},{3,2},{4,7},{5,4},{6,5},{7,6},{8,11},{9,8},{10,9... | collective-permute-start | bytes 12296 | tf_op jit(solution)/shard_map/ppermute | solution.py:259
  80.3 24.6 %all-to-all-start.1 = ((f32[64,8,128]{2,1,0:T(8,128)}), f32[64,8,128]{2,1,0:T(8,128)S(1)}, u32[]{:S(2)}, u32[]{:S(2)}) async-start(f32[64,8,128]{2,1,0:T(8,128)} %broadcast_in_dim.3), calls=%async_computation.1 | async-start | bytes 524288 | tf_op jit(solution)/shard_map/all_to_all | solution.py:289
  92.6 24.1 %collective-permute-start.8 = (bf16[768,256]{1,0:T(8,128)(2,1)}, bf16[768,256]{1,0:T(8,128)(2,1)}, u32[]{:S(2)}, u32[]{:S(2)}) collective-permute-start(bf16[768,256]{1,0:T(8,128)(2,1)} %slice.38), channel_id=1, source_target_pairs={{0,1},{1,2},{2,3},{3,0},{4,5},{5,6},{6,7},{7,4},{8,9},{9,10},{10,1... | collective-permute-start | bytes 1179656 | tf_op jit(solution)/shard_map/ppermute | solution.py:259
  95.5 21.2 %collective-permute-start.9 = (bf16[768,256]{1,0:T(8,128)(2,1)}, bf16[768,256]{1,0:T(8,128)(2,1)}, u32[]{:S(2)}, u32[]{:S(2)}) collective-permute-start(bf16[768,256]{1,0:T(8,128)(2,1)} %slice.39), channel_id=1, source_target_pairs={{0,3},{1,0},{2,1},{3,2},{4,7},{5,4},{6,5},{7,6},{8,11},{9,8},{10,9... | collective-permute-start | bytes 1179656 | tf_op jit(solution)/shard_map/ppermute | solution.py:259
  104.9 0.7 copy-start.2
  105.6 0.9 copy-start.3
  124.1 1.6 %collective-permute-start.10 = (f32[32,16,128]{2,1,0:T(8,128)S(1)}, f32[32,16,128]{2,1,0:T(8,128)S(1)}, u32[]{:S(2)}, u32[]{:S(2)}) collective-permute-start(f32[32,16,128]{2,1,0:T(8,128)S(1)} %dynamic-slice_bitcast_fusion), channel_id=1, source_target_pairs={{0,4},{4,0},{1,5},{5,1},{2,6},{6,2},{3,7},{7,3},{8,12},{12,8},{9,1... | collective-permute-start | bytes 786440 | tf_op jit(solution)/shard_map/ppermute | solution.py:259
  126.5 15.5 %all-to-all-start.2 = ((f32[32,16,128]{2,1,0:T(8,128)}), f32[32,16,128]{2,1,0:T(8,128)S(1)}, u32[]{:S(2)}, u32[]{:S(2)}) async-start(f32[32,16,128]{2,1,0:T(8,128)} %bitcast_add_fusion), calls=%async_computation.2 | async-start | bytes 524288 | tf_op jit(solution)/shard_map/all_to_all | solution.py:297

commit v2 on v1

v2 whole, which is shorter than its diff:
```python
import functools

import jax
import jax.numpy as jnp
from jax import lax
from jax.experimental import pallas as pl
from jax.experimental.pallas import tpu as pltpu
from jax.sharding import Mesh, PartitionSpec as P

HIGHEST = lax.Precision.HIGHEST
CHOL_BLOCK = 64
PIVOTS = 8
PAD = 16
MIB = 1024 * 1024
FIRST = (((0,), (0,)), ((), ()))


def params(mib=16):
    return pltpu.CompilerParams(vmem_limit_bytes=mib * MIB)


def cost(flops, nbytes):
    return pl.CostEstimate(flops=flops, bytes_accessed=nbytes, transcendentals=0)


def sketch_kernel(which, snap, omega, out, *, scaled, pad):
    n, half, _ = out.shape
    half -= pad
    value = jnp.dot(snap[...], omega[...], preferred_element_type=jnp.float32)
    for h in range(n):
        part = value[half * h : half * (h + 1)]
        if pad:
            top = jnp.max(jnp.abs(part), axis=0, keepdims=True)
            power = jnp.ceil(jnp.log2(jnp.maximum(top, 1e-30))) + 1.0
            scale = jnp.exp2(14.0 - power)
            part = part * jnp.where(pl.program_id(0) * n + h < scaled, scale, 1.0)
            out[h, half:, :] = jnp.broadcast_to(power, (pad, power.shape[1]))
        out[h, :half, :] = part


def sketch_rows(snapshots, omega, which, half, per_step, scaled, pad, name):
    cols, rank = omega.shape
    n = which.shape[0]
    return pl.pallas_call(
        functools.partial(sketch_kernel, scaled=scaled, pad=pad),
        grid_spec=pltpu.PrefetchScalarGridSpec(
            num_scalar_prefetch=1,
            grid=(n,),
            in_specs=[
                pl.BlockSpec((per_step * half, cols), lambda i, which: (which[i], 0)),
                pl.BlockSpec((cols, rank), lambda i, which: (0, 0)),
            ],
            out_specs=pl.BlockSpec((per_step, half + pad, rank), lambda i, which: (i, 0, 0)),
        ),
        out_shape=jax.ShapeDtypeStruct((n * per_step, half + pad, rank), jnp.float32),
        compiler_params=params(48),
        cost_estimate=cost(2 * n * per_step * half * cols * rank, 4 * n * per_step * half * cols),
        name=name,
    )(which, snapshots, omega)


def add_back(got, half):
    power = got[half : half + 1].astype(jnp.float32)
    return got[:half].astype(jnp.float32) * jnp.exp2(power - 14.0)


def relay(got, later, half):
    before = got[half : half + 1].astype(jnp.float32)
    power = jnp.maximum(before, later[half : half + 1]) + 1.0
    value = got.astype(jnp.float32) * jnp.exp2(before - 14.0) + later
    value = value * jnp.exp2(14.0 - power)
    row = lax.broadcasted_iota(jnp.int32, value.shape, 0)
    return jnp.where(row < half, value, power).astype(jnp.float16)


def gram_kernel(top, bottom, out, low):
    half = top.shape[0]
    out[...] = lax.dot_general(top[...], top[...], FIRST, precision=HIGHEST) + lax.dot_general(
        bottom[...], bottom[...], FIRST, precision=HIGHEST
    )
    low[:half, :] = top[...].astype(low.dtype)
    low[half:, :] = bottom[...].astype(low.dtype)


def gram_of(top, bottom):
    rows, rank = top.shape
    return pl.pallas_call(
        gram_kernel,
        out_shape=[
            jax.ShapeDtypeStruct((rank, rank), jnp.float32),
            jax.ShapeDtypeStruct((2 * rows, rank), jnp.bfloat16),
        ],
        compiler_params=params(),
        cost_estimate=cost(24 * rows * rank * rank, 12 * rows * rank),
        name="gram_of",
    )(top, bottom)


def spread_kernel(got, out):
    total = got[0]
    for i in range(1, got.shape[0]):
        total = total + got[i]
    for i in range(out.shape[0]):
        out[i] = total


def sum_copies(got, n):
    return pl.pallas_call(
        spread_kernel,
        out_shape=jax.ShapeDtypeStruct((n,) + got.shape[1:], got.dtype),
        compiler_params=params(),
        name="sum_copies",
    )(got)


def cross_kernel(which, snap, *refs, has_before):
    refs, out = refs[:-1], refs[-1]
    before, lows = (refs[0], refs[1:]) if has_before else (None, refs)
    step = pl.program_id(0)
    for i, low in enumerate(lows):

        @pl.when(step == i)
        def _():
            part = lax.dot_general(low[...], snap[...], FIRST, preferred_element_type=jnp.float32)
            if i:
                out[...] += part
            elif before is not None:
                out[...] = before[...] + part
            else:
                out[...] = part


def cross_part(snapshots, order, lows, before=None):
    rows, rank = lows[0].shape
    cols = snapshots.shape[1]
    n = len(lows)
    whole = lambda i, which: (0, 0)
    start = [] if before is None else [before]
    return pl.pallas_call(
        functools.partial(cross_kernel, has_before=before is not None),
        grid_spec=pltpu.PrefetchScalarGridSpec(
            num_scalar_prefetch=1,
            grid=(n,),
            in_specs=[pl.BlockSpec((rows, cols), lambda i, which: (which[i], 0))]
            + [pl.BlockSpec((rank, cols), whole)] * len(start)
            + [pl.BlockSpec((rows, rank), whole)] * n,
            out_specs=pl.BlockSpec((rank, cols), whole),
        ),
        out_shape=jax.ShapeDtypeStruct((rank, cols), jnp.float32),
        compiler_params=params(48),
        cost_estimate=cost(2 * n * rows * cols * rank, 2 * n * rows * (cols + rank)),
        name="cross_part",
    )(order, snapshots, *start, *lows)


def eliminate(groups, size, step):
    sub = lax.broadcasted_iota(jnp.int32, (8, 128), 0)
    count = size // 8
    for k in range(0, size, step):
        g, s = divmod(k, 8)
        cols = {
            i: [jnp.broadcast_to(groups[i][:, k + j : k + j + 1], (8, 128)) for j in range(step)]
            for i in range(g, count)
        }
        pivot = [
            [
                jnp.broadcast_to(cols[g][j][s + i : s + i + 1, :], (8, 128)) if j <= i else None
                for j in range(step)
            ]
            for i in range(step)
        ]
        inv, low = [], [[None] * step for _ in range(step)]
        for j in range(step):
            if j % 2 == 0:
                a, b, d = pivot[j][j], pivot[j + 1][j], pivot[j + 1][j + 1]
                guess = a * (1.0 / (a * d - b * b))
                inv.append(1.0 / a)
            else:
                inv.append(guess * (2.0 - pivot[j][j] * guess))
            for i in range(j + 1, step):
                low[i][j] = pivot[i][j] * inv[j]
            for i in range(j + 1, step):
                for m in range(j + 1, i + 1):
                    pivot[i][m] = pivot[i][m] - low[i][j] * pivot[m][j]
        rows = []
        for i in range(step):
            row = jnp.broadcast_to(groups[g][s + i : s + i + 1, :], (8, 128))
            for j in range(i):
                row = row - low[i][j] * rows[j]
            rows.append(row)
        for i in range(g, count):
            new = groups[i]
            if i > g or s + step < 8:
                mult = []
                for j in range(step):
                    c = cols[i][j]
                    for q in range(j):
                        c = c - mult[q] * pivot[j][q]
                    mult.append(c * inv[j])
                for j in range(step):
                    new = new - mult[j] * rows[j]
            if i == g:
                for j in range(step):
                    new = jnp.where(sub == s + j, rows[j], new)
                if s:
                    new = jnp.where(sub < s, groups[g], new)
            groups[i] = new
    return groups


def block_inverse(block, step):
    size = block.shape[0]
    at = lambda d: lax.broadcasted_iota(jnp.int32, (size, size), d)
    eye = at(0) == at(1)
    both = jnp.concatenate([block, eye.astype(jnp.float32)], axis=1)
    groups = [both[8 * i : 8 * i + 8] for i in range(size // 8)]
    both = jnp.concatenate(eliminate(groups, size, step), axis=0)
    diag = jnp.sum(jnp.where(eye, both[:, :size], 0.0), axis=1, keepdims=True)
    return both[:, size:] * lax.rsqrt(diag)


def inverse_kernel(core, held, other, inverse, work, rest):
    n = work.shape[0]
    half = n // 2
    work[pl.ds(pl.multiple_of(core[0] * half, half), half), :] = held[...]
    work[pl.ds(pl.multiple_of((1 - core[0]) * half, half), half), :] = other[...]
    inverse[...] = jnp.zeros_like(inverse)
    rest[...] = jnp.zeros_like(rest)
    for k in range(0, n, CHOL_BLOCK):
        e = k + CHOL_BLOCK
        w = block_inverse(work[k:e, k:e], PIVOTS)
        inverse[k:e, k:e] = w
        if k:
            inverse[k:e, :k] = jnp.dot(w, rest[k:e, :k], precision=HIGHEST)
        if e < n:
            solved = jnp.dot(w, work[k:e, e:], precision=HIGHEST)
            work[e:, e:] -= lax.dot_general(solved, solved, FIRST, precision=HIGHEST)
            rest[e:, :e] -= lax.dot_general(solved, inverse[k:e, :e], FIRST, precision=HIGHEST)


def lower_inverse(core, held, other):
    half, rank = held.shape
    return pl.pallas_call(
        inverse_kernel,
        grid_spec=pltpu.PrefetchScalarGridSpec(
            num_scalar_prefetch=1,
            grid=(1,),
            in_specs=[pl.BlockSpec((half, rank), lambda i, core: (0, 0))] * 2,
            out_specs=pl.BlockSpec((rank, rank), lambda i, core: (0, 0)),
            scratch_shapes=[pltpu.VMEM((rank, rank), jnp.float32)] * 2,
        ),
        out_shape=jax.ShapeDtypeStruct((rank, rank), jnp.float32),
        compiler_params=params(),
        cost_estimate=cost(5 * 10**9, 4 * rank * rank),
        name="lower_inverse",
    )(core, held, other)


def coeff_kernel(which, inverse, near, low, snap, out, *, factor):
    cross = near[...] + lax.dot_general(
        low[...], snap[...], FIRST, preferred_element_type=jnp.float32
    )
    value = jnp.dot(inverse[...], cross, precision=HIGHEST) * factor
    cores, chips, sub, _ = out.shape
    blocks = value.shape[1] // 128
    each = sub // blocks
    for q in range(blocks):
        part = value[:, 128 * q : 128 * (q + 1)].reshape(chips, cores * each, 128)
        for c in range(cores):
            out[c, :, each * q : each * (q + 1), :] = part[:, each * c : each * (c + 1), :]


def coeff_parts(inverse, near, low, snapshots, block, factor, cores, chips):
    rank, cols = near.shape
    rows = low.shape[0]
    sub = rank // (cores * chips) * (cols // 128)
    whole = lambda *shape: pl.BlockSpec(shape, lambda i, which: (0,) * len(shape))
    return pl.pallas_call(
        functools.partial(coeff_kernel, factor=factor),
        grid_spec=pltpu.PrefetchScalarGridSpec(
            num_scalar_prefetch=1,
            grid=(1,),
            in_specs=[
                whole(rank, rank),
                whole(rank, cols),
                whole(rows, rank),
                pl.BlockSpec((rows, cols), lambda i, which: (which[0], 0)),
            ],
            out_specs=whole(cores, chips, sub, 128),
        ),
        out_shape=jax.ShapeDtypeStruct((cores, chips, sub, 128), jnp.float32),
        compiler_params=params(48),
        cost_estimate=cost(2 * rows * cols * rank + 12 * rank * rank * cols, 2 * rows * cols),
        name="coeff_parts",
    )(block, inverse, near, low, snapshots)


def basis_kernel(top, bottom, inverse, out, *, factor, steps):
    dims = (((1,), (1,)), ((), ()))
    mine = jnp.where(pl.program_id(0) < steps, top[...], bottom[...])
    out[...] = lax.dot_general(mine, inverse[...], dims, precision=HIGHEST) * factor


def basis_rows(top, bottom, inverse, factor):
    rows, rank = top.shape
    steps = 2
    tile = rows // steps
    return pl.pallas_call(
        functools.partial(basis_kernel, factor=factor, steps=steps),
        grid=(2 * steps,),
        in_specs=[
            pl.BlockSpec((tile, rank), lambda i: (jnp.minimum(i, steps - 1), 0)),
            pl.BlockSpec((tile, rank), lambda i: (jnp.maximum(i - steps, 0), 0)),
            pl.BlockSpec((rank, rank), lambda i: (0, 0)),
        ],
        out_specs=pl.BlockSpec((tile, rank), lambda i: (i, 0)),
        out_shape=jax.ShapeDtypeStruct((2 * rows, rank), jnp.float32),
        compiler_params=params(),
        cost_estimate=cost(24 * rows * rank * rank, 16 * rows * rank),
        name="basis_rows",
    )(top, bottom, inverse)


def shift(value, axis, by):
    n = lax.axis_size(axis)
    return lax.ppermute(value, axis, [(i, (i + by) % n) for i in range(n)])


def exchange(value, axes):
    return lax.all_to_all(value, axes, 0, 0, tiled=True)


def per_device(snapshots, omega):
    x, c = lax.axis_index("x"), lax.axis_index("c")
    nx, nz, cores = lax.axis_size("x"), lax.axis_size("z"), lax.axis_size("c")
    chips = nz * lax.axis_size("y")
    cols, rank = omega.shape
    rows = snapshots.shape[0] // nx
    half = rows // 2
    total_rows = snapshots.shape[0] * chips * cores
    total_cols = cols * nx
    ahead = lambda d: 2 * lax.rem(x + d, nx)
    at = lambda *places: jnp.stack(places).astype(jnp.int32)
    sketch = functools.partial(sketch_rows, snapshots, omega, half=half)
    half16 = lambda v: v.astype(jnp.float16)

    far = sketch(which=at(lax.rem(x + 2, nx)), per_step=2, scaled=2, pad=PAD, name="far_chunk")
    far_up, far_down = shift(half16(far[0]), "x", 1), shift(half16(far[1]), "x", -1)
    places = at(ahead(1) + 1, ahead(3), ahead(1), ahead(3) + 1)
    near = sketch(which=places, per_step=1, scaled=2, pad=PAD, name="near_chunks")
    near_up, near_down = shift(half16(near[0]), "x", 1), shift(half16(near[1]), "x", -1)
    own = sketch(which=at(x), per_step=2, scaled=0, pad=0, name="own_chunk")
    far_up = shift(relay(far_up, near[2], half), "x", 1)
    far_down = shift(relay(far_down, near[3], half), "x", -1)
    top = own[0] + add_back(near_down, half) + add_back(far_up, half)
    bottom = own[1] + add_back(near_up, half) + add_back(far_down, half)

    tie = lax.optimization_barrier
    block = lambda *ds: at(*[lax.rem(x + d, nx) for d in ds])
    gram, low = gram_of(top, bottom)
    halves = gram.reshape(cores, rank // cores, rank)
    pick = lambda v, i: lax.dynamic_index_in_dim(v, i, 0, keepdims=False)
    held = pick(halves, c) + shift(pick(halves, 1 - c), "c", 1)
    held, low = tie((held, low))
    left, right = shift(low, "x", 1), shift(low, "x", -1)
    cross = cross_part(snapshots, block(0), [low])
    held, cross = tie((exchange(held.reshape(nz, -1, rank), "z"), cross))

    held = exchange(sum_copies(held, lax.axis_size("y") * nx), ("y", "x"))

    held, low, cross = tie((sum_copies(held, nz), low, cross))
    across = shift(low, "x", 2)
    cross = cross_part(snapshots, block(3, 1), [left, right], cross)
    held, cross = tie((exchange(held, "z").reshape(-1, rank), cross))
    other = shift(held, "c", 1)
    inverse = lower_inverse(c.astype(jnp.int32).reshape(1), held, other)

    factor = (total_cols / total_rows) ** 0.5
    parts = coeff_parts(inverse, cross, across, snapshots, block(2), factor, cores, chips)
    both = pick(parts, c) + shift(pick(parts, 1 - c), "c", 1)
    coeff = jnp.sum(exchange(both, ("z", "y")), axis=0)
    coeff = coeff.reshape(cols // 128, -1, 128).transpose(1, 0, 2).reshape(-1, cols)

    basis = basis_rows(top, bottom, inverse, total_rows**0.5)
    return basis, coeff


def solution(mesh):
    fine = Mesh(mesh.devices.reshape(8, 4, 2, 4), ("z", "y", "c", "x"))
    space = ("z", "y", "c")
    return jax.shard_map(
        per_device,
        mesh=fine,
        in_specs=(P(space, "x"), P("x", None)),
        out_specs=(P(space + ("x",), None), P(space, "x")),
        check_vma=False,
    )
```

time: 144 us -> 123 us (0.85)
  waiting for transfers between devices: 52.5 us -> 30.2 us
  blocking collectives: 0 us -> 12.9 us
  starting transfers between devices: 45.3 us -> 36.3 us
  local copies, waits for them, and re-layouts: 5.91 us -> 3.14 us
  Pallas kernels: 30 us -> 31.6 us
    ppermute x11 -> x12, waiting for transfers between devices: 25.8 us -> 11.9 us  [shift(): return lax.ppermute(value, axis, [(i, (i + by) % n) for i in range(n)])]
    all_to_all x0 -> x1, blocking collectives: none -> 12.9 us  [exchange(): return lax.all_to_all(value, axes, 0, 0, tiled=True)]
    all_to_all x3, starting transfers between devices: 27.7 us -> 16.5 us  [exchange(): return lax.all_to_all(value, axes, 0, 0, tiled=True)]
    all_to_all x3, waiting for transfers between devices: 26.7 us -> 18.3 us  [exchange(): return lax.all_to_all(value, axes, 0, 0, tiled=True)]
    convert_element_type x7 -> x1, other arithmetic: 5.23 us -> 1.49 us  [relay(): return jnp.where(row < half, value, power).astype(jnp.float16)]
    slice x2 -> x0, local copies, waits for them, and re-layouts: 2.56 us -> none  [the longest x1 1.77 us: per_device(): from_right[half:]]
    ppermute x11 -> x12, starting transfers between devices: 17.6 us -> 19.8 us  [shift(): return lax.ppermute(value, axis, [(i, (i + by) % n) for i in range(n)])]
    add x2 -> x3, other arithmetic: 0.73 us -> 2.88 us  [the longest x1 1.49 us: per_device(): bottom = own[1] + add_back(near_up, half) + add_back(far_down, half)]
  transfers between devices with their start and end apart: 14 -> 15, of which waited for: 7 -> 10; matrix products, arithmetic and copies ran while one was open for 6% -> 4% of each run, Pallas kernels for 14% -> 20%
where the time goes in v2:
time: 123 us
  starting transfers between devices  36.3 us (30%)
  Pallas kernels  31.6 us (26%)
  waiting for transfers between devices  30.2 us (25%)
  blocking collectives  12.9 us (10%)
  other arithmetic  7.62 us (6%)
  local copies, waits for them, and re-layouts  3.14 us (3%)
    ppermute x12, starting transfers between devices, shift(): return lax.ppermute(value, axis, [(i, (i + by) % n) for i in range(n)])  19.8 us
    all_to_all x3, waiting for transfers between devices, exchange(): return lax.all_to_all(value, axes, 0, 0, tiled=True)  18.3 us
    all_to_all x3, starting transfers between devices, exchange(): return lax.all_to_all(value, axes, 0, 0, tiled=True)  16.5 us
    all_to_all x1, blocking collectives, exchange(): return lax.all_to_all(value, axes, 0, 0, tiled=True)  12.9 us
    ppermute x12, waiting for transfers between devices, shift(): return lax.ppermute(value, axis, [(i, (i + by) % n) for i in range(n)])  11.9 us
    pallas_call x1, Pallas kernels, lower_inverse(): pl.pallas_call(inverse_kernel, grid_spec=pltpu.PrefetchScalarGridSpec(num...  9.7 us
    pallas_call x3, Pallas kernels, sketch_rows(): pl.pallas_call(functools.partial(sketch_kernel, scaled=scaled, pad=pad),...  8.32 us
    pallas_call x2, Pallas kernels, cross_part(): pl.pallas_call(functools.partial(cross_kernel, has_before=before is not N...  5.2 us
  transfers between devices with their start and end apart: 15, of which 10 were waited for; matrix products, arithmetic and copies ran while one was open for 4% of the time, Pallas kernels for 20%

profile of v2, /device:TPU:1, one launch (start us, length us, event | category | flops | bytes accessed | tf_op | source)
XLA Modules:
  0.0 122.7 jit_solution(3860451140565763412)
XLA Ops:
  1.6 2.1 %far_chunk.1 = f32[2,784,256]{2,1,0:T(8,128)S(1)} custom-call(s32[1]{0:T(128)} %bitcast.8.which, bf16[6144,512]{1,0:T(8,128)(2,1)} %snap.11, bf16[512,256]{1,0:T(8,128)(2,1)S(1)} %copy-done), custom_call_target="tpu_custom_call" | custom-call | flops 402653184 | bytes 3145728 | tf_op jit(solution)/shard_map/far_chunk/pallas_call | solution.py:44
  3.8 1.1 slice_bitcast_fusion.4
  4.9 2.0 %collective-permute-start.1 = (f16[784,256]{1,0:T(8,128)(2,1)}, f16[784,256]{1,0:T(8,128)(2,1)}, u32[]{:S(2)}, u32[]{:S(2)}) collective-permute-start(f16[784,256]{1,0:T(8,128)(2,1)} %get-tuple-element.37), channel_id=1, source_target_pairs={{0,1},{1,2},{2,3},{3,0},{4,5},{5,6},{6,7},{7,4},{8,9},{9,10},{10,1... | collective-permute-start | bytes 1204232 | tf_op jit(solution)/shard_map/ppermute | solution.py:326
  6.9 1.3 %collective-permute-start.4 = (f16[784,256]{1,0:T(8,128)(2,1)}, f16[784,256]{1,0:T(8,128)(2,1)}, u32[]{:S(2)}, u32[]{:S(2)}) collective-permute-start(f16[784,256]{1,0:T(8,128)(2,1)} %get-tuple-element.36), channel_id=1, source_target_pairs={{0,3},{1,0},{2,1},{3,2},{4,7},{5,4},{6,5},{7,6},{8,11},{9,8},{10,9... | collective-permute-start | bytes 1204232 | tf_op jit(solution)/shard_map/ppermute | solution.py:326
  8.3 4.3 %near_chunks.1 = f32[4,784,256]{2,1,0:T(8,128)S(1)} custom-call(s32[4]{0:T(128)S(1)} %pad_add_fusion.which, bf16[6144,512]{1,0:T(8,128)(2,1)} %snap.11, bf16[512,256]{1,0:T(8,128)(2,1)S(1)} %copy-done.1), custom_call_target="tpu_custom_call" | custom-call | flops 805306368 | bytes 6291456 | tf_op jit(solution)/shard_map/near_chunks/pallas_call | solution.py:44
  12.8 1.1 slice_bitcast_fusion.5
  14.1 2.5 %collective-permute-start = (f16[784,256]{1,0:T(8,128)(2,1)}, f16[784,256]{1,0:T(8,128)(2,1)}, u32[]{:S(2)}, u32[]{:S(2)}) collective-permute-start(f16[784,256]{1,0:T(8,128)(2,1)} %get-tuple-element.33), channel_id=1, source_target_pairs={{0,3},{1,0},{2,1},{3,2},{4,7},{5,4},{6,5},{7,6},{8,11},{9,8},{10,9... | collective-permute-start | bytes 1204232 | tf_op jit(solution)/shard_map/ppermute | solution.py:326
  16.5 2.0 %own_chunk.1 = f32[2,768,256]{2,1,0:T(8,128)S(1)} custom-call(s32[1]{0:T(128)} %bitcast.which, bf16[6144,512]{1,0:T(8,128)(2,1)} %snap.11, bf16[512,256]{1,0:T(8,128)(2,1)S(1)} %copy-done.1), custom_call_target="tpu_custom_call" | custom-call | flops 402653184 | bytes 3145728 | tf_op jit(solution)/shard_map/own_chunk/pallas_call | solution.py:44
  19.3 1.5 %fusion.3 = (f16[784,256]{1,0:T(8,128)(2,1)S(1)}, f16[784,256]{1,0:T(8,128)(2,1)S(1)}) fusion(f32[4,784,256]{2,1,0:T(8,128)S(1)} %near_chunks.1, f16[784,256]{1,0:T(8,128)(2,1)} %collective-permute-done.4, f32[256]{0:T(256)S(1)} %bitcast.96, f32[256]{0:T(256)S(1)} %bitcast.95, f32[256]{0:T(256)S(1)} %bitcast.100, pred[784]{0:T(1024)(128)(4,1)S(1)} %iota_compare_fusion, ...), kind=kLoop, calls=%fused_computation.4 | loop fusion | flops 2408448 | bytes 3218192 | tf_op jit(solution)/shard_map/convert_element_type | solution.py:73
  20.8 2.7 %collective-permute-start.5 = (f16[784,256]{1,0:T(8,128)(2,1)S(1)}, f16[784,256]{1,0:T(8,128)(2,1)S(1)}, u32[]{:S(2)}, u32[]{:S(2)}) collective-permute-start(f16[784,256]{1,0:T(8,128)(2,1)S(1)} %get-tuple-element.28), channel_id=1, source_target_pairs={{0,3},{1,0},{2,1},{3,2},{4,7},{5,4},{6,5},{7,6},{8,11},{9,8},{10,9... | collective-permute-start | bytes 1204232 | tf_op jit(solution)/shard_map/ppermute | solution.py:326
  25.9 7.5 %collective-permute-done.2 = f16[784,256]{1,0:T(8,128)(2,1)S(1)} collective-permute-done((f16[784,256]{1,0:T(8,128)(2,1)S(1)}, f16[784,256]{1,0:T(8,128)(2,1)S(1)}, u32[]{:S(2)}, u32[]{:S(2)}) %collective-permute-start.2) | collective-permute-done | bytes 401440 | tf_op jit(solution)/shard_map/ppermute | solution.py:326
  33.7 1.5 %fusion.9 = (f32[768,256]{1,0:T(8,128)S(1)}, f32[768,256]{1,0:T(8,128)S(1)}) fusion(f32[2,768,256]{2,1,0:T(8,128)S(1)} %own_chunk.1, f16[784,256]{1,0:T(8,128)(2,1)S(1)} %collective-permute-done.5, f16[784,256]{1,0:T(8,128)(2,1)} %collective-permute-done.3, f32[256]{0:T(256)S(1)} %bitcast.104, f32[256]{0:T(256)S(1)} %bitcast.101, f32[256]{0:T(256)S(1)} %bitcast.103, ...), kind=kLoop, calls=%fused_computation.12 | loop fusion | flops 2359296 | bytes 4722688 | tf_op jit(solution)/shard_map/add | solution.py:356
  35.2 1.7 %gram_of.1 = (f32[256,256]{1,0:T(8,128)S(1)}, bf16[1536,256]{1,0:T(8,128)(2,1)S(1)}) custom-call(f32[768,256]{1,0:T(8,128)S(1)} %get-tuple-element.35.top, f32[768,256]{1,0:T(8,128)S(1)} %get-tuple-element.34.bottom), custom_call_target="tpu_custom_call" | custom-call | flops 1207959552 | bytes 2359296 | tf_op jit(solution)/shard_map/gram_of/pallas_call | solution.py:87
  36.9 2.5 %collective-permute-start.6 = (f32[128,256]{1,0:T(8,128)S(1)}, f32[128,256]{1,0:T(8,128)S(1)}, u32[]{:S(2)}, u32[]{:S(2)}) collective-permute-start(f32[128,256]{1,0:T(8,128)S(1)} %dynamic-slice_bitcast_fusion.1), channel_id=1, source_target_pairs={{0,4},{4,0},{1,5},{5,1},{2,6},{6,2},{3,7},{7,3},{8,12},{12,8},{9,1... | collective-permute-start | bytes 393224 | tf_op jit(solution)/shard_map/ppermute | solution.py:326
  39.4 1.0 collective-permute-done.6
  41.1 1.2 collective-permute-start.7
  42.3 1.5 %collective-permute-start.8 = (bf16[1536,256]{1,0:T(8,128)(2,1)S(1)}, bf16[1536,256]{1,0:T(8,128)(2,1)S(1)}, u32[]{:S(2)}, u32[]{:S(2)}) collective-permute-start(bf16[1536,256]{1,0:T(8,128)(2,1)S(1)} %get-tuple-element.23.refs_0_), channel_id=1, source_target_pairs={{0,3},{1,0},{2,1},{3,2},{4,7},{5,4},{6,5},{7,6},{8,11},{9,8},{10,9... | collective-permute-start | bytes 2359304 | tf_op jit(solution)/shard_map/ppermute | solution.py:326
  43.7 8.2 %all-to-all-start = ((f32[8,16,256]{2,1,0:T(8,128)}), f32[8,16,256]{2,1,0:T(8,128)S(1)}, u32[]{:S(2)}, u32[]{:S(2)}) async-start(f32[8,16,256]{2,1,0:T(8,128)} %bitcast.30), calls=%async_computation | async-start | bytes 262144 | tf_op jit(solution)/shard_map/all_to_all | solution.py:330
  51.9 2.0 %cross_part.2.refs_0_ = f32[256,512]{1,0:T(8,128)S(1)} custom-call(s32[1]{0:T(128)} %bitcast.31.which, bf16[6144,512]{1,0:T(8,128)(2,1)} %snap.11, bf16[1536,256]{1,0:T(8,128)(2,1)S(1)} %get-tuple-element.23.refs_0_), custom_call_target="tpu_custom_call" | custom-call | flops 402653184 | bytes 2359296 | tf_op jit(solution)/shard_map/cross_part/pallas_call | solution.py:139
  53.9 5.9 %all-to-all-done.got = f32[8,16,256]{2,1,0:T(8,128)S(1)} async-done(((f32[8,16,256]{2,1,0:T(8,128)}), f32[8,16,256]{2,1,0:T(8,128)S(1)}, u32[]{:S(2)}, u32[]{:S(2)}) %all-to-all-start) | async-done | bytes 131104 | tf_op jit(solution)/shard_map/all_to_all | solution.py:330
  59.9 12.9 %all_to_all.20.got = f32[16,16,256]{2,1,0:T(8,128)S(1)} all-to-all(f32[16,16,256]{2,1,0:T(8,128)S(1)} %sum_copies.2), channel_id=1, replica_groups=mesh['z'=8,'y'=4,'c'=2,'x'=4] {'y','x'}, dimensions={0} | all-to-all | bytes 524288 | tf_op jit(solution)/shard_map/all_to_all | solution.py:330
  73.5 3.4 %all-to-all-start.2 = ((f32[8,16,256]{2,1,0:T(8,128)}), f32[8,16,256]{2,1,0:T(8,128)S(1)}, u32[]{:S(2)}, u32[]{:S(2)}) async-start(f32[8,16,256]{2,1,0:T(8,128)} %sum_copies.3), calls=%async_computation.2 | async-start | bytes 262144 | tf_op jit(solution)/shard_map/all_to_all | solution.py:330
  77.6 3.2 %cross_part.3.near = f32[256,512]{1,0:T(8,128)S(1)} custom-call(s32[2]{0:T(128)S(1)} %pad_add_fusion.1.which, bf16[6144,512]{1,0:T(8,128)(2,1)} %snap.11, f32[256,512]{1,0:T(8,128)S(1)} %cross_part.2.refs_0_, bf16[1536,256]{1,0:T(8,128)(2,1)S(1)} %collective-permute-done.7.refs_1_, bf16[1536,256]{1,0:T(8,128)(2,1)S(1)} %collective-permute-done.8.refs_2_), custom_call_target="tpu_custom_call" | custom-call | flops 805306368 | bytes 4718592 | tf_op jit(solution)/shard_map/cross_part/pallas_call | solution.py:139
  80.8 3.9 %all-to-all-done.2 = f32[8,16,256]{2,1,0:T(8,128)S(1)} async-done(((f32[8,16,256]{2,1,0:T(8,128)}), f32[8,16,256]{2,1,0:T(8,128)S(1)}, u32[]{:S(2)}, u32[]{:S(2)}) %all-to-all-start.2) | async-done | bytes 131104 | tf_op jit(solution)/shard_map/all_to_all | solution.py:330
  84.7 4.8 %collective-permute-start.9 = (f32[128,256]{1,0:T(8,128)S(1)}, f32[128,256]{1,0:T(8,128)S(1)}, u32[]{:S(2)}, u32[]{:S(2)}) collective-permute-start(f32[128,256]{1,0:T(8,128)S(1)} %bitcast.92), channel_id=1, source_target_pairs={{0,4},{4,0},{1,5},{5,1},{2,6},{6,2},{3,7},{7,3},{8,12},{12,8},{9,1... | collective-permute-start | bytes 393224 | tf_op jit(solution)/shard_map/ppermute | solution.py:326
  89.5 1.0 collective-permute-done.9.other
  90.5 9.7 %lower_inverse.1.inverse = f32[256,256]{1,0:T(8,128)S(1)} custom-call(s32[1]{0:T(128)} %bitcast.26.core, f32[128,256]{1,0:T(8,128)S(1)} %bitcast.93, f32[128,256]{1,0:T(8,128)S(1)} %collective-permute-done.9.other), custom_call_target="tpu_custom_call" | custom-call | flops 5000000000 | bytes 262144 | tf_op jit(solution)/shard_map/lower_inverse/pallas_call | solution.py:243
  100.2 2.9 %coeff_parts.1 = f32[2,32,16,128]{3,2,1,0:T(8,128)S(1)} custom-call(s32[1]{0:T(128)} %bitcast.8.which, f32[256,256]{1,0:T(8,128)S(1)} %lower_inverse.1.inverse, f32[256,512]{1,0:T(8,128)S(1)} %cross_part.3.near, bf16[1536,256]{1,0:T(8,128)(2,1)} %collective-permute-done.10.low, bf16[6144,512]{1,0:T(8,128)(2,1)} %snap.11), custom_call_target="tpu_custom_call" | custom-call | flops 805306368 | bytes 1572864 | tf_op jit(solution)/shard_map/coeff_parts/pallas_call | solution.py:278
  103.6 1.2 collective-permute-done.11
  105.5 4.9 %all-to-all-start.3 = ((f32[32,16,128]{2,1,0:T(8,128)}), f32[32,16,128]{2,1,0:T(8,128)S(1)}, u32[]{:S(2)}, u32[]{:S(2)}) async-start(f32[32,16,128]{2,1,0:T(8,128)} %bitcast_add_fusion), calls=%async_computation.3 | async-start | bytes 524288 | tf_op jit(solution)/shard_map/all_to_all | solution.py:330
  110.5 3.1 %basis_rows.1 = f32[1536,256]{1,0:T(8,128)} custom-call(f32[768,256]{1,0:T(8,128)S(1)} %copy-done.5, f32[768,256]{1,0:T(8,128)S(1)} %copy-done.3, f32[256,256]{1,0:T(8,128)S(1)} %lower_inverse.1.inverse), custom_call_target="tpu_custom_call" | custom-call | flops 1207959552 | bytes 3145728 | tf_op jit(solution)/shard_map/basis_rows/pallas_call | solution.py:308
  113.6 8.5 %all-to-all-done.3 = f32[32,16,128]{2,1,0:T(8,128)S(1)} async-done(((f32[32,16,128]{2,1,0:T(8,128)}), f32[32,16,128]{2,1,0:T(8,128)S(1)}, u32[]{:S(2)}, u32[]{:S(2)}) %all-to-all-start.3) | async-done | bytes 262176 | tf_op jit(solution)/shard_map/all_to_all | solution.py:330
  (41 shorter events, 9.0 us)
Async XLA Ops:
  0.6 1.0 copy-start
  3.7 4.6 %copy-start.1 = (bf16[512,256]{1,0:T(8,128)(2,1)S(1)}, bf16[512,256]{1,0:T(8,128)(2,1)}, u32[]{:S(2)}) copy-start(bf16[512,256]{1,0:T(8,128)(2,1)} %omega.5) | copy-start | bytes 786436
  4.9 13.6 %collective-permute-start.1 = (f16[784,256]{1,0:T(8,128)(2,1)}, f16[784,256]{1,0:T(8,128)(2,1)}, u32[]{:S(2)}, u32[]{:S(2)}) collective-permute-start(f16[784,256]{1,0:T(8,128)(2,1)} %get-tuple-element.37), channel_id=1, source_target_pairs={{0,1},{1,2},{2,3},{3,0},{4,5},{5,6},{6,7},{7,4},{8,9},{9,10},{10,1... | collective-permute-start | bytes 1204232 | tf_op jit(solution)/shard_map/ppermute | solution.py:326
  6.9 11.6 %collective-permute-start.4 = (f16[784,256]{1,0:T(8,128)(2,1)}, f16[784,256]{1,0:T(8,128)(2,1)}, u32[]{:S(2)}, u32[]{:S(2)}) collective-permute-start(f16[784,256]{1,0:T(8,128)(2,1)} %get-tuple-element.36), channel_id=1, source_target_pairs={{0,3},{1,0},{2,1},{3,2},{4,7},{5,4},{6,5},{7,6},{8,11},{9,8},{10,9... | collective-permute-start | bytes 1204232 | tf_op jit(solution)/shard_map/ppermute | solution.py:326
  13.9 9.7 %collective-permute-start.3 = (f16[784,256]{1,0:T(8,128)(2,1)}, f16[784,256]{1,0:T(8,128)(2,1)}, u32[]{:S(2)}, u32[]{:S(2)}) collective-permute-start(f16[784,256]{1,0:T(8,128)(2,1)} %get-tuple-element.32), channel_id=1, source_target_pairs={{0,1},{1,2},{2,3},{3,0},{4,5},{5,6},{6,7},{7,4},{8,9},{9,10},{10,1... | collective-permute-start | bytes 1204232 | tf_op jit(solution)/shard_map/ppermute | solution.py:326
  14.1 11.1 %collective-permute-start = (f16[784,256]{1,0:T(8,128)(2,1)}, f16[784,256]{1,0:T(8,128)(2,1)}, u32[]{:S(2)}, u32[]{:S(2)}) collective-permute-start(f16[784,256]{1,0:T(8,128)(2,1)} %get-tuple-element.33), channel_id=1, source_target_pairs={{0,3},{1,0},{2,1},{3,2},{4,7},{5,4},{6,5},{7,6},{8,11},{9,8},{10,9... | collective-permute-start | bytes 1204232 | tf_op jit(solution)/shard_map/ppermute | solution.py:326
  20.8 12.6 %collective-permute-start.2 = (f16[784,256]{1,0:T(8,128)(2,1)S(1)}, f16[784,256]{1,0:T(8,128)(2,1)S(1)}, u32[]{:S(2)}, u32[]{:S(2)}) collective-permute-start(f16[784,256]{1,0:T(8,128)(2,1)S(1)} %get-tuple-element.29), channel_id=1, source_target_pairs={{0,1},{1,2},{2,3},{3,0},{4,5},{5,6},{6,7},{7,4},{8,9},{9,10},{10,1... | collective-permute-start | bytes 1204232 | tf_op jit(solution)/shard_map/ppermute | solution.py:326
  20.8 12.8 %collective-permute-start.5 = (f16[784,256]{1,0:T(8,128)(2,1)S(1)}, f16[784,256]{1,0:T(8,128)(2,1)S(1)}, u32[]{:S(2)}, u32[]{:S(2)}) collective-permute-start(f16[784,256]{1,0:T(8,128)(2,1)S(1)} %get-tuple-element.28), channel_id=1, source_target_pairs={{0,3},{1,0},{2,1},{3,2},{4,7},{5,4},{6,5},{7,6},{8,11},{9,8},{10,9... | collective-permute-start | bytes 1204232 | tf_op jit(solution)/shard_map/ppermute | solution.py:326
  35.2 1.7 %copy-start.2 = (f32[768,256]{1,0:T(8,128)}, f32[768,256]{1,0:T(8,128)S(1)}, u32[]{:S(2)}) copy-start(f32[768,256]{1,0:T(8,128)S(1)} %get-tuple-element.34.bottom) | copy-start | bytes 2359300
  35.2 1.7 %copy-start.4 = (f32[768,256]{1,0:T(8,128)}, f32[768,256]{1,0:T(8,128)S(1)}, u32[]{:S(2)}) copy-start(f32[768,256]{1,0:T(8,128)S(1)} %get-tuple-element.35.top) | copy-start | bytes 2359300
  36.9 3.5 %collective-permute-start.6 = (f32[128,256]{1,0:T(8,128)S(1)}, f32[128,256]{1,0:T(8,128)S(1)}, u32[]{:S(2)}, u32[]{:S(2)}) collective-permute-start(f32[128,256]{1,0:T(8,128)S(1)} %dynamic-slice_bitcast_fusion.1), channel_id=1, source_target_pairs={{0,4},{4,0},{1,5},{5,1},{2,6},{6,2},{3,7},{7,3},{8,12},{12,8},{9,1... | collective-permute-start | bytes 393224 | tf_op jit(solution)/shard_map/ppermute | solution.py:326
  41.1 36.5 %collective-permute-start.7 = (bf16[1536,256]{1,0:T(8,128)(2,1)S(1)}, bf16[1536,256]{1,0:T(8,128)(2,1)S(1)}, u32[]{:S(2)}, u32[]{:S(2)}) collective-permute-start(bf16[1536,256]{1,0:T(8,128)(2,1)S(1)} %get-tuple-element.23.refs_0_), channel_id=1, source_target_pairs={{0,1},{1,2},{2,3},{3,0},{4,5},{5,6},{6,7},{7,4},{8,9},{9,10},{10,1... | collective-permute-start | bytes 2359304 | tf_op jit(solution)/shard_map/ppermute | solution.py:326
  42.3 35.3 %collective-permute-start.8 = (bf16[1536,256]{1,0:T(8,128)(2,1)S(1)}, bf16[1536,256]{1,0:T(8,128)(2,1)S(1)}, u32[]{:S(2)}, u32[]{:S(2)}) collective-permute-start(bf16[1536,256]{1,0:T(8,128)(2,1)S(1)} %get-tuple-element.23.refs_0_), channel_id=1, source_target_pairs={{0,3},{1,0},{2,1},{3,2},{4,7},{5,4},{6,5},{7,6},{8,11},{9,8},{10,9... | collective-permute-start | bytes 2359304 | tf_op jit(solution)/shard_map/ppermute | solution.py:326
  43.7 16.1 %all-to-all-start = ((f32[8,16,256]{2,1,0:T(8,128)}), f32[8,16,256]{2,1,0:T(8,128)S(1)}, u32[]{:S(2)}, u32[]{:S(2)}) async-start(f32[8,16,256]{2,1,0:T(8,128)} %bitcast.30), calls=%async_computation | async-start | bytes 262144 | tf_op jit(solution)/shard_map/all_to_all | solution.py:330
  73.5 11.2 %all-to-all-start.2 = ((f32[8,16,256]{2,1,0:T(8,128)}), f32[8,16,256]{2,1,0:T(8,128)S(1)}, u32[]{:S(2)}, u32[]{:S(2)}) async-start(f32[8,16,256]{2,1,0:T(8,128)} %sum_copies.3), calls=%async_computation.2 | async-start | bytes 262144 | tf_op jit(solution)/shard_map/all_to_all | solution.py:330
  76.9 23.4 %collective-permute-start.10 = (bf16[1536,256]{1,0:T(8,128)(2,1)S(1)}, bf16[1536,256]{1,0:T(8,128)(2,1)}, u32[]{:S(2)}, u32[]{:S(2)}) collective-permute-start(bf16[1536,256]{1,0:T(8,128)(2,1)S(1)} %get-tuple-element.23.refs_0_), channel_id=1, source_target_pairs={{0,2},{1,3},{2,0},{3,1},{4,6},{5,7},{6,4},{7,5},{8,10},{9,11},{10,... | collective-permute-start | bytes 2359304 | tf_op jit(solution)/shard_map/ppermute | solution.py:326
  84.7 5.8 %collective-permute-start.9 = (f32[128,256]{1,0:T(8,128)S(1)}, f32[128,256]{1,0:T(8,128)S(1)}, u32[]{:S(2)}, u32[]{:S(2)}) collective-permute-start(f32[128,256]{1,0:T(8,128)S(1)} %bitcast.92), channel_id=1, source_target_pairs={{0,4},{4,0},{1,5},{5,1},{2,6},{6,2},{3,7},{7,3},{8,12},{12,8},{9,1... | collective-permute-start | bytes 393224 | tf_op jit(solution)/shard_map/ppermute | solution.py:326
  103.1 7.4 %copy-start.3 = (f32[768,256]{1,0:T(8,128)S(1)}, f32[768,256]{1,0:T(8,128)}, u32[]{:S(2)}) copy-start(f32[768,256]{1,0:T(8,128)} %copy-done.2) | copy-start | bytes 2359300
  103.1 7.4 %copy-start.5 = (f32[768,256]{1,0:T(8,128)S(1)}, f32[768,256]{1,0:T(8,128)}, u32[]{:S(2)}) copy-start(f32[768,256]{1,0:T(8,128)} %copy-done.4) | copy-start | bytes 2359300
  103.2 1.6 %collective-permute-start.11 = (f32[32,16,128]{2,1,0:T(8,128)S(1)}, f32[32,16,128]{2,1,0:T(8,128)S(1)}, u32[]{:S(2)}, u32[]{:S(2)}) collective-permute-start(f32[32,16,128]{2,1,0:T(8,128)S(1)} %dynamic-slice_bitcast_fusion), channel_id=1, source_target_pairs={{0,4},{4,0},{1,5},{5,1},{2,6},{6,2},{3,7},{7,3},{8,12},{12,8},{9,1... | collective-permute-start | bytes 786440 | tf_op jit(solution)/shard_map/ppermute | solution.py:326
  105.5 16.5 %all-to-all-start.3 = ((f32[32,16,128]{2,1,0:T(8,128)}), f32[32,16,128]{2,1,0:T(8,128)S(1)}, u32[]{:S(2)}, u32[]{:S(2)}) async-start(f32[32,16,128]{2,1,0:T(8,128)} %bitcast_add_fusion), calls=%async_computation.3 | async-start | bytes 524288 | tf_op jit(solution)/shard_map/all_to_all | solution.py:330

commit v3 on v2

--- a/solution.py
+++ b/solution.py
@@ -8,8 +8,6 @@
 from jax.sharding import Mesh, PartitionSpec as P
 
 HIGHEST = lax.Precision.HIGHEST
-CHOL_BLOCK = 64
-PIVOTS = 8
 PAD = 16
 MIB = 1024 * 1024
 FIRST = (((0,), (0,)), ((), ()))
@@ -73,27 +71,34 @@
     return jnp.where(row < half, value, power).astype(jnp.float16)
 
 
-def gram_kernel(top, bottom, out, low):
-    half = top.shape[0]
-    out[...] = lax.dot_general(top[...], top[...], FIRST, precision=HIGHEST) + lax.dot_general(
+def gram_kernel(core, top, bottom, keep, send, low, buf):
+    half, rows, rank = top.shape[0], keep.shape[0], top.shape[1]
+    gram = lax.dot_general(top[...], top[...], FIRST, precision=HIGHEST) + lax.dot_general(
         bottom[...], bottom[...], FIRST, precision=HIGHEST
     )
+    buf[:, :rank] = gram[: rank // 2]
+    buf[:, rank:] = gram[rank // 2 :, rank // 2 :]
+    keep[...] = buf[pl.ds(pl.multiple_of(core[0] * rows, rows), rows), :]
+    send[...] = buf[pl.ds(pl.multiple_of((1 - core[0]) * rows, rows), rows), :]
     low[:half, :] = top[...].astype(low.dtype)
     low[half:, :] = bottom[...].astype(low.dtype)
 
 
-def gram_of(top, bottom):
+def gram_of(core, top, bottom):
     rows, rank = top.shape
+    vmem = pl.BlockSpec(memory_space=pltpu.VMEM)
+    packed = (rank // 2, rank + rank // 2)
     return pl.pallas_call(
         gram_kernel,
-        out_shape=[
-            jax.ShapeDtypeStruct((rank, rank), jnp.float32),
-            jax.ShapeDtypeStruct((2 * rows, rank), jnp.bfloat16),
-        ],
+        in_specs=[pl.BlockSpec(memory_space=pltpu.SMEM), vmem, vmem],
+        out_specs=[vmem] * 3,
+        out_shape=[jax.ShapeDtypeStruct((packed[0] // 2, packed[1]), jnp.float32)] * 2
+        + [jax.ShapeDtypeStruct((2 * rows, rank), jnp.bfloat16)],
+        scratch_shapes=[pltpu.VMEM(packed, jnp.float32)],
         compiler_params=params(),
         cost_estimate=cost(24 * rows * rank * rank, 12 * rows * rank),
         name="gram_of",
-    )(top, bottom)
+    )(core, top, bottom)
 
 
 def spread_kernel(got, out):
@@ -153,127 +158,126 @@
     )(order, snapshots, *start, *lows)
 
 
-def eliminate(groups, size, step):
-    sub = lax.broadcasted_iota(jnp.int32, (8, 128), 0)
-    count = size // 8
-    for k in range(0, size, step):
-        g, s = divmod(k, 8)
+def eliminate(groups, buf):
+    shape = groups[0].shape
+    sub = lax.broadcasted_iota(jnp.int32, shape, 0)
+    lane = lax.broadcasted_iota(jnp.int32, shape, 1)
+    spread = lambda v: jnp.broadcast_to(v, shape)
+    diags = []
+    for g in range(len(groups)):
+        k = 8 * g
         cols = {
-            i: [jnp.broadcast_to(groups[i][:, k + j : k + j + 1], (8, 128)) for j in range(step)]
-            for i in range(g, count)
+            i: [spread(groups[i][:, k + j : k + j + 1]) for j in range(8)]
+            for i in range(g, len(groups))
         }
-        pivot = [
-            [
-                jnp.broadcast_to(cols[g][j][s + i : s + i + 1, :], (8, 128)) if j <= i else None
-                for j in range(step)
-            ]
-            for i in range(step)
-        ]
-        inv, low = [], [[None] * step for _ in range(step)]
-        for j in range(step):
+        base = g % 2 * 64
+        for j in range(8):
+            buf[base + 8 * j : base + 8 * j + 8, :] = cols[g][j]
+        at = lambda i, j: base + 8 * j + i
+        pivot = [[spread(buf[at(i, j) : at(i, j) + 1, :]) for j in range(i + 1)] for i in range(8)]
+        inside = (lane >= k) & (lane < k + 8)
+        here = jnp.where(inside, jnp.where(lane - k == sub, 1.0, 0.0), groups[g])
+        inv, low = [], [[None] * 8 for _ in range(8)]
+        for j in range(8):
             if j % 2 == 0:
                 a, b, d = pivot[j][j], pivot[j + 1][j], pivot[j + 1][j + 1]
                 guess = a * (1.0 / (a * d - b * b))
                 inv.append(1.0 / a)
             else:
                 inv.append(guess * (2.0 - pivot[j][j] * guess))
-            for i in range(j + 1, step):
+            for i in range(j + 1, 8):
                 low[i][j] = pivot[i][j] * inv[j]
-            for i in range(j + 1, step):
+            for i in range(j + 1, 8):
                 for m in range(j + 1, i + 1):
                     pivot[i][m] = pivot[i][m] - low[i][j] * pivot[m][j]
         rows = []
-        for i in range(step):
-            row = jnp.broadcast_to(groups[g][s + i : s + i + 1, :], (8, 128))
+        for i in range(8):
+            row = spread(here[i : i + 1, :])
             for j in range(i):
                 row = row - low[i][j] * rows[j]
             rows.append(row)
-        for i in range(g, count):
-            new = groups[i]
-            if i > g or s + step < 8:
-                mult = []
-                for j in range(step):
-                    c = cols[i][j]
-                    for q in range(j):
-                        c = c - mult[q] * pivot[j][q]
-                    mult.append(c * inv[j])
-                for j in range(step):
-                    new = new - mult[j] * rows[j]
-            if i == g:
-                for j in range(step):
-                    new = jnp.where(sub == s + j, rows[j], new)
-                if s:
-                    new = jnp.where(sub < s, groups[g], new)
+        new, diag = rows[0], pivot[0][0]
+        for j in range(1, 8):
+            new = jnp.where(sub == j, rows[j], new)
+            diag = jnp.where(sub == j, pivot[j][j], diag)
+        groups[g] = new
+        diags.append(diag)
+        for i in range(g + 1, len(groups)):
+            mult = []
+            for j in range(8):
+                c = cols[i][j]
+                for q in range(j):
+                    c = c - mult[q] * pivot[j][q]
+                mult.append(c * inv[j])
+            new = jnp.where(inside, 0.0, groups[i])
+            for j in range(8):
+                new = new - mult[j] * rows[j]
             groups[i] = new
-    return groups
-
-
-def block_inverse(block, step):
-    size = block.shape[0]
-    at = lambda d: lax.broadcasted_iota(jnp.int32, (size, size), d)
-    eye = at(0) == at(1)
-    both = jnp.concatenate([block, eye.astype(jnp.float32)], axis=1)
-    groups = [both[8 * i : 8 * i + 8] for i in range(size // 8)]
-    both = jnp.concatenate(eliminate(groups, size, step), axis=0)
-    diag = jnp.sum(jnp.where(eye, both[:, :size], 0.0), axis=1, keepdims=True)
-    return both[:, size:] * lax.rsqrt(diag)
-
-
-def inverse_kernel(core, held, other, inverse, work, rest):
-    n = work.shape[0]
-    half = n // 2
-    work[pl.ds(pl.multiple_of(core[0] * half, half), half), :] = held[...]
-    work[pl.ds(pl.multiple_of((1 - core[0]) * half, half), half), :] = other[...]
-    inverse[...] = jnp.zeros_like(inverse)
-    rest[...] = jnp.zeros_like(rest)
-    for k in range(0, n, CHOL_BLOCK):
-        e = k + CHOL_BLOCK
-        w = block_inverse(work[k:e, k:e], PIVOTS)
-        inverse[k:e, k:e] = w
-        if k:
-            inverse[k:e, :k] = jnp.dot(w, rest[k:e, :k], precision=HIGHEST)
-        if e < n:
-            solved = jnp.dot(w, work[k:e, e:], precision=HIGHEST)
-            work[e:, e:] -= lax.dot_general(solved, solved, FIRST, precision=HIGHEST)
-            rest[e:, :e] -= lax.dot_general(solved, inverse[k:e, :e], FIRST, precision=HIGHEST)
+    return [
+        jnp.where(lane <= sub + 8 * g, v, 0.0) * lax.rsqrt(d)
+        for g, (v, d) in enumerate(zip(groups, diags))
+    ]
+
+
+def block_inverse(block, buf):
+    groups = [block[8 * i : 8 * i + 8] for i in range(block.shape[0] // 8)]
+    return jnp.concatenate(eliminate(groups, buf), axis=0)
+
+
+def inverse_kernel(core, held, other, inverse, packed, buf):
+    rows, n = held.shape[0], inverse.shape[0] // 2
+    packed[pl.ds(pl.multiple_of(core[0] * rows, rows), rows), :] = held[...]
+    packed[pl.ds(pl.multiple_of((1 - core[0]) * rows, rows), rows), :] = other[...]
+    first = block_inverse(packed[:, :n], buf)
+    solved = jnp.dot(first, packed[:, n : 2 * n], precision=HIGHEST)
+    inverse[:n, :n] = first
+    inverse[:n, n:] = jnp.zeros((n, n), jnp.float32)
+    update = lax.dot_general(solved, solved, FIRST, precision=HIGHEST)
+    second = block_inverse(packed[:, 2 * n :] - update, buf)
+    inverse[n:, n:] = second
+    below = lax.dot_general(solved, first, FIRST, precision=HIGHEST)
+    inverse[n:, :n] = -jnp.dot(second, below, precision=HIGHEST)
 
 
 def lower_inverse(core, held, other):
-    half, rank = held.shape
+    rows, width = held.shape
+    n = width // 3
+    vmem = pl.BlockSpec(memory_space=pltpu.VMEM)
     return pl.pallas_call(
         inverse_kernel,
-        grid_spec=pltpu.PrefetchScalarGridSpec(
-            num_scalar_prefetch=1,
-            grid=(1,),
-            in_specs=[pl.BlockSpec((half, rank), lambda i, core: (0, 0))] * 2,
-            out_specs=pl.BlockSpec((rank, rank), lambda i, core: (0, 0)),
-            scratch_shapes=[pltpu.VMEM((rank, rank), jnp.float32)] * 2,
-        ),
-        out_shape=jax.ShapeDtypeStruct((rank, rank), jnp.float32),
+        in_specs=[pl.BlockSpec(memory_space=pltpu.SMEM), vmem, vmem],
+        out_specs=vmem,
+        out_shape=jax.ShapeDtypeStruct((2 * n, 2 * n), jnp.float32),
+        scratch_shapes=[
+            pltpu.VMEM((2 * rows, width), jnp.float32),
+            pltpu.VMEM((128, n), jnp.float32),
+        ],
         compiler_params=params(),
-        cost_estimate=cost(5 * 10**9, 4 * rank * rank),
+        cost_estimate=cost(5 * 10**9, 4 * rows * width),
         name="lower_inverse",
     )(core, held, other)
 
 
-def coeff_kernel(which, inverse, near, low, snap, out, *, factor):
+def coeff_kernel(core, inverse, near, low, snap, keep, send, *, factor):
     cross = near[...] + lax.dot_general(
         low[...], snap[...], FIRST, preferred_element_type=jnp.float32
     )
     value = jnp.dot(inverse[...], cross, precision=HIGHEST) * factor
-    cores, chips, sub, _ = out.shape
+    chips, sub, _ = keep.shape
     blocks = value.shape[1] // 128
     each = sub // blocks
+    first = core[0] == 0
     for q in range(blocks):
-        part = value[:, 128 * q : 128 * (q + 1)].reshape(chips, cores * each, 128)
-        for c in range(cores):
-            out[c, :, each * q : each * (q + 1), :] = part[:, each * c : each * (c + 1), :]
-
-
-def coeff_parts(inverse, near, low, snapshots, block, factor, cores, chips):
+        part = value[:, 128 * q : 128 * (q + 1)].reshape(chips, 2 * each, 128)
+        one, two = part[:, :each, :], part[:, each:, :]
+        keep[:, each * q : each * (q + 1), :] = jnp.where(first, one, two)
+        send[:, each * q : each * (q + 1), :] = jnp.where(first, two, one)
+
+
+def coeff_parts(core_block, inverse, near, low, snapshots, factor, chips):
     rank, cols = near.shape
     rows = low.shape[0]
-    sub = rank // (cores * chips) * (cols // 128)
+    sub = rank // (2 * chips) * (cols // 128)
     whole = lambda *shape: pl.BlockSpec(shape, lambda i, which: (0,) * len(shape))
     return pl.pallas_call(
         functools.partial(coeff_kernel, factor=factor),
@@ -284,15 +288,15 @@
                 whole(rank, rank),
                 whole(rank, cols),
                 whole(rows, rank),
-                pl.BlockSpec((rows, cols), lambda i, which: (which[0], 0)),
+                pl.BlockSpec((rows, cols), lambda i, which: (which[1], 0)),
             ],
-            out_specs=whole(cores, chips, sub, 128),
+            out_specs=[whole(chips, sub, 128)] * 2,
         ),
-        out_shape=jax.ShapeDtypeStruct((cores, chips, sub, 128), jnp.float32),
+        out_shape=[jax.ShapeDtypeStruct((chips, sub, 128), jnp.float32)] * 2,
         compiler_params=params(48),
         cost_estimate=cost(2 * rows * cols * rank + 12 * rank * rank * cols, 2 * rows * cols),
         name="coeff_parts",
-    )(block, inverse, near, low, snapshots)
+    )(core_block, inverse, near, low, snapshots)
 
 
 def basis_kernel(top, bottom, inverse, out, *, factor, steps):
@@ -357,27 +361,28 @@
 
     tie = lax.optimization_barrier
     block = lambda *ds: at(*[lax.rem(x + d, nx) for d in ds])
-    gram, low = gram_of(top, bottom)
-    halves = gram.reshape(cores, rank // cores, rank)
-    pick = lambda v, i: lax.dynamic_index_in_dim(v, i, 0, keepdims=False)
-    held = pick(halves, c) + shift(pick(halves, 1 - c), "c", 1)
-    held, low = tie((held, low))
+    core = c.astype(jnp.int32).reshape(1)
+    keep, send, low = gram_of(core, top, bottom)
+    held = keep + shift(send, "c", 1)
     left, right = shift(low, "x", 1), shift(low, "x", -1)
     cross = cross_part(snapshots, block(0), [low])
-    held, cross = tie((exchange(held.reshape(nz, -1, rank), "z"), cross))
-
-    held = exchange(sum_copies(held, lax.axis_size("y") * nx), ("y", "x"))
-
-    held, low, cross = tie((sum_copies(held, nz), low, cross))
+    held, cross = tie((exchange(held.reshape(nz, -1, held.shape[1]), "z"), cross))
+
+    held, cross = tie((sum_copies(held, lax.axis_size("y") * nx), cross))
+    cross = cross_part(snapshots, block(3, 1), [left, right], cross)
+    held, cross = tie((exchange(held, ("y", "x")), cross))
+
+    low, cross = tie((low, cross))
     across = shift(low, "x", 2)
-    cross = cross_part(snapshots, block(3, 1), [left, right], cross)
-    held, cross = tie((exchange(held, "z").reshape(-1, rank), cross))
+    held = exchange(sum_copies(held, nz), "z")
+    held = held.reshape(-1, held.shape[2])
     other = shift(held, "c", 1)
-    inverse = lower_inverse(c.astype(jnp.int32).reshape(1), held, other)
+    inverse = lower_inverse(core, held, other)
 
     factor = (total_cols / total_rows) ** 0.5
-    parts = coeff_parts(inverse, cross, across, snapshots, block(2), factor, cores, chips)
-    both = pick(parts, c) + shift(pick(parts, 1 - c), "c", 1)
+    where = at(c, lax.rem(x + 2, nx))
+    keep, send = coeff_parts(where, inverse, cross, across, snapshots, factor, chips)
+    both = keep + shift(send, "c", 1)
     coeff = jnp.sum(exchange(both, ("z", "y")), axis=0)
     coeff = coeff.reshape(cols // 128, -1, 128).transpose(1, 0, 2).reshape(-1, cols)
 

time: 123 us -> 120 us (0.976)
  blocking collectives: 12.9 us -> 9.95 us
  starting transfers between devices: 36.3 us -> 38.1 us
  Pallas kernels: 31.6 us -> 29.8 us
    pallas_call x2, Pallas kernels: 11.4 us -> 8.35 us  [the longest x1 6.65 us: lower_inverse(): pl.pallas_call(inverse_kernel, in_specs=[pl.BlockSpec(memory_space=pltpu....]
    all_to_all x1, blocking collectives: 12.9 us -> 9.95 us  [exchange(): return lax.all_to_all(value, axes, 0, 0, tiled=True)]
  transfers between devices with their start and end apart: 15 -> 15, of which waited for: 10 -> 10; matrix products, arithmetic and copies ran while one was open for 4% -> 5% of each run, Pallas kernels for 20% -> 19%
where the time goes in v3:
time: 120 us; the launch traced here: 119 us
  starting transfers between devices  38.1 us (32%)
  waiting for transfers between devices  29.9 us (25%)
  Pallas kernels  29.8 us (25%)
  blocking collectives  9.95 us (8%)
  other arithmetic  7.71 us (6%)
  local copies, waits for them, and re-layouts  3.11 us (3%)
    ppermute x12, starting transfers between devices, shift(): return lax.ppermute(value, axis, [(i, (i + by) % n) for i in range(n)])  20.6 us
    all_to_all x3, waiting for transfers between devices, exchange(): return lax.all_to_all(value, axes, 0, 0, tiled=True)  18.1 us
    all_to_all x3, starting transfers between devices, exchange(): return lax.all_to_all(value, axes, 0, 0, tiled=True)  17.6 us
    ppermute x12, waiting for transfers between devices, shift(): return lax.ppermute(value, axis, [(i, (i + by) % n) for i in range(n)])  11.8 us
    all_to_all x1, blocking collectives, exchange(): return lax.all_to_all(value, axes, 0, 0, tiled=True)  9.95 us
    pallas_call x3, Pallas kernels, sketch_rows(): pl.pallas_call(functools.partial(sketch_kernel, scaled=scaled, pad=pad),...  8.32 us
    pallas_call x1, Pallas kernels, lower_inverse(): pl.pallas_call(inverse_kernel, in_specs=[pl.BlockSpec(memory_space=pltpu....  6.65 us
    pallas_call x2, Pallas kernels, cross_part(): pl.pallas_call(functools.partial(cross_kernel, has_before=before is not N...  5.2 us
  transfers between devices with their start and end apart: 15, of which 10 were waited for; matrix products, arithmetic and copies ran while one was open for 5% of the time, Pallas kernels for 19%

profile of v3, /device:TPU:1, one launch (start us, length us, event | category | flops | bytes accessed | tf_op | source)
XLA Modules:
  0.0 119.5 jit_solution(8451129460198678354)
XLA Ops:
  0.6 0.9 copy-done
  1.6 2.1 %far_chunk.1 = f32[2,784,256]{2,1,0:T(8,128)S(1)} custom-call(s32[1]{0:T(128)} %bitcast.8.which, bf16[6144,512]{1,0:T(8,128)(2,1)} %snap.11, bf16[512,256]{1,0:T(8,128)(2,1)S(1)} %copy-done), custom_call_target="tpu_custom_call" | custom-call | flops 402653184 | bytes 3145728 | tf_op jit(solution)/shard_map/far_chunk/pallas_call | solution.py:42
  3.8 1.1 slice_bitcast_fusion.4
  4.9 2.0 %collective-permute-start.1 = (f16[784,256]{1,0:T(8,128)(2,1)}, f16[784,256]{1,0:T(8,128)(2,1)}, u32[]{:S(2)}, u32[]{:S(2)}) collective-permute-start(f16[784,256]{1,0:T(8,128)(2,1)} %get-tuple-element.41), channel_id=1, source_target_pairs={{0,1},{1,2},{2,3},{3,0},{4,5},{5,6},{6,7},{7,4},{8,9},{9,10},{10,1... | collective-permute-start | bytes 1204232 | tf_op jit(solution)/shard_map/ppermute | solution.py:330
  7.0 1.3 %collective-permute-start.4 = (f16[784,256]{1,0:T(8,128)(2,1)}, f16[784,256]{1,0:T(8,128)(2,1)}, u32[]{:S(2)}, u32[]{:S(2)}) collective-permute-start(f16[784,256]{1,0:T(8,128)(2,1)} %get-tuple-element.40), channel_id=1, source_target_pairs={{0,3},{1,0},{2,1},{3,2},{4,7},{5,4},{6,5},{7,6},{8,11},{9,8},{10,9... | collective-permute-start | bytes 1204232 | tf_op jit(solution)/shard_map/ppermute | solution.py:330
  8.3 4.3 %near_chunks.1 = f32[4,784,256]{2,1,0:T(8,128)S(1)} custom-call(s32[4]{0:T(128)S(1)} %pad_add_fusion.which, bf16[6144,512]{1,0:T(8,128)(2,1)} %snap.11, bf16[512,256]{1,0:T(8,128)(2,1)S(1)} %copy-done.1), custom_call_target="tpu_custom_call" | custom-call | flops 805306368 | bytes 6291456 | tf_op jit(solution)/shard_map/near_chunks/pallas_call | solution.py:42
  12.8 1.1 slice_bitcast_fusion.5
  14.1 2.5 %collective-permute-start = (f16[784,256]{1,0:T(8,128)(2,1)}, f16[784,256]{1,0:T(8,128)(2,1)}, u32[]{:S(2)}, u32[]{:S(2)}) collective-permute-start(f16[784,256]{1,0:T(8,128)(2,1)} %get-tuple-element.37), channel_id=1, source_target_pairs={{0,3},{1,0},{2,1},{3,2},{4,7},{5,4},{6,5},{7,6},{8,11},{9,8},{10,9... | collective-permute-start | bytes 1204232 | tf_op jit(solution)/shard_map/ppermute | solution.py:330
  16.6 2.0 %own_chunk.1 = f32[2,768,256]{2,1,0:T(8,128)S(1)} custom-call(s32[1]{0:T(128)} %bitcast.which, bf16[6144,512]{1,0:T(8,128)(2,1)} %snap.11, bf16[512,256]{1,0:T(8,128)(2,1)S(1)} %copy-done.1), custom_call_target="tpu_custom_call" | custom-call | flops 402653184 | bytes 3145728 | tf_op jit(solution)/shard_map/own_chunk/pallas_call | solution.py:42
  19.3 1.5 %fusion.3 = (f16[784,256]{1,0:T(8,128)(2,1)S(1)}, f16[784,256]{1,0:T(8,128)(2,1)S(1)}) fusion(f32[4,784,256]{2,1,0:T(8,128)S(1)} %near_chunks.1, f16[784,256]{1,0:T(8,128)(2,1)} %collective-permute-done.4, f32[256]{0:T(256)S(1)} %bitcast.86, f32[256]{0:T(256)S(1)} %bitcast.85, f32[256]{0:T(256)S(1)} %bitcast.90, pred[784]{0:T(1024)(128)(4,1)S(1)} %iota_compare_fusion, ...), kind=kLoop, calls=%fused_computation.4 | loop fusion | flops 2408448 | bytes 3218192 | tf_op jit(solution)/shard_map/convert_element_type | solution.py:71
  20.9 2.7 %collective-permute-start.5 = (f16[784,256]{1,0:T(8,128)(2,1)S(1)}, f16[784,256]{1,0:T(8,128)(2,1)S(1)}, u32[]{:S(2)}, u32[]{:S(2)}) collective-permute-start(f16[784,256]{1,0:T(8,128)(2,1)S(1)} %get-tuple-element.32), channel_id=1, source_target_pairs={{0,3},{1,0},{2,1},{3,2},{4,7},{5,4},{6,5},{7,6},{8,11},{9,8},{10,9... | collective-permute-start | bytes 1204232 | tf_op jit(solution)/shard_map/ppermute | solution.py:330
  25.9 7.5 %collective-permute-done.2 = f16[784,256]{1,0:T(8,128)(2,1)S(1)} collective-permute-done((f16[784,256]{1,0:T(8,128)(2,1)S(1)}, f16[784,256]{1,0:T(8,128)(2,1)S(1)}, u32[]{:S(2)}, u32[]{:S(2)}) %collective-permute-start.2) | collective-permute-done | bytes 401440 | tf_op jit(solution)/shard_map/ppermute | solution.py:330
  33.7 1.5 %fusion.9 = (f32[768,256]{1,0:T(8,128)S(1)}, f32[768,256]{1,0:T(8,128)S(1)}) fusion(f32[2,768,256]{2,1,0:T(8,128)S(1)} %own_chunk.1, f16[784,256]{1,0:T(8,128)(2,1)S(1)} %collective-permute-done.5, f16[784,256]{1,0:T(8,128)(2,1)} %collective-permute-done.3, f32[256]{0:T(256)S(1)} %bitcast.94, f32[256]{0:T(256)S(1)} %bitcast.91, f32[256]{0:T(256)S(1)} %bitcast.93, ...), kind=kLoop, calls=%fused_computation.12 | loop fusion | flops 2359296 | bytes 4722688 | tf_op jit(solution)/shard_map/add | solution.py:360
  35.2 1.7 %gram_of.1 = (f32[64,384]{1,0:T(8,128)S(1)}, f32[64,384]{1,0:T(8,128)S(1)}, bf16[1536,256]{1,0:T(8,128)(2,1)S(1)}) custom-call(s32[1]{0:T(128)} %bitcast.26.core, f32[768,256]{1,0:T(8,128)S(1)} %get-tuple-element.39.top, f32[768,256]{1,0:T(8,128)S(1)} %get-tuple-element.38.bottom), custom_call_target="tpu_custom_call" | custom-call | flops 1207959552 | bytes 2359296 | tf_op jit(solution)/shard_map/gram_of/pallas_call | solution.py:91
  36.9 1.8 %collective-permute-start.7 = (bf16[1536,256]{1,0:T(8,128)(2,1)S(1)}, bf16[1536,256]{1,0:T(8,128)(2,1)S(1)}, u32[]{:S(2)}, u32[]{:S(2)}) collective-permute-start(bf16[1536,256]{1,0:T(8,128)(2,1)S(1)} %get-tuple-element.25.refs_0_), channel_id=1, source_target_pairs={{0,1},{1,2},{2,3},{3,0},{4,5},{5,6},{6,7},{7,4},{8,9},{9,10},{10,1... | collective-permute-start | bytes 2359304 | tf_op jit(solution)/shard_map/ppermute | solution.py:330
  39.7 3.0 %collective-permute-start.6 = (f32[64,384]{1,0:T(8,128)S(1)}, f32[64,384]{1,0:T(8,128)S(1)}, u32[]{:S(2)}, u32[]{:S(2)}) collective-permute-start(f32[64,384]{1,0:T(8,128)S(1)} %get-tuple-element.16), channel_id=1, source_target_pairs={{0,4},{4,0},{1,5},{5,1},{2,6},{6,2},{3,7},{7,3},{8,12},{12,8},{9,1... | collective-permute-start | bytes 294920 | tf_op jit(solution)/shard_map/ppermute | solution.py:330
  42.6 0.9 collective-permute-done.6
  44.2 8.2 %all-to-all-start = ((f32[8,8,384]{2,1,0:T(8,128)}), f32[8,8,384]{2,1,0:T(8,128)S(1)}, u32[]{:S(2)}, u32[]{:S(2)}) async-start(f32[8,8,384]{2,1,0:T(8,128)} %add_bitcast_fusion), calls=%async_computation | async-start | bytes 196608 | tf_op jit(solution)/shard_map/all_to_all | solution.py:334
  52.4 2.0 %cross_part.2.refs_0_ = f32[256,512]{1,0:T(8,128)S(1)} custom-call(s32[1]{0:T(128)} %bitcast.28.which, bf16[6144,512]{1,0:T(8,128)(2,1)} %snap.11, bf16[1536,256]{1,0:T(8,128)(2,1)S(1)} %get-tuple-element.25.refs_0_), custom_call_target="tpu_custom_call" | custom-call | flops 402653184 | bytes 2359296 | tf_op jit(solution)/shard_map/cross_part/pallas_call | solution.py:144
  54.4 5.5 %all-to-all-done.got = f32[8,8,384]{2,1,0:T(8,128)S(1)} async-done(((f32[8,8,384]{2,1,0:T(8,128)}), f32[8,8,384]{2,1,0:T(8,128)S(1)}, u32[]{:S(2)}, u32[]{:S(2)}) %all-to-all-start) | async-done | bytes 98336 | tf_op jit(solution)/shard_map/all_to_all | solution.py:334
  60.6 5.5 %all-to-all-start.1 = ((f32[16,8,384]{2,1,0:T(8,128)}), f32[16,8,384]{2,1,0:T(8,128)}, u32[]{:S(2)}, u32[]{:S(2)}) async-start(f32[16,8,384]{2,1,0:T(8,128)} %sum_copies.2), calls=%async_computation.1 | async-start | bytes 393216 | tf_op jit(solution)/shard_map/all_to_all | solution.py:334
  66.2 3.2 %cross_part.3.near = f32[256,512]{1,0:T(8,128)S(1)} custom-call(s32[2]{0:T(128)S(1)} %pad_add_fusion.1.which, bf16[6144,512]{1,0:T(8,128)(2,1)} %snap.11, f32[256,512]{1,0:T(8,128)S(1)} %cross_part.2.refs_0_, bf16[1536,256]{1,0:T(8,128)(2,1)S(1)} %collective-permute-done.7.refs_1_, bf16[1536,256]{1,0:T(8,128)(2,1)S(1)} %collective-permute-done.8.refs_2_), custom_call_target="tpu_custom_call" | custom-call | flops 805306368 | bytes 4718592 | tf_op jit(solution)/shard_map/cross_part/pallas_call | solution.py:144
  69.4 4.0 %all-to-all-done.1.got = f32[16,8,384]{2,1,0:T(8,128)} async-done(((f32[16,8,384]{2,1,0:T(8,128)}), f32[16,8,384]{2,1,0:T(8,128)}, u32[]{:S(2)}, u32[]{:S(2)}) %all-to-all-start.1) | async-done | bytes 196640 | tf_op jit(solution)/shard_map/all_to_all | solution.py:334
  74.2 0.9 sum_copies.3
  75.1 10.0 %all_to_all.20 = f32[8,8,384]{2,1,0:T(8,128)S(1)} all-to-all(f32[8,8,384]{2,1,0:T(8,128)S(1)} %sum_copies.3), channel_id=1, replica_groups=mesh['z'=8,'y'=4,'c'=2,'x'=4] {'z'}, dimensions={0} | all-to-all | bytes 196608 | tf_op jit(solution)/shard_map/all_to_all | solution.py:334
  85.1 4.9 %collective-permute-start.9 = (f32[64,384]{1,0:T(8,128)S(1)}, f32[64,384]{1,0:T(8,128)S(1)}, u32[]{:S(2)}, u32[]{:S(2)}) collective-permute-start(f32[64,384]{1,0:T(8,128)S(1)} %bitcast.82), channel_id=1, source_target_pairs={{0,4},{4,0},{1,5},{5,1},{2,6},{6,2},{3,7},{7,3},{8,12},{12,8},{9,1... | collective-permute-start | bytes 294920 | tf_op jit(solution)/shard_map/ppermute | solution.py:330
  90.9 6.6 %lower_inverse.1.inverse = f32[256,256]{1,0:T(8,128)S(1)} custom-call(s32[1]{0:T(128)} %bitcast.26.core, f32[64,384]{1,0:T(8,128)S(1)} %bitcast.83, f32[64,384]{1,0:T(8,128)S(1)} %collective-permute-done.9.other), custom_call_target="tpu_custom_call" | custom-call | flops 5000000000 | bytes 98304 | tf_op jit(solution)/shard_map/lower_inverse/pallas_call | solution.py:246
  97.5 3.2 %coeff_parts.1 = (f32[32,16,128]{2,1,0:T(8,128)S(1)}, f32[32,16,128]{2,1,0:T(8,128)S(1)}) custom-call(s32[2]{0:T(128)S(1)} %pad_add_fusion.2.core, f32[256,256]{1,0:T(8,128)S(1)} %lower_inverse.1.inverse, f32[256,512]{1,0:T(8,128)S(1)} %cross_part.3.near, bf16[1536,256]{1,0:T(8,128)(2,1)S(1)} %collective-permute-done.10.low, bf16[6144,512]{1,0:T(8,128)(2,1)} %snap.11), custom_call_target="tpu_custom_call" | custom-call | flops 805306368 | bytes 1572864 | tf_op jit(solution)/shard_map/coeff_parts/pallas_call | solution.py:282
  101.2 1.2 collective-permute-done.11
  103.1 3.9 %all-to-all-start.3 = ((f32[32,16,128]{2,1,0:T(8,128)}), f32[32,16,128]{2,1,0:T(8,128)S(1)}, u32[]{:S(2)}, u32[]{:S(2)}) async-start(f32[32,16,128]{2,1,0:T(8,128)} %add.70), calls=%async_computation.3 | async-start | bytes 524288 | tf_op jit(solution)/shard_map/all_to_all | solution.py:334
  107.0 3.1 %basis_rows.1 = f32[1536,256]{1,0:T(8,128)} custom-call(f32[768,256]{1,0:T(8,128)S(1)} %copy-done.5, f32[768,256]{1,0:T(8,128)S(1)} %copy-done.3, f32[256,256]{1,0:T(8,128)S(1)} %lower_inverse.1.inverse), custom_call_target="tpu_custom_call" | custom-call | flops 1207959552 | bytes 3145728 | tf_op jit(solution)/shard_map/basis_rows/pallas_call | solution.py:312
  110.1 8.7 %all-to-all-done.3 = f32[32,16,128]{2,1,0:T(8,128)S(1)} async-done(((f32[32,16,128]{2,1,0:T(8,128)}), f32[32,16,128]{2,1,0:T(8,128)S(1)}, u32[]{:S(2)}, u32[]{:S(2)}) %all-to-all-start.3) | async-done | bytes 262176 | tf_op jit(solution)/shard_map/all_to_all | solution.py:334
  (40 shorter events, 10.1 us)
Async XLA Ops:
  0.6 1.0 copy-start
  3.7 4.6 %copy-start.1 = (bf16[512,256]{1,0:T(8,128)(2,1)S(1)}, bf16[512,256]{1,0:T(8,128)(2,1)}, u32[]{:S(2)}) copy-start(bf16[512,256]{1,0:T(8,128)(2,1)} %omega.5) | copy-start | bytes 786436
  4.9 13.6 %collective-permute-start.1 = (f16[784,256]{1,0:T(8,128)(2,1)}, f16[784,256]{1,0:T(8,128)(2,1)}, u32[]{:S(2)}, u32[]{:S(2)}) collective-permute-start(f16[784,256]{1,0:T(8,128)(2,1)} %get-tuple-element.41), channel_id=1, source_target_pairs={{0,1},{1,2},{2,3},{3,0},{4,5},{5,6},{6,7},{7,4},{8,9},{9,10},{10,1... | collective-permute-start | bytes 1204232 | tf_op jit(solution)/shard_map/ppermute | solution.py:330
  7.0 11.6 %collective-permute-start.4 = (f16[784,256]{1,0:T(8,128)(2,1)}, f16[784,256]{1,0:T(8,128)(2,1)}, u32[]{:S(2)}, u32[]{:S(2)}) collective-permute-start(f16[784,256]{1,0:T(8,128)(2,1)} %get-tuple-element.40), channel_id=1, source_target_pairs={{0,3},{1,0},{2,1},{3,2},{4,7},{5,4},{6,5},{7,6},{8,11},{9,8},{10,9... | collective-permute-start | bytes 1204232 | tf_op jit(solution)/shard_map/ppermute | solution.py:330
  13.9 9.7 %collective-permute-start.3 = (f16[784,256]{1,0:T(8,128)(2,1)}, f16[784,256]{1,0:T(8,128)(2,1)}, u32[]{:S(2)}, u32[]{:S(2)}) collective-permute-start(f16[784,256]{1,0:T(8,128)(2,1)} %get-tuple-element.36), channel_id=1, source_target_pairs={{0,1},{1,2},{2,3},{3,0},{4,5},{5,6},{6,7},{7,4},{8,9},{9,10},{10,1... | collective-permute-start | bytes 1204232 | tf_op jit(solution)/shard_map/ppermute | solution.py:330
  14.1 11.1 %collective-permute-start = (f16[784,256]{1,0:T(8,128)(2,1)}, f16[784,256]{1,0:T(8,128)(2,1)}, u32[]{:S(2)}, u32[]{:S(2)}) collective-permute-start(f16[784,256]{1,0:T(8,128)(2,1)} %get-tuple-element.37), channel_id=1, source_target_pairs={{0,3},{1,0},{2,1},{3,2},{4,7},{5,4},{6,5},{7,6},{8,11},{9,8},{10,9... | collective-permute-start | bytes 1204232 | tf_op jit(solution)/shard_map/ppermute | solution.py:330
  20.8 12.6 %collective-permute-start.2 = (f16[784,256]{1,0:T(8,128)(2,1)S(1)}, f16[784,256]{1,0:T(8,128)(2,1)S(1)}, u32[]{:S(2)}, u32[]{:S(2)}) collective-permute-start(f16[784,256]{1,0:T(8,128)(2,1)S(1)} %get-tuple-element.33), channel_id=1, source_target_pairs={{0,1},{1,2},{2,3},{3,0},{4,5},{5,6},{6,7},{7,4},{8,9},{9,10},{10,1... | collective-permute-start | bytes 1204232 | tf_op jit(solution)/shard_map/ppermute | solution.py:330
  20.9 12.8 %collective-permute-start.5 = (f16[784,256]{1,0:T(8,128)(2,1)S(1)}, f16[784,256]{1,0:T(8,128)(2,1)S(1)}, u32[]{:S(2)}, u32[]{:S(2)}) collective-permute-start(f16[784,256]{1,0:T(8,128)(2,1)S(1)} %get-tuple-element.32), channel_id=1, source_target_pairs={{0,3},{1,0},{2,1},{3,2},{4,7},{5,4},{6,5},{7,6},{8,11},{9,8},{10,9... | collective-permute-start | bytes 1204232 | tf_op jit(solution)/shard_map/ppermute | solution.py:330
  35.2 1.7 %copy-start.2 = (f32[768,256]{1,0:T(8,128)}, f32[768,256]{1,0:T(8,128)S(1)}, u32[]{:S(2)}) copy-start(f32[768,256]{1,0:T(8,128)S(1)} %get-tuple-element.38.bottom) | copy-start | bytes 2359300
  35.2 1.7 %copy-start.4 = (f32[768,256]{1,0:T(8,128)}, f32[768,256]{1,0:T(8,128)S(1)}, u32[]{:S(2)}) copy-start(f32[768,256]{1,0:T(8,128)S(1)} %get-tuple-element.39.top) | copy-start | bytes 2359300
  36.9 29.3 %collective-permute-start.7 = (bf16[1536,256]{1,0:T(8,128)(2,1)S(1)}, bf16[1536,256]{1,0:T(8,128)(2,1)S(1)}, u32[]{:S(2)}, u32[]{:S(2)}) collective-permute-start(bf16[1536,256]{1,0:T(8,128)(2,1)S(1)} %get-tuple-element.25.refs_0_), channel_id=1, source_target_pairs={{0,1},{1,2},{2,3},{3,0},{4,5},{5,6},{6,7},{7,4},{8,9},{9,10},{10,1... | collective-permute-start | bytes 2359304 | tf_op jit(solution)/shard_map/ppermute | solution.py:330
  38.8 27.4 %collective-permute-start.8 = (bf16[1536,256]{1,0:T(8,128)(2,1)S(1)}, bf16[1536,256]{1,0:T(8,128)(2,1)S(1)}, u32[]{:S(2)}, u32[]{:S(2)}) collective-permute-start(bf16[1536,256]{1,0:T(8,128)(2,1)S(1)} %get-tuple-element.25.refs_0_), channel_id=1, source_target_pairs={{0,3},{1,0},{2,1},{3,2},{4,7},{5,4},{6,5},{7,6},{8,11},{9,8},{10,9... | collective-permute-start | bytes 2359304 | tf_op jit(solution)/shard_map/ppermute | solution.py:330
  39.7 3.9 %collective-permute-start.6 = (f32[64,384]{1,0:T(8,128)S(1)}, f32[64,384]{1,0:T(8,128)S(1)}, u32[]{:S(2)}, u32[]{:S(2)}) collective-permute-start(f32[64,384]{1,0:T(8,128)S(1)} %get-tuple-element.16), channel_id=1, source_target_pairs={{0,4},{4,0},{1,5},{5,1},{2,6},{6,2},{3,7},{7,3},{8,12},{12,8},{9,1... | collective-permute-start | bytes 294920 | tf_op jit(solution)/shard_map/ppermute | solution.py:330
  44.2 15.7 %all-to-all-start = ((f32[8,8,384]{2,1,0:T(8,128)}), f32[8,8,384]{2,1,0:T(8,128)S(1)}, u32[]{:S(2)}, u32[]{:S(2)}) async-start(f32[8,8,384]{2,1,0:T(8,128)} %add_bitcast_fusion), calls=%async_computation | async-start | bytes 196608 | tf_op jit(solution)/shard_map/all_to_all | solution.py:334
  60.6 12.8 %all-to-all-start.1 = ((f32[16,8,384]{2,1,0:T(8,128)}), f32[16,8,384]{2,1,0:T(8,128)}, u32[]{:S(2)}, u32[]{:S(2)}) async-start(f32[16,8,384]{2,1,0:T(8,128)} %sum_copies.2), calls=%async_computation.1 | async-start | bytes 393216 | tf_op jit(solution)/shard_map/all_to_all | solution.py:334
  73.4 24.2 %collective-permute-start.10 = (bf16[1536,256]{1,0:T(8,128)(2,1)S(1)}, bf16[1536,256]{1,0:T(8,128)(2,1)S(1)}, u32[]{:S(2)}, u32[]{:S(2)}) collective-permute-start(bf16[1536,256]{1,0:T(8,128)(2,1)S(1)} %get-tuple-element.25.refs_0_), channel_id=1, source_target_pairs={{0,2},{1,3},{2,0},{3,1},{4,6},{5,7},{6,4},{7,5},{8,10},{9,11},{10,... | collective-permute-start | bytes 2359304 | tf_op jit(solution)/shard_map/ppermute | solution.py:330
  85.1 5.8 %collective-permute-start.9 = (f32[64,384]{1,0:T(8,128)S(1)}, f32[64,384]{1,0:T(8,128)S(1)}, u32[]{:S(2)}, u32[]{:S(2)}) collective-permute-start(f32[64,384]{1,0:T(8,128)S(1)} %bitcast.82), channel_id=1, source_target_pairs={{0,4},{4,0},{1,5},{5,1},{2,6},{6,2},{3,7},{7,3},{8,12},{12,8},{9,1... | collective-permute-start | bytes 294920 | tf_op jit(solution)/shard_map/ppermute | solution.py:330
  97.5 9.5 %copy-start.3 = (f32[768,256]{1,0:T(8,128)S(1)}, f32[768,256]{1,0:T(8,128)}, u32[]{:S(2)}) copy-start(f32[768,256]{1,0:T(8,128)} %copy-done.2) | copy-start | bytes 2359300
  97.5 9.5 %copy-start.5 = (f32[768,256]{1,0:T(8,128)S(1)}, f32[768,256]{1,0:T(8,128)}, u32[]{:S(2)}) copy-start(f32[768,256]{1,0:T(8,128)} %copy-done.4) | copy-start | bytes 2359300
  100.7 1.6 %collective-permute-start.11 = (f32[32,16,128]{2,1,0:T(8,128)S(1)}, f32[32,16,128]{2,1,0:T(8,128)S(1)}, u32[]{:S(2)}, u32[]{:S(2)}) collective-permute-start(f32[32,16,128]{2,1,0:T(8,128)S(1)} %get-tuple-element.27), channel_id=1, source_target_pairs={{0,4},{4,0},{1,5},{5,1},{2,6},{6,2},{3,7},{7,3},{8,12},{12,8},{9,1... | collective-permute-start | bytes 786440 | tf_op jit(solution)/shard_map/ppermute | solution.py:330
  103.1 15.7 %all-to-all-start.3 = ((f32[32,16,128]{2,1,0:T(8,128)}), f32[32,16,128]{2,1,0:T(8,128)S(1)}, u32[]{:S(2)}, u32[]{:S(2)}) async-start(f32[32,16,128]{2,1,0:T(8,128)} %add.70), calls=%async_computation.3 | async-start | bytes 524288 | tf_op jit(solution)/shard_map/all_to_all | solution.py:334

commit v4 on v3

--- a/solution.py
+++ b/solution.py
@@ -51,7 +51,7 @@
             out_specs=pl.BlockSpec((per_step, half + pad, rank), lambda i, which: (i, 0, 0)),
         ),
         out_shape=jax.ShapeDtypeStruct((n * per_step, half + pad, rank), jnp.float32),
-        compiler_params=params(48),
+        compiler_params=params(52),
         cost_estimate=cost(2 * n * per_step * half * cols * rank, 4 * n * per_step * half * cols),
         name=name,
     )(which, snapshots, omega)
@@ -152,7 +152,7 @@
             out_specs=pl.BlockSpec((rank, cols), whole),
         ),
         out_shape=jax.ShapeDtypeStruct((rank, cols), jnp.float32),
-        compiler_params=params(48),
+        compiler_params=params(52),
         cost_estimate=cost(2 * n * rows * cols * rank, 2 * n * rows * (cols + rank)),
         name="cross_part",
     )(order, snapshots, *start, *lows)
@@ -274,29 +274,20 @@
         send[:, each * q : each * (q + 1), :] = jnp.where(first, two, one)
 
 
-def coeff_parts(core_block, inverse, near, low, snapshots, factor, chips):
+def coeff_parts(core, inverse, near, low, snap, factor, chips):
     rank, cols = near.shape
     rows = low.shape[0]
     sub = rank // (2 * chips) * (cols // 128)
-    whole = lambda *shape: pl.BlockSpec(shape, lambda i, which: (0,) * len(shape))
+    vmem = pl.BlockSpec(memory_space=pltpu.VMEM)
     return pl.pallas_call(
         functools.partial(coeff_kernel, factor=factor),
-        grid_spec=pltpu.PrefetchScalarGridSpec(
-            num_scalar_prefetch=1,
-            grid=(1,),
-            in_specs=[
-                whole(rank, rank),
-                whole(rank, cols),
-                whole(rows, rank),
-                pl.BlockSpec((rows, cols), lambda i, which: (which[1], 0)),
-            ],
-            out_specs=[whole(chips, sub, 128)] * 2,
-        ),
+        in_specs=[pl.BlockSpec(memory_space=pltpu.SMEM)] + [vmem] * 4,
+        out_specs=[vmem] * 2,
         out_shape=[jax.ShapeDtypeStruct((chips, sub, 128), jnp.float32)] * 2,
-        compiler_params=params(48),
+        compiler_params=params(),
         cost_estimate=cost(2 * rows * cols * rank + 12 * rank * rank * cols, 2 * rows * cols),
         name="coeff_parts",
-    )(core_block, inverse, near, low, snapshots)
+    )(core, inverse, near, low, snap)
 
 
 def basis_kernel(top, bottom, inverse, out, *, factor, steps):
@@ -368,20 +359,21 @@
     cross = cross_part(snapshots, block(0), [low])
     held, cross = tie((exchange(held.reshape(nz, -1, held.shape[1]), "z"), cross))
 
-    held, cross = tie((sum_copies(held, lax.axis_size("y") * nx), cross))
+    place = lax.rem(x + 2, nx) * rows
+    held, cross, place = tie((sum_copies(held, lax.axis_size("y") * nx), cross, place))
     cross = cross_part(snapshots, block(3, 1), [left, right], cross)
-    held, cross = tie((exchange(held, ("y", "x")), cross))
-
-    low, cross = tie((low, cross))
+    snap = lax.dynamic_slice_in_dim(snapshots, place, rows, 0)
+    held, cross, snap = tie((exchange(held, ("y", "x")), cross, snap))
+
+    held, low = tie((sum_copies(held, nz), low))
     across = shift(low, "x", 2)
-    held = exchange(sum_copies(held, nz), "z")
+    held = exchange(held, "z")
     held = held.reshape(-1, held.shape[2])
     other = shift(held, "c", 1)
     inverse = lower_inverse(core, held, other)
 
     factor = (total_cols / total_rows) ** 0.5
-    where = at(c, lax.rem(x + 2, nx))
-    keep, send = coeff_parts(where, inverse, cross, across, snapshots, factor, chips)
+    keep, send = coeff_parts(core, inverse, cross, across, snap, factor, chips)
     both = keep + shift(send, "c", 1)
     coeff = jnp.sum(exchange(both, ("z", "y")), axis=0)
     coeff = coeff.reshape(cols // 128, -1, 128).transpose(1, 0, 2).reshape(-1, cols)

time: 120 us -> 118 us (0.983)
  waiting for transfers between devices: 29.9 us -> 26.4 us
  other arithmetic: 7.71 us -> 5.23 us
  local copies, waits for them, and re-layouts: 3.11 us -> 5.41 us
  starting transfers between devices: 38.1 us -> 39.5 us
    all_to_all x3, waiting for transfers between devices: 18.1 us -> 13.5 us  [exchange(): return lax.all_to_all(value, axes, 0, 0, tiled=True)]
    unnamed x12 -> x18, local copies, waits for them, and re-layouts: 0.97 us -> 3.26 us
    pallas_call x1, Pallas kernels: 3.17 us -> 1.22 us  [coeff_parts(): pl.pallas_call(functools.partial(coeff_kernel, factor=factor), in_specs=[...]
    another operation x2, other arithmetic: 0.37 us -> 2.25 us
    dynamic_slice x0 -> x1, local copies, waits for them, and re-layouts: none -> 1.8 us  [per_device(): snap = lax.dynamic_slice_in_dim(snapshots, place, rows, 0)]
    convert_element_type x2, local copies, waits for them, and re-layouts: 2.14 us -> 0.35 us  [per_device(): half16 = lambda v: v.astype(jnp.float16)]
    pallas_call x3, Pallas kernels: 8.32 us -> 9.76 us  [sketch_rows(): pl.pallas_call(functools.partial(sketch_kernel, scaled=scaled, pad=pad),...]
    exp2 x4, other arithmetic: 1.4 us -> 0.03 us  [add_back(): return got[:half].astype(jnp.float32) * jnp.exp2(power - 14.0)]
  transfers between devices with their start and end apart: 15 -> 15, of which waited for: 10 -> 8; matrix products, arithmetic and copies ran while one was open for 5% -> 5% of each run, Pallas kernels for 19% -> 20%
where the time goes in v4:
time: 118 us; the launch traced here: 117 us
  starting transfers between devices  39.5 us (33%)
  Pallas kernels  29.7 us (25%)
  waiting for transfers between devices  26.4 us (22%)
  blocking collectives  9.94 us (8%)
  local copies, waits for them, and re-layouts  5.41 us (5%)
  other arithmetic  5.23 us (4%)
    ppermute x12, starting transfers between devices, shift(): return lax.ppermute(value, axis, [(i, (i + by) % n) for i in range(n)])  21.8 us
    all_to_all x3, starting transfers between devices, exchange(): return lax.all_to_all(value, axes, 0, 0, tiled=True)  17.7 us
    all_to_all x3, waiting for transfers between devices, exchange(): return lax.all_to_all(value, axes, 0, 0, tiled=True)  13.5 us
    ppermute x12, waiting for transfers between devices, shift(): return lax.ppermute(value, axis, [(i, (i + by) % n) for i in range(n)])  13 us
    all_to_all x1, blocking collectives, exchange(): return lax.all_to_all(value, axes, 0, 0, tiled=True)  9.94 us
    pallas_call x3, Pallas kernels, sketch_rows(): pl.pallas_call(functools.partial(sketch_kernel, scaled=scaled, pad=pad),...  9.76 us
    pallas_call x1, Pallas kernels, lower_inverse(): pl.pallas_call(inverse_kernel, in_specs=[pl.BlockSpec(memory_space=pltpu....  6.65 us
    pallas_call x2, Pallas kernels, cross_part(): pl.pallas_call(functools.partial(cross_kernel, has_before=before is not N...  5.65 us
  transfers between devices with their start and end apart: 15, of which 8 were waited for; matrix products, arithmetic and copies ran while one was open for 5% of the time, Pallas kernels for 20%

profile of v4, /device:TPU:1, one launch (start us, length us, event | category | flops | bytes accessed | tf_op | source)
XLA Modules:
  0.0 117.1 jit_solution(4234229902024271975)
XLA Ops:
  1.6 2.1 %far_chunk.1 = f32[2,784,256]{2,1,0:T(8,128)S(1)} custom-call(s32[1]{0:T(128)} %bitcast.8.which, bf16[6144,512]{1,0:T(8,128)(2,1)} %snap.9, bf16[512,256]{1,0:T(8,128)(2,1)S(1)} %copy-done), custom_call_target="tpu_custom_call" | custom-call | flops 402653184 | bytes 3145728 | tf_op jit(solution)/shard_map/far_chunk/pallas_call | solution.py:42
  4.0 2.1 %collective-permute-start.1 = (f16[784,256]{1,0:T(8,128)(2,1)S(1)}, f16[784,256]{1,0:T(8,128)(2,1)S(1)}, u32[]{:S(2)}, u32[]{:S(2)}) collective-permute-start(f16[784,256]{1,0:T(8,128)(2,1)S(1)} %get-tuple-element.45), channel_id=1, source_target_pairs={{0,1},{1,2},{2,3},{3,0},{4,5},{5,6},{6,7},{7,4},{8,9},{9,10},{10,1... | collective-permute-start | bytes 1204232 | tf_op jit(solution)/shard_map/ppermute | solution.py:321
  6.1 1.4 %collective-permute-start.4 = (f16[784,256]{1,0:T(8,128)(2,1)S(1)}, f16[784,256]{1,0:T(8,128)(2,1)S(1)}, u32[]{:S(2)}, u32[]{:S(2)}) collective-permute-start(f16[784,256]{1,0:T(8,128)(2,1)S(1)} %get-tuple-element.44), channel_id=1, source_target_pairs={{0,3},{1,0},{2,1},{3,2},{4,7},{5,4},{6,5},{7,6},{8,11},{9,8},{10,9... | collective-permute-start | bytes 1204232 | tf_op jit(solution)/shard_map/ppermute | solution.py:321
  7.6 5.6 %near_chunks.1 = f32[4,784,256]{2,1,0:T(8,128)} custom-call(s32[4]{0:T(128)S(1)} %pad_add_fusion.which, bf16[6144,512]{1,0:T(8,128)(2,1)} %snap.9, bf16[512,256]{1,0:T(8,128)(2,1)S(1)} %copy-done.1), custom_call_target="tpu_custom_call" | custom-call | flops 805306368 | bytes 6291456 | tf_op jit(solution)/shard_map/near_chunks/pallas_call | solution.py:42
  13.1 2.1 %convert.8 = f16[4,784,256]{2,1,0:T(8,128)(2,1)S(1)} convert(f32[4,784,256]{2,1,0:T(8,128)} %near_chunks.1) | non-fusion elementwise | flops 802816 | bytes 4816896 | tf_op jit(solution)/shard_map/convert.3
  15.6 2.6 %collective-permute-start = (f16[784,256]{1,0:T(8,128)(2,1)S(1)}, f16[784,256]{1,0:T(8,128)(2,1)S(1)}, u32[]{:S(2)}, u32[]{:S(2)}) collective-permute-start(f16[784,256]{1,0:T(8,128)(2,1)S(1)} %get-tuple-element.41), channel_id=1, source_target_pairs={{0,3},{1,0},{2,1},{3,2},{4,7},{5,4},{6,5},{7,6},{8,11},{9,8},{10,9... | collective-permute-start | bytes 1204232 | tf_op jit(solution)/shard_map/ppermute | solution.py:321
  18.2 2.1 %own_chunk.1 = f32[2,768,256]{2,1,0:T(8,128)S(1)} custom-call(s32[1]{0:T(128)} %bitcast.which, bf16[6144,512]{1,0:T(8,128)(2,1)} %snap.9, bf16[512,256]{1,0:T(8,128)(2,1)S(1)} %copy-done.1), custom_call_target="tpu_custom_call" | custom-call | flops 402653184 | bytes 3145728 | tf_op jit(solution)/shard_map/own_chunk/pallas_call | solution.py:42
  21.1 2.7 %collective-permute-start.5 = (f16[784,256]{1,0:T(8,128)(2,1)S(1)}, f16[784,256]{1,0:T(8,128)(2,1)S(1)}, u32[]{:S(2)}, u32[]{:S(2)}) collective-permute-start(f16[784,256]{1,0:T(8,128)(2,1)S(1)} %get-tuple-element.36), channel_id=1, source_target_pairs={{0,3},{1,0},{2,1},{3,2},{4,7},{5,4},{6,5},{7,6},{8,11},{9,8},{10,9... | collective-permute-start | bytes 1204232 | tf_op jit(solution)/shard_map/ppermute | solution.py:321
  24.4 9.2 %collective-permute-done.2 = f16[784,256]{1,0:T(8,128)(2,1)S(1)} collective-permute-done((f16[784,256]{1,0:T(8,128)(2,1)S(1)}, f16[784,256]{1,0:T(8,128)(2,1)S(1)}, u32[]{:S(2)}, u32[]{:S(2)}) %collective-permute-start.2) | collective-permute-done | bytes 401440 | tf_op jit(solution)/shard_map/ppermute | solution.py:321
  34.1 1.7 %gram_of.1 = (f32[64,384]{1,0:T(8,128)S(1)}, f32[64,384]{1,0:T(8,128)S(1)}, bf16[1536,256]{1,0:T(8,128)(2,1)S(1)}) custom-call(s32[1]{0:T(128)} %bitcast.26.core, f32[768,256]{1,0:T(8,128)S(1)} %get-tuple-element.43.top, f32[768,256]{1,0:T(8,128)S(1)} %get-tuple-element.42.bottom), custom_call_target="tpu_custom_call" | custom-call | flops 1207959552 | bytes 2359296 | tf_op jit(solution)/shard_map/gram_of/pallas_call | solution.py:91
  35.8 1.1 collective-permute-start.7
  36.9 1.7 %collective-permute-start.8 = (bf16[1536,256]{1,0:T(8,128)(2,1)S(1)}, bf16[1536,256]{1,0:T(8,128)(2,1)}, u32[]{:S(2)}, u32[]{:S(2)}) collective-permute-start(bf16[1536,256]{1,0:T(8,128)(2,1)S(1)} %get-tuple-element.28.refs_0_), channel_id=1, source_target_pairs={{0,3},{1,0},{2,1},{3,2},{4,7},{5,4},{6,5},{7,6},{8,11},{9,8},{10,9... | collective-permute-start | bytes 2359304 | tf_op jit(solution)/shard_map/ppermute | solution.py:321
  38.6 3.9 %collective-permute-start.6 = (f32[64,384]{1,0:T(8,128)S(1)}, f32[64,384]{1,0:T(8,128)S(1)}, u32[]{:S(2)}, u32[]{:S(2)}) collective-permute-start(f32[64,384]{1,0:T(8,128)S(1)} %get-tuple-element.18), channel_id=1, source_target_pairs={{0,4},{4,0},{1,5},{5,1},{2,6},{6,2},{3,7},{7,3},{8,12},{12,8},{9,1... | collective-permute-start | bytes 294920 | tf_op jit(solution)/shard_map/ppermute | solution.py:321
  44.0 8.3 %all-to-all-start = ((f32[8,8,384]{2,1,0:T(8,128)}), f32[8,8,384]{2,1,0:T(8,128)S(1)}, u32[]{:S(2)}, u32[]{:S(2)}) async-start(f32[8,8,384]{2,1,0:T(8,128)} %add_bitcast_fusion), calls=%async_computation | async-start | bytes 196608 | tf_op jit(solution)/shard_map/all_to_all | solution.py:325
  52.4 2.0 %cross_part.2.refs_0_ = f32[256,512]{1,0:T(8,128)S(1)} custom-call(s32[1]{0:T(128)} %bitcast.28.which, bf16[6144,512]{1,0:T(8,128)(2,1)} %snap.9, bf16[1536,256]{1,0:T(8,128)(2,1)S(1)} %get-tuple-element.28.refs_0_), custom_call_target="tpu_custom_call" | custom-call | flops 402653184 | bytes 2359296 | tf_op jit(solution)/shard_map/cross_part/pallas_call | solution.py:144
  54.4 5.4 %all-to-all-done.got = f32[8,8,384]{2,1,0:T(8,128)S(1)} async-done(((f32[8,8,384]{2,1,0:T(8,128)}), f32[8,8,384]{2,1,0:T(8,128)S(1)}, u32[]{:S(2)}, u32[]{:S(2)}) %all-to-all-start) | async-done | bytes 98336 | tf_op jit(solution)/shard_map/all_to_all | solution.py:325
  60.5 5.5 %all-to-all-start.1 = ((f32[16,8,384]{2,1,0:T(8,128)}), f32[16,8,384]{2,1,0:T(8,128)}, u32[]{:S(2)}, u32[]{:S(2)}) async-start(f32[16,8,384]{2,1,0:T(8,128)} %sum_copies.2), calls=%async_computation.1 | async-start | bytes 393216 | tf_op jit(solution)/shard_map/all_to_all | solution.py:325
  66.0 1.8 %constant_dynamic-slice_fusion.snap = bf16[1536,512]{1,0:T(8,128)(2,1)S(1)} fusion(bf16[6144,512]{1,0:T(8,128)(2,1)} %snap.9, s32[]{:T(128)S(6)} %select_n.12), kind=kLoop, calls=%fused_computation.52 | loop fusion | bytes 3145732 | tf_op jit(solution)/shard_map/dynamic_slice | solution.py:365
  67.8 3.7 %cross_part.3.near = f32[256,512]{1,0:T(8,128)S(1)} custom-call(s32[2]{0:T(128)S(1)} %pad_add_fusion.1.which, bf16[6144,512]{1,0:T(8,128)(2,1)} %snap.9, f32[256,512]{1,0:T(8,128)S(1)} %cross_part.2.refs_0_, bf16[1536,256]{1,0:T(8,128)(2,1)} %collective-permute-done.7.refs_1_, bf16[1536,256]{1,0:T(8,128)(2,1)} %collective-permute-done.8.refs_2_), custom_call_target="tpu_custom_call" | custom-call | flops 805306368 | bytes 4718592 | tf_op jit(solution)/shard_map/cross_part/pallas_call | solution.py:144
  71.5 1.8 %all-to-all-done.1.got = f32[16,8,384]{2,1,0:T(8,128)} async-done(((f32[16,8,384]{2,1,0:T(8,128)}), f32[16,8,384]{2,1,0:T(8,128)}, u32[]{:S(2)}, u32[]{:S(2)}) %all-to-all-start.1) | async-done | bytes 196640 | tf_op jit(solution)/shard_map/all_to_all | solution.py:325
  73.3 0.9 sum_copies.3
  74.2 1.1 collective-permute-start.10
  75.4 9.9 %all_to_all.20 = f32[8,8,384]{2,1,0:T(8,128)S(1)} all-to-all(f32[8,8,384]{2,1,0:T(8,128)S(1)} %sum_copies.3), channel_id=1, replica_groups=mesh['z'=8,'y'=4,'c'=2,'x'=4] {'z'}, dimensions={0} | all-to-all | bytes 196608 | tf_op jit(solution)/shard_map/all_to_all | solution.py:325
  85.3 4.6 %collective-permute-start.9 = (f32[64,384]{1,0:T(8,128)S(1)}, f32[64,384]{1,0:T(8,128)S(1)}, u32[]{:S(2)}, u32[]{:S(2)}) collective-permute-start(f32[64,384]{1,0:T(8,128)S(1)} %bitcast.82), channel_id=1, source_target_pairs={{0,4},{4,0},{1,5},{5,1},{2,6},{6,2},{3,7},{7,3},{8,12},{12,8},{9,1... | collective-permute-start | bytes 294920 | tf_op jit(solution)/shard_map/ppermute | solution.py:321
  90.8 6.6 %lower_inverse.1.inverse = f32[256,256]{1,0:T(8,128)S(1)} custom-call(s32[1]{0:T(128)} %bitcast.26.core, f32[64,384]{1,0:T(8,128)S(1)} %bitcast.83, f32[64,384]{1,0:T(8,128)S(1)} %collective-permute-done.9.other), custom_call_target="tpu_custom_call" | custom-call | flops 5000000000 | bytes 98304 | tf_op jit(solution)/shard_map/lower_inverse/pallas_call | solution.py:246
  97.5 1.2 %coeff_parts.1 = (f32[32,16,128]{2,1,0:T(8,128)S(1)}, f32[32,16,128]{2,1,0:T(8,128)S(1)}) custom-call(s32[1]{0:T(128)} %bitcast.26.core, f32[256,256]{1,0:T(8,128)S(1)} %lower_inverse.1.inverse, f32[256,512]{1,0:T(8,128)S(1)} %cross_part.3.near, bf16[1536,256]{1,0:T(8,128)(2,1)S(1)} %collective-permute-done.10.low, ...), custom_call_target="tpu_custom_call" | custom-call | flops 805306368 | bytes 1572864 | tf_op jit(solution)/shard_map/coeff_parts/pallas_call | solution.py:282
  99.2 1.2 %collective-permute-done.11 = f32[32,16,128]{2,1,0:T(8,128)S(1)} collective-permute-done((f32[32,16,128]{2,1,0:T(8,128)S(1)}, f32[32,16,128]{2,1,0:T(8,128)S(1)}, u32[]{:S(2)}, u32[]{:S(2)}) %collective-permute-start.11) | collective-permute-done | bytes 262176 | tf_op jit(solution)/shard_map/ppermute | solution.py:321
  101.1 3.9 %all-to-all-start.3 = ((f32[32,16,128]{2,1,0:T(8,128)}), f32[32,16,128]{2,1,0:T(8,128)S(1)}, u32[]{:S(2)}, u32[]{:S(2)}) async-start(f32[32,16,128]{2,1,0:T(8,128)} %add.74), calls=%async_computation.3 | async-start | bytes 524288 | tf_op jit(solution)/shard_map/all_to_all | solution.py:325
  105.0 1.1 copy-done.5
  106.2 0.9 copy-done.7
  107.1 3.1 %basis_rows.1 = f32[1536,256]{1,0:T(8,128)} custom-call(f32[768,256]{1,0:T(8,128)S(1)} %copy-done.5, f32[768,256]{1,0:T(8,128)S(1)} %copy-done.3, f32[256,256]{1,0:T(8,128)S(1)} %copy-done.7), custom_call_target="tpu_custom_call" | custom-call | flops 1207959552 | bytes 3145728 | tf_op jit(solution)/shard_map/basis_rows/pallas_call | solution.py:303
  110.2 6.3 %all-to-all-done.3 = f32[32,16,128]{2,1,0:T(8,128)S(1)} async-done(((f32[32,16,128]{2,1,0:T(8,128)}), f32[32,16,128]{2,1,0:T(8,128)S(1)}, u32[]{:S(2)}, u32[]{:S(2)}) %all-to-all-start.3) | async-done | bytes 262176 | tf_op jit(solution)/shard_map/all_to_all | solution.py:325
  (46 shorter events, 8.6 us)
Async XLA Ops:
  0.6 1.0 copy-start
  3.7 3.9 %copy-start.1 = (bf16[512,256]{1,0:T(8,128)(2,1)S(1)}, bf16[512,256]{1,0:T(8,128)(2,1)}, u32[]{:S(2)}) copy-start(bf16[512,256]{1,0:T(8,128)(2,1)} %omega.5) | copy-start | bytes 786436
  4.0 16.3 %collective-permute-start.1 = (f16[784,256]{1,0:T(8,128)(2,1)S(1)}, f16[784,256]{1,0:T(8,128)(2,1)S(1)}, u32[]{:S(2)}, u32[]{:S(2)}) collective-permute-start(f16[784,256]{1,0:T(8,128)(2,1)S(1)} %get-tuple-element.45), channel_id=1, source_target_pairs={{0,1},{1,2},{2,3},{3,0},{4,5},{5,6},{6,7},{7,4},{8,9},{9,10},{10,1... | collective-permute-start | bytes 1204232 | tf_op jit(solution)/shard_map/ppermute | solution.py:321
  6.1 14.2 %collective-permute-start.4 = (f16[784,256]{1,0:T(8,128)(2,1)S(1)}, f16[784,256]{1,0:T(8,128)(2,1)S(1)}, u32[]{:S(2)}, u32[]{:S(2)}) collective-permute-start(f16[784,256]{1,0:T(8,128)(2,1)S(1)} %get-tuple-element.44), channel_id=1, source_target_pairs={{0,3},{1,0},{2,1},{3,2},{4,7},{5,4},{6,5},{7,6},{8,11},{9,8},{10,9... | collective-permute-start | bytes 1204232 | tf_op jit(solution)/shard_map/ppermute | solution.py:321
  15.4 9.0 %collective-permute-start.3 = (f16[784,256]{1,0:T(8,128)(2,1)S(1)}, f16[784,256]{1,0:T(8,128)(2,1)S(1)}, u32[]{:S(2)}, u32[]{:S(2)}) collective-permute-start(f16[784,256]{1,0:T(8,128)(2,1)S(1)} %get-tuple-element.40), channel_id=1, source_target_pairs={{0,1},{1,2},{2,3},{3,0},{4,5},{5,6},{6,7},{7,4},{8,9},{9,10},{10,1... | collective-permute-start | bytes 1204232 | tf_op jit(solution)/shard_map/ppermute | solution.py:321
  15.6 8.8 %collective-permute-start = (f16[784,256]{1,0:T(8,128)(2,1)S(1)}, f16[784,256]{1,0:T(8,128)(2,1)S(1)}, u32[]{:S(2)}, u32[]{:S(2)}) collective-permute-start(f16[784,256]{1,0:T(8,128)(2,1)S(1)} %get-tuple-element.41), channel_id=1, source_target_pairs={{0,3},{1,0},{2,1},{3,2},{4,7},{5,4},{6,5},{7,6},{8,11},{9,8},{10,9... | collective-permute-start | bytes 1204232 | tf_op jit(solution)/shard_map/ppermute | solution.py:321
  18.2 2.4 %copy-start.8 = (f32[4,784,256]{2,1,0:T(8,128)S(1)}, f32[4,784,256]{2,1,0:T(8,128)}, u32[]{:S(2)}) copy-start(f32[4,784,256]{2,1,0:T(8,128)} %near_chunks.1) | copy-start | bytes 9633796
  21.0 12.7 %collective-permute-start.2 = (f16[784,256]{1,0:T(8,128)(2,1)S(1)}, f16[784,256]{1,0:T(8,128)(2,1)S(1)}, u32[]{:S(2)}, u32[]{:S(2)}) collective-permute-start(f16[784,256]{1,0:T(8,128)(2,1)S(1)} %get-tuple-element.37), channel_id=1, source_target_pairs={{0,1},{1,2},{2,3},{3,0},{4,5},{5,6},{6,7},{7,4},{8,9},{9,10},{10,1... | collective-permute-start | bytes 1204232 | tf_op jit(solution)/shard_map/ppermute | solution.py:321
  21.1 12.6 %collective-permute-start.5 = (f16[784,256]{1,0:T(8,128)(2,1)S(1)}, f16[784,256]{1,0:T(8,128)(2,1)S(1)}, u32[]{:S(2)}, u32[]{:S(2)}) collective-permute-start(f16[784,256]{1,0:T(8,128)(2,1)S(1)} %get-tuple-element.36), channel_id=1, source_target_pairs={{0,3},{1,0},{2,1},{3,2},{4,7},{5,4},{6,5},{7,6},{8,11},{9,8},{10,9... | collective-permute-start | bytes 1204232 | tf_op jit(solution)/shard_map/ppermute | solution.py:321
  34.0 1.7 %copy-start.2 = (f32[768,256]{1,0:T(8,128)}, f32[768,256]{1,0:T(8,128)S(1)}, u32[]{:S(2)}) copy-start(f32[768,256]{1,0:T(8,128)S(1)} %get-tuple-element.42.bottom) | copy-start | bytes 2359300
  34.0 1.7 %copy-start.4 = (f32[768,256]{1,0:T(8,128)}, f32[768,256]{1,0:T(8,128)S(1)}, u32[]{:S(2)}) copy-start(f32[768,256]{1,0:T(8,128)S(1)} %get-tuple-element.43.top) | copy-start | bytes 2359300
  35.8 32.1 %collective-permute-start.7 = (bf16[1536,256]{1,0:T(8,128)(2,1)S(1)}, bf16[1536,256]{1,0:T(8,128)(2,1)}, u32[]{:S(2)}, u32[]{:S(2)}) collective-permute-start(bf16[1536,256]{1,0:T(8,128)(2,1)S(1)} %get-tuple-element.28.refs_0_), channel_id=1, source_target_pairs={{0,1},{1,2},{2,3},{3,0},{4,5},{5,6},{6,7},{7,4},{8,9},{9,10},{10,1... | collective-permute-start | bytes 2359304 | tf_op jit(solution)/shard_map/ppermute | solution.py:321
  36.9 31.0 %collective-permute-start.8 = (bf16[1536,256]{1,0:T(8,128)(2,1)S(1)}, bf16[1536,256]{1,0:T(8,128)(2,1)}, u32[]{:S(2)}, u32[]{:S(2)}) collective-permute-start(bf16[1536,256]{1,0:T(8,128)(2,1)S(1)} %get-tuple-element.28.refs_0_), channel_id=1, source_target_pairs={{0,3},{1,0},{2,1},{3,2},{4,7},{5,4},{6,5},{7,6},{8,11},{9,8},{10,9... | collective-permute-start | bytes 2359304 | tf_op jit(solution)/shard_map/ppermute | solution.py:321
  38.6 4.8 %collective-permute-start.6 = (f32[64,384]{1,0:T(8,128)S(1)}, f32[64,384]{1,0:T(8,128)S(1)}, u32[]{:S(2)}, u32[]{:S(2)}) collective-permute-start(f32[64,384]{1,0:T(8,128)S(1)} %get-tuple-element.18), channel_id=1, source_target_pairs={{0,4},{4,0},{1,5},{5,1},{2,6},{6,2},{3,7},{7,3},{8,12},{12,8},{9,1... | collective-permute-start | bytes 294920 | tf_op jit(solution)/shard_map/ppermute | solution.py:321
  44.0 15.7 %all-to-all-start = ((f32[8,8,384]{2,1,0:T(8,128)}), f32[8,8,384]{2,1,0:T(8,128)S(1)}, u32[]{:S(2)}, u32[]{:S(2)}) async-start(f32[8,8,384]{2,1,0:T(8,128)} %add_bitcast_fusion), calls=%async_computation | async-start | bytes 196608 | tf_op jit(solution)/shard_map/all_to_all | solution.py:325
  60.5 12.8 %all-to-all-start.1 = ((f32[16,8,384]{2,1,0:T(8,128)}), f32[16,8,384]{2,1,0:T(8,128)}, u32[]{:S(2)}, u32[]{:S(2)}) async-start(f32[16,8,384]{2,1,0:T(8,128)} %sum_copies.2), calls=%async_computation.1 | async-start | bytes 393216 | tf_op jit(solution)/shard_map/all_to_all | solution.py:325
  74.2 23.3 %collective-permute-start.10 = (bf16[1536,256]{1,0:T(8,128)(2,1)S(1)}, bf16[1536,256]{1,0:T(8,128)(2,1)S(1)}, u32[]{:S(2)}, u32[]{:S(2)}) collective-permute-start(bf16[1536,256]{1,0:T(8,128)(2,1)S(1)} %get-tuple-element.28.refs_0_), channel_id=1, source_target_pairs={{0,2},{1,3},{2,0},{3,1},{4,6},{5,7},{6,4},{7,5},{8,10},{9,11},{10,... | collective-permute-start | bytes 2359304 | tf_op jit(solution)/shard_map/ppermute | solution.py:321
  85.3 5.5 %collective-permute-start.9 = (f32[64,384]{1,0:T(8,128)S(1)}, f32[64,384]{1,0:T(8,128)S(1)}, u32[]{:S(2)}, u32[]{:S(2)}) collective-permute-start(f32[64,384]{1,0:T(8,128)S(1)} %bitcast.82), channel_id=1, source_target_pairs={{0,4},{4,0},{1,5},{5,1},{2,6},{6,2},{3,7},{7,3},{8,12},{12,8},{9,1... | collective-permute-start | bytes 294920 | tf_op jit(solution)/shard_map/ppermute | solution.py:321
  97.5 1.3 %copy-start.6 = (f32[256,256]{1,0:T(8,128)}, f32[256,256]{1,0:T(8,128)S(1)}, u32[]{:S(2)}) copy-start(f32[256,256]{1,0:T(8,128)S(1)} %lower_inverse.1.inverse) | copy-start | bytes 786436
  97.5 7.5 %copy-start.3 = (f32[768,256]{1,0:T(8,128)S(1)}, f32[768,256]{1,0:T(8,128)}, u32[]{:S(2)}) copy-start(f32[768,256]{1,0:T(8,128)} %copy-done.2) | copy-start | bytes 2359300
  98.8 1.6 %collective-permute-start.11 = (f32[32,16,128]{2,1,0:T(8,128)S(1)}, f32[32,16,128]{2,1,0:T(8,128)S(1)}, u32[]{:S(2)}, u32[]{:S(2)}) collective-permute-start(f32[32,16,128]{2,1,0:T(8,128)S(1)} %get-tuple-element.31), channel_id=1, source_target_pairs={{0,4},{4,0},{1,5},{5,1},{2,6},{6,2},{3,7},{7,3},{8,12},{12,8},{9,1... | collective-permute-start | bytes 786440 | tf_op jit(solution)/shard_map/ppermute | solution.py:321
  101.1 15.4 %all-to-all-start.3 = ((f32[32,16,128]{2,1,0:T(8,128)}), f32[32,16,128]{2,1,0:T(8,128)S(1)}, u32[]{:S(2)}, u32[]{:S(2)}) async-start(f32[32,16,128]{2,1,0:T(8,128)} %add.74), calls=%async_computation.3 | async-start | bytes 524288 | tf_op jit(solution)/shard_map/all_to_all | solution.py:325
  105.0 1.1 copy-start.5
  106.1 0.9 copy-start.7

commit v5 on v4

--- a/solution.py
+++ b/solution.py
@@ -341,12 +341,14 @@
 
     far = sketch(which=at(lax.rem(x + 2, nx)), per_step=2, scaled=2, pad=PAD, name="far_chunk")
     far_up, far_down = shift(half16(far[0]), "x", 1), shift(half16(far[1]), "x", -1)
-    places = at(ahead(1) + 1, ahead(3), ahead(1), ahead(3) + 1)
-    near = sketch(which=places, per_step=1, scaled=2, pad=PAD, name="near_chunks")
+    places = at(ahead(1) + 1, ahead(3))
+    near = sketch(which=places, per_step=1, scaled=2, pad=PAD, name="near_halves")
     near_up, near_down = shift(half16(near[0]), "x", 1), shift(half16(near[1]), "x", -1)
+    places = at(ahead(1), ahead(3) + 1)
+    later = sketch(which=places, per_step=1, scaled=0, pad=PAD, name="relay_halves")
     own = sketch(which=at(x), per_step=2, scaled=0, pad=0, name="own_chunk")
-    far_up = shift(relay(far_up, near[2], half), "x", 1)
-    far_down = shift(relay(far_down, near[3], half), "x", -1)
+    far_up = shift(relay(far_up, later[0], half), "x", 1)
+    far_down = shift(relay(far_down, later[1], half), "x", -1)
     top = own[0] + add_back(near_down, half) + add_back(far_up, half)
     bottom = own[1] + add_back(near_up, half) + add_back(far_down, half)
 

time: 118 us -> 117 us (level)
  waiting for transfers between devices: 26.4 us -> 32.3 us
  starting transfers between devices: 39.5 us -> 35.5 us
  other arithmetic: 5.23 us -> 3.3 us
    ppermute x12, waiting for transfers between devices: 13 us -> 18.8 us  [shift(): return lax.ppermute(value, axis, [(i, (i + by) % n) for i in range(n)])]
    ppermute x12, starting transfers between devices: 21.8 us -> 19.1 us  [shift(): return lax.ppermute(value, axis, [(i, (i + by) % n) for i in range(n)])]
    another operation x2, other arithmetic: 2.25 us -> 0.26 us
    all_to_all x3, starting transfers between devices: 17.7 us -> 16.4 us  [exchange(): return lax.all_to_all(value, axes, 0, 0, tiled=True)]
    pallas_call x3 -> x4, Pallas kernels: 9.76 us -> 9.27 us  [sketch_rows(): pl.pallas_call(functools.partial(sketch_kernel, scaled=scaled, pad=pad),...]
    unnamed x18 -> x16, local copies, waits for them, and re-layouts: 3.26 us -> 3.05 us
  transfers between devices with their start and end apart: 15 -> 15, of which waited for: 8 -> 10; matrix products, arithmetic and copies ran while one was open for 5% -> 3% of each run, Pallas kernels for 20% -> 20%
where the time goes in v5:
time: 117 us; the launch traced here: 116 us
  starting transfers between devices  35.5 us (30%)
  waiting for transfers between devices  32.3 us (28%)
  Pallas kernels  29.2 us (25%)
  blocking collectives  9.94 us (8%)
  local copies, waits for them, and re-layouts  5.18 us (4%)
  other arithmetic  3.3 us (3%)
    ppermute x12, starting transfers between devices, shift(): return lax.ppermute(value, axis, [(i, (i + by) % n) for i in range(n)])  19.1 us
    ppermute x12, waiting for transfers between devices, shift(): return lax.ppermute(value, axis, [(i, (i + by) % n) for i in range(n)])  18.8 us
    all_to_all x3, starting transfers between devices, exchange(): return lax.all_to_all(value, axes, 0, 0, tiled=True)  16.4 us
    all_to_all x3, waiting for transfers between devices, exchange(): return lax.all_to_all(value, axes, 0, 0, tiled=True)  13.5 us
    all_to_all x1, blocking collectives, exchange(): return lax.all_to_all(value, axes, 0, 0, tiled=True)  9.94 us
    pallas_call x4, Pallas kernels, sketch_rows(): pl.pallas_call(functools.partial(sketch_kernel, scaled=scaled, pad=pad),...  9.27 us
    pallas_call x1, Pallas kernels, lower_inverse(): pl.pallas_call(inverse_kernel, in_specs=[pl.BlockSpec(memory_space=pltpu....  6.65 us
    pallas_call x2, Pallas kernels, cross_part(): pl.pallas_call(functools.partial(cross_kernel, has_before=before is not N...  5.65 us
  transfers between devices with their start and end apart: 15, of which 10 were waited for; matrix products, arithmetic and copies ran while one was open for 3% of the time, Pallas kernels for 20%

profile of v5, /device:TPU:1, one launch (start us, length us, event | category | flops | bytes accessed | tf_op | source)
XLA Modules:
  0.0 116.3 jit_solution(15179464476739221878)
XLA Ops:
  1.6 2.1 %far_chunk.1 = f32[2,784,256]{2,1,0:T(8,128)S(1)} custom-call(s32[1]{0:T(128)} %bitcast.6.which, bf16[6144,512]{1,0:T(8,128)(2,1)} %snap.11, bf16[512,256]{1,0:T(8,128)(2,1)S(1)} %copy-done), custom_call_target="tpu_custom_call" | custom-call | flops 402653184 | bytes 3145728 | tf_op jit(solution)/shard_map/far_chunk/pallas_call | solution.py:42
  4.0 3.4 %collective-permute-start.4 = (f16[784,256]{1,0:T(8,128)(2,1)S(1)}, f16[784,256]{1,0:T(8,128)(2,1)S(1)}, u32[]{:S(2)}, u32[]{:S(2)}) collective-permute-start(f16[784,256]{1,0:T(8,128)(2,1)S(1)} %get-tuple-element.44), channel_id=1, source_target_pairs={{0,3},{1,0},{2,1},{3,2},{4,7},{5,4},{6,5},{7,6},{8,11},{9,8},{10,9... | collective-permute-start | bytes 1204232 | tf_op jit(solution)/shard_map/ppermute | solution.py:321
  7.5 2.6 %near_halves.1 = f32[2,784,256]{2,1,0:T(8,128)S(1)} custom-call(s32[2]{0:T(128)S(1)} %pad_add_fusion.which, bf16[6144,512]{1,0:T(8,128)(2,1)} %snap.11, bf16[512,256]{1,0:T(8,128)(2,1)S(1)} %copy-done.1), custom_call_target="tpu_custom_call" | custom-call | flops 402653184 | bytes 3145728 | tf_op jit(solution)/shard_map/near_halves/pallas_call | solution.py:42
  10.7 2.6 %collective-permute-start = (f16[784,256]{1,0:T(8,128)(2,1)S(1)}, f16[784,256]{1,0:T(8,128)(2,1)S(1)}, u32[]{:S(2)}, u32[]{:S(2)}) collective-permute-start(f16[784,256]{1,0:T(8,128)(2,1)S(1)} %get-tuple-element.43), channel_id=1, source_target_pairs={{0,3},{1,0},{2,1},{3,2},{4,7},{5,4},{6,5},{7,6},{8,11},{9,8},{10,9... | collective-permute-start | bytes 1204232 | tf_op jit(solution)/shard_map/ppermute | solution.py:321
  13.2 2.0 %own_chunk.1 = f32[2,768,256]{2,1,0:T(8,128)S(1)} custom-call(s32[1]{0:T(128)} %bitcast.which, bf16[6144,512]{1,0:T(8,128)(2,1)} %snap.11, bf16[512,256]{1,0:T(8,128)(2,1)S(1)} %copy-done.1), custom_call_target="tpu_custom_call" | custom-call | flops 402653184 | bytes 3145728 | tf_op jit(solution)/shard_map/own_chunk/pallas_call | solution.py:42
  15.3 2.6 %relay_halves.1 = f32[2,784,256]{2,1,0:T(8,128)S(1)} custom-call(s32[2]{0:T(128)S(1)} %pad_add_fusion.1.which, bf16[6144,512]{1,0:T(8,128)(2,1)} %snap.11, bf16[512,256]{1,0:T(8,128)(2,1)S(1)} %copy-done.1), custom_call_target="tpu_custom_call" | custom-call | flops 402653184 | bytes 3145728 | tf_op jit(solution)/shard_map/relay_halves/pallas_call | solution.py:42
  18.8 1.0 collective-permute-start.5
  20.4 6.6 %collective-permute-done.3 = f16[784,256]{1,0:T(8,128)(2,1)S(1)} collective-permute-done((f16[784,256]{1,0:T(8,128)(2,1)S(1)}, f16[784,256]{1,0:T(8,128)(2,1)S(1)}, u32[]{:S(2)}, u32[]{:S(2)}) %collective-permute-start.3) | collective-permute-done | bytes 401440 | tf_op jit(solution)/shard_map/ppermute | solution.py:321
  27.1 5.5 %collective-permute-done.5 = f16[784,256]{1,0:T(8,128)(2,1)S(1)} collective-permute-done((f16[784,256]{1,0:T(8,128)(2,1)S(1)}, f16[784,256]{1,0:T(8,128)(2,1)S(1)}, u32[]{:S(2)}, u32[]{:S(2)}) %collective-permute-start.5) | collective-permute-done | bytes 401440 | tf_op jit(solution)/shard_map/ppermute | solution.py:321
  32.5 3.1 %collective-permute-done.2 = f16[784,256]{1,0:T(8,128)(2,1)S(1)} collective-permute-done((f16[784,256]{1,0:T(8,128)(2,1)S(1)}, f16[784,256]{1,0:T(8,128)(2,1)S(1)}, u32[]{:S(2)}, u32[]{:S(2)}) %collective-permute-start.2) | collective-permute-done | bytes 401440 | tf_op jit(solution)/shard_map/ppermute | solution.py:321
  36.0 1.7 %gram_of.1 = (f32[64,384]{1,0:T(8,128)S(1)}, f32[64,384]{1,0:T(8,128)S(1)}, bf16[1536,256]{1,0:T(8,128)(2,1)S(1)}) custom-call(s32[1]{0:T(128)} %bitcast.26.core, f32[768,256]{1,0:T(8,128)S(1)} %get-tuple-element.41.top, f32[768,256]{1,0:T(8,128)S(1)} %get-tuple-element.40.bottom), custom_call_target="tpu_custom_call" | custom-call | flops 1207959552 | bytes 2359296 | tf_op jit(solution)/shard_map/gram_of/pallas_call | solution.py:91
  37.8 2.7 %collective-permute-start.8 = (bf16[1536,256]{1,0:T(8,128)(2,1)S(1)}, bf16[1536,256]{1,0:T(8,128)(2,1)}, u32[]{:S(2)}, u32[]{:S(2)}) collective-permute-start(bf16[1536,256]{1,0:T(8,128)(2,1)S(1)} %get-tuple-element.28.refs_0_), channel_id=1, source_target_pairs={{0,3},{1,0},{2,1},{3,2},{4,7},{5,4},{6,5},{7,6},{8,11},{9,8},{10,9... | collective-permute-start | bytes 2359304 | tf_op jit(solution)/shard_map/ppermute | solution.py:321
  40.5 2.4 %collective-permute-start.6 = (f32[64,384]{1,0:T(8,128)S(1)}, f32[64,384]{1,0:T(8,128)S(1)}, u32[]{:S(2)}, u32[]{:S(2)}) collective-permute-start(f32[64,384]{1,0:T(8,128)S(1)} %get-tuple-element.18), channel_id=1, source_target_pairs={{0,4},{4,0},{1,5},{5,1},{2,6},{6,2},{3,7},{7,3},{8,12},{12,8},{9,1... | collective-permute-start | bytes 294920 | tf_op jit(solution)/shard_map/ppermute | solution.py:321
  44.5 8.2 %all-to-all-start = ((f32[8,8,384]{2,1,0:T(8,128)}), f32[8,8,384]{2,1,0:T(8,128)S(1)}, u32[]{:S(2)}, u32[]{:S(2)}) async-start(f32[8,8,384]{2,1,0:T(8,128)} %add_bitcast_fusion), calls=%async_computation | async-start | bytes 196608 | tf_op jit(solution)/shard_map/all_to_all | solution.py:325
  52.8 2.0 %cross_part.2.refs_0_ = f32[256,512]{1,0:T(8,128)S(1)} custom-call(s32[1]{0:T(128)} %bitcast.28.which, bf16[6144,512]{1,0:T(8,128)(2,1)} %snap.11, bf16[1536,256]{1,0:T(8,128)(2,1)S(1)} %get-tuple-element.28.refs_0_), custom_call_target="tpu_custom_call" | custom-call | flops 402653184 | bytes 2359296 | tf_op jit(solution)/shard_map/cross_part/pallas_call | solution.py:144
  54.8 5.4 %all-to-all-done.got = f32[8,8,384]{2,1,0:T(8,128)S(1)} async-done(((f32[8,8,384]{2,1,0:T(8,128)}), f32[8,8,384]{2,1,0:T(8,128)S(1)}, u32[]{:S(2)}, u32[]{:S(2)}) %all-to-all-start) | async-done | bytes 98336 | tf_op jit(solution)/shard_map/all_to_all | solution.py:325
  60.8 4.3 %all-to-all-start.1 = ((f32[16,8,384]{2,1,0:T(8,128)}), f32[16,8,384]{2,1,0:T(8,128)}, u32[]{:S(2)}, u32[]{:S(2)}) async-start(f32[16,8,384]{2,1,0:T(8,128)} %sum_copies.2), calls=%async_computation.1 | async-start | bytes 393216 | tf_op jit(solution)/shard_map/all_to_all | solution.py:325
  65.2 1.8 %constant_dynamic-slice_fusion.snap = bf16[1536,512]{1,0:T(8,128)(2,1)S(1)} fusion(bf16[6144,512]{1,0:T(8,128)(2,1)} %snap.11, s32[]{:T(128)S(6)} %select_n.12), kind=kLoop, calls=%fused_computation.53 | loop fusion | bytes 3145732 | tf_op jit(solution)/shard_map/dynamic_slice | solution.py:367
  67.0 3.7 %cross_part.3.near = f32[256,512]{1,0:T(8,128)S(1)} custom-call(s32[2]{0:T(128)S(1)} %pad_add_fusion.2.which, bf16[6144,512]{1,0:T(8,128)(2,1)} %snap.11, f32[256,512]{1,0:T(8,128)S(1)} %cross_part.2.refs_0_, bf16[1536,256]{1,0:T(8,128)(2,1)} %collective-permute-done.7.refs_1_, bf16[1536,256]{1,0:T(8,128)(2,1)} %collective-permute-done.8.refs_2_), custom_call_target="tpu_custom_call" | custom-call | flops 805306368 | bytes 4718592 | tf_op jit(solution)/shard_map/cross_part/pallas_call | solution.py:144
  70.7 1.8 %all-to-all-done.1.got = f32[16,8,384]{2,1,0:T(8,128)} async-done(((f32[16,8,384]{2,1,0:T(8,128)}), f32[16,8,384]{2,1,0:T(8,128)}, u32[]{:S(2)}, u32[]{:S(2)}) %all-to-all-start.1) | async-done | bytes 196640 | tf_op jit(solution)/shard_map/all_to_all | solution.py:325
  72.5 0.9 sum_copies.3
  73.4 1.1 collective-permute-start.10
  74.6 9.9 %all_to_all.20 = f32[8,8,384]{2,1,0:T(8,128)S(1)} all-to-all(f32[8,8,384]{2,1,0:T(8,128)S(1)} %sum_copies.3), channel_id=1, replica_groups=mesh['z'=8,'y'=4,'c'=2,'x'=4] {'z'}, dimensions={0} | all-to-all | bytes 196608 | tf_op jit(solution)/shard_map/all_to_all | solution.py:325
  84.5 4.6 %collective-permute-start.9 = (f32[64,384]{1,0:T(8,128)S(1)}, f32[64,384]{1,0:T(8,128)S(1)}, u32[]{:S(2)}, u32[]{:S(2)}) collective-permute-start(f32[64,384]{1,0:T(8,128)S(1)} %bitcast.82), channel_id=1, source_target_pairs={{0,4},{4,0},{1,5},{5,1},{2,6},{6,2},{3,7},{7,3},{8,12},{12,8},{9,1... | collective-permute-start | bytes 294920 | tf_op jit(solution)/shard_map/ppermute | solution.py:321
  90.0 6.6 %lower_inverse.1.inverse = f32[256,256]{1,0:T(8,128)S(1)} custom-call(s32[1]{0:T(128)} %bitcast.26.core, f32[64,384]{1,0:T(8,128)S(1)} %bitcast.83, f32[64,384]{1,0:T(8,128)S(1)} %collective-permute-done.9.other), custom_call_target="tpu_custom_call" | custom-call | flops 5000000000 | bytes 98304 | tf_op jit(solution)/shard_map/lower_inverse/pallas_call | solution.py:246
  96.7 1.2 %coeff_parts.1 = (f32[32,16,128]{2,1,0:T(8,128)S(1)}, f32[32,16,128]{2,1,0:T(8,128)S(1)}) custom-call(s32[1]{0:T(128)} %bitcast.26.core, f32[256,256]{1,0:T(8,128)S(1)} %lower_inverse.1.inverse, f32[256,512]{1,0:T(8,128)S(1)} %cross_part.3.near, bf16[1536,256]{1,0:T(8,128)(2,1)S(1)} %collective-permute-done.10.low, ...), custom_call_target="tpu_custom_call" | custom-call | flops 805306368 | bytes 1572864 | tf_op jit(solution)/shard_map/coeff_parts/pallas_call | solution.py:282
  98.4 1.2 %collective-permute-done.11 = f32[32,16,128]{2,1,0:T(8,128)S(1)} collective-permute-done((f32[32,16,128]{2,1,0:T(8,128)S(1)}, f32[32,16,128]{2,1,0:T(8,128)S(1)}, u32[]{:S(2)}, u32[]{:S(2)}) %collective-permute-start.11) | collective-permute-done | bytes 262176 | tf_op jit(solution)/shard_map/ppermute | solution.py:321
  100.3 3.9 %all-to-all-start.3 = ((f32[32,16,128]{2,1,0:T(8,128)}), f32[32,16,128]{2,1,0:T(8,128)S(1)}, u32[]{:S(2)}, u32[]{:S(2)}) async-start(f32[32,16,128]{2,1,0:T(8,128)} %add.74), calls=%async_computation.3 | async-start | bytes 524288 | tf_op jit(solution)/shard_map/all_to_all | solution.py:325
  104.2 1.1 copy-done.5
  105.3 0.9 copy-done.7
  106.3 3.1 %basis_rows.1 = f32[1536,256]{1,0:T(8,128)} custom-call(f32[768,256]{1,0:T(8,128)S(1)} %copy-done.5, f32[768,256]{1,0:T(8,128)S(1)} %copy-done.3, f32[256,256]{1,0:T(8,128)S(1)} %copy-done.7), custom_call_target="tpu_custom_call" | custom-call | flops 1207959552 | bytes 3145728 | tf_op jit(solution)/shard_map/basis_rows/pallas_call | solution.py:303
  109.4 6.3 %all-to-all-done.3 = f32[32,16,128]{2,1,0:T(8,128)S(1)} async-done(((f32[32,16,128]{2,1,0:T(8,128)}), f32[32,16,128]{2,1,0:T(8,128)S(1)}, u32[]{:S(2)}, u32[]{:S(2)}) %all-to-all-start.3) | async-done | bytes 262176 | tf_op jit(solution)/shard_map/all_to_all | solution.py:325
  (46 shorter events, 9.1 us)
Async XLA Ops:
  0.6 1.0 copy-start
  3.7 3.8 %copy-start.1 = (bf16[512,256]{1,0:T(8,128)(2,1)S(1)}, bf16[512,256]{1,0:T(8,128)(2,1)}, u32[]{:S(2)}) copy-start(bf16[512,256]{1,0:T(8,128)(2,1)} %omega.7) | copy-start | bytes 786436
  4.0 13.9 %collective-permute-start.4 = (f16[784,256]{1,0:T(8,128)(2,1)S(1)}, f16[784,256]{1,0:T(8,128)(2,1)S(1)}, u32[]{:S(2)}, u32[]{:S(2)}) collective-permute-start(f16[784,256]{1,0:T(8,128)(2,1)S(1)} %get-tuple-element.44), channel_id=1, source_target_pairs={{0,3},{1,0},{2,1},{3,2},{4,7},{5,4},{6,5},{7,6},{8,11},{9,8},{10,9... | collective-permute-start | bytes 1204232 | tf_op jit(solution)/shard_map/ppermute | solution.py:321
  7.4 11.0 %collective-permute-start.1 = (f16[784,256]{1,0:T(8,128)(2,1)S(1)}, f16[784,256]{1,0:T(8,128)(2,1)S(1)}, u32[]{:S(2)}, u32[]{:S(2)}) collective-permute-start(f16[784,256]{1,0:T(8,128)(2,1)S(1)} %get-tuple-element.45), channel_id=1, source_target_pairs={{0,1},{1,2},{2,3},{3,0},{4,5},{5,6},{6,7},{7,4},{8,9},{9,10},{10,1... | collective-permute-start | bytes 1204232 | tf_op jit(solution)/shard_map/ppermute | solution.py:321
  10.4 16.6 %collective-permute-start.3 = (f16[784,256]{1,0:T(8,128)(2,1)S(1)}, f16[784,256]{1,0:T(8,128)(2,1)S(1)}, u32[]{:S(2)}, u32[]{:S(2)}) collective-permute-start(f16[784,256]{1,0:T(8,128)(2,1)S(1)} %get-tuple-element.42), channel_id=1, source_target_pairs={{0,1},{1,2},{2,3},{3,0},{4,5},{5,6},{6,7},{7,4},{8,9},{9,10},{10,1... | collective-permute-start | bytes 1204232 | tf_op jit(solution)/shard_map/ppermute | solution.py:321
  10.7 16.4 %collective-permute-start = (f16[784,256]{1,0:T(8,128)(2,1)S(1)}, f16[784,256]{1,0:T(8,128)(2,1)S(1)}, u32[]{:S(2)}, u32[]{:S(2)}) collective-permute-start(f16[784,256]{1,0:T(8,128)(2,1)S(1)} %get-tuple-element.43), channel_id=1, source_target_pairs={{0,3},{1,0},{2,1},{3,2},{4,7},{5,4},{6,5},{7,6},{8,11},{9,8},{10,9... | collective-permute-start | bytes 1204232 | tf_op jit(solution)/shard_map/ppermute | solution.py:321
  18.8 13.7 %collective-permute-start.5 = (f16[784,256]{1,0:T(8,128)(2,1)S(1)}, f16[784,256]{1,0:T(8,128)(2,1)S(1)}, u32[]{:S(2)}, u32[]{:S(2)}) collective-permute-start(f16[784,256]{1,0:T(8,128)(2,1)S(1)} %get-tuple-element.36), channel_id=1, source_target_pairs={{0,3},{1,0},{2,1},{3,2},{4,7},{5,4},{6,5},{7,6},{8,11},{9,8},{10,9... | collective-permute-start | bytes 1204232 | tf_op jit(solution)/shard_map/ppermute | solution.py:321
  19.8 15.8 %collective-permute-start.2 = (f16[784,256]{1,0:T(8,128)(2,1)S(1)}, f16[784,256]{1,0:T(8,128)(2,1)S(1)}, u32[]{:S(2)}, u32[]{:S(2)}) collective-permute-start(f16[784,256]{1,0:T(8,128)(2,1)S(1)} %get-tuple-element.37), channel_id=1, source_target_pairs={{0,1},{1,2},{2,3},{3,0},{4,5},{5,6},{6,7},{7,4},{8,9},{9,10},{10,1... | collective-permute-start | bytes 1204232 | tf_op jit(solution)/shard_map/ppermute | solution.py:321
  36.0 1.7 %copy-start.2 = (f32[768,256]{1,0:T(8,128)}, f32[768,256]{1,0:T(8,128)S(1)}, u32[]{:S(2)}) copy-start(f32[768,256]{1,0:T(8,128)S(1)} %get-tuple-element.40.bottom) | copy-start | bytes 2359300
  36.0 1.7 %copy-start.4 = (f32[768,256]{1,0:T(8,128)}, f32[768,256]{1,0:T(8,128)S(1)}, u32[]{:S(2)}) copy-start(f32[768,256]{1,0:T(8,128)S(1)} %get-tuple-element.41.top) | copy-start | bytes 2359300
  37.7 29.3 %collective-permute-start.7 = (bf16[1536,256]{1,0:T(8,128)(2,1)S(1)}, bf16[1536,256]{1,0:T(8,128)(2,1)}, u32[]{:S(2)}, u32[]{:S(2)}) collective-permute-start(bf16[1536,256]{1,0:T(8,128)(2,1)S(1)} %get-tuple-element.28.refs_0_), channel_id=1, source_target_pairs={{0,1},{1,2},{2,3},{3,0},{4,5},{5,6},{6,7},{7,4},{8,9},{9,10},{10,1... | collective-permute-start | bytes 2359304 | tf_op jit(solution)/shard_map/ppermute | solution.py:321
  37.8 29.2 %collective-permute-start.8 = (bf16[1536,256]{1,0:T(8,128)(2,1)S(1)}, bf16[1536,256]{1,0:T(8,128)(2,1)}, u32[]{:S(2)}, u32[]{:S(2)}) collective-permute-start(bf16[1536,256]{1,0:T(8,128)(2,1)S(1)} %get-tuple-element.28.refs_0_), channel_id=1, source_target_pairs={{0,3},{1,0},{2,1},{3,2},{4,7},{5,4},{6,5},{7,6},{8,11},{9,8},{10,9... | collective-permute-start | bytes 2359304 | tf_op jit(solution)/shard_map/ppermute | solution.py:321
  40.5 3.4 %collective-permute-start.6 = (f32[64,384]{1,0:T(8,128)S(1)}, f32[64,384]{1,0:T(8,128)S(1)}, u32[]{:S(2)}, u32[]{:S(2)}) collective-permute-start(f32[64,384]{1,0:T(8,128)S(1)} %get-tuple-element.18), channel_id=1, source_target_pairs={{0,4},{4,0},{1,5},{5,1},{2,6},{6,2},{3,7},{7,3},{8,12},{12,8},{9,1... | collective-permute-start | bytes 294920 | tf_op jit(solution)/shard_map/ppermute | solution.py:321
  44.5 15.6 %all-to-all-start = ((f32[8,8,384]{2,1,0:T(8,128)}), f32[8,8,384]{2,1,0:T(8,128)S(1)}, u32[]{:S(2)}, u32[]{:S(2)}) async-start(f32[8,8,384]{2,1,0:T(8,128)} %add_bitcast_fusion), calls=%async_computation | async-start | bytes 196608 | tf_op jit(solution)/shard_map/all_to_all | solution.py:325
  60.8 11.6 %all-to-all-start.1 = ((f32[16,8,384]{2,1,0:T(8,128)}), f32[16,8,384]{2,1,0:T(8,128)}, u32[]{:S(2)}, u32[]{:S(2)}) async-start(f32[16,8,384]{2,1,0:T(8,128)} %sum_copies.2), calls=%async_computation.1 | async-start | bytes 393216 | tf_op jit(solution)/shard_map/all_to_all | solution.py:325
  73.4 23.3 %collective-permute-start.10 = (bf16[1536,256]{1,0:T(8,128)(2,1)S(1)}, bf16[1536,256]{1,0:T(8,128)(2,1)S(1)}, u32[]{:S(2)}, u32[]{:S(2)}) collective-permute-start(bf16[1536,256]{1,0:T(8,128)(2,1)S(1)} %get-tuple-element.28.refs_0_), channel_id=1, source_target_pairs={{0,2},{1,3},{2,0},{3,1},{4,6},{5,7},{6,4},{7,5},{8,10},{9,11},{10,... | collective-permute-start | bytes 2359304 | tf_op jit(solution)/shard_map/ppermute | solution.py:321
  84.5 5.5 %collective-permute-start.9 = (f32[64,384]{1,0:T(8,128)S(1)}, f32[64,384]{1,0:T(8,128)S(1)}, u32[]{:S(2)}, u32[]{:S(2)}) collective-permute-start(f32[64,384]{1,0:T(8,128)S(1)} %bitcast.82), channel_id=1, source_target_pairs={{0,4},{4,0},{1,5},{5,1},{2,6},{6,2},{3,7},{7,3},{8,12},{12,8},{9,1... | collective-permute-start | bytes 294920 | tf_op jit(solution)/shard_map/ppermute | solution.py:321
  96.7 1.3 %copy-start.6 = (f32[256,256]{1,0:T(8,128)}, f32[256,256]{1,0:T(8,128)S(1)}, u32[]{:S(2)}) copy-start(f32[256,256]{1,0:T(8,128)S(1)} %lower_inverse.1.inverse) | copy-start | bytes 786436
  96.7 7.5 %copy-start.3 = (f32[768,256]{1,0:T(8,128)S(1)}, f32[768,256]{1,0:T(8,128)}, u32[]{:S(2)}) copy-start(f32[768,256]{1,0:T(8,128)} %copy-done.2) | copy-start | bytes 2359300
  97.9 1.6 %collective-permute-start.11 = (f32[32,16,128]{2,1,0:T(8,128)S(1)}, f32[32,16,128]{2,1,0:T(8,128)S(1)}, u32[]{:S(2)}, u32[]{:S(2)}) collective-permute-start(f32[32,16,128]{2,1,0:T(8,128)S(1)} %get-tuple-element.31), channel_id=1, source_target_pairs={{0,4},{4,0},{1,5},{5,1},{2,6},{6,2},{3,7},{7,3},{8,12},{12,8},{9,1... | collective-permute-start | bytes 786440 | tf_op jit(solution)/shard_map/ppermute | solution.py:321
  100.3 15.4 %all-to-all-start.3 = ((f32[32,16,128]{2,1,0:T(8,128)}), f32[32,16,128]{2,1,0:T(8,128)S(1)}, u32[]{:S(2)}, u32[]{:S(2)}) async-start(f32[32,16,128]{2,1,0:T(8,128)} %add.74), calls=%async_computation.3 | async-start | bytes 524288 | tf_op jit(solution)/shard_map/all_to_all | solution.py:325
  104.2 1.1 copy-start.5
  105.3 0.9 copy-start.7
